TPU v7x, 32 devices: a whole 2x2x4 slice. The times are simulated.
32 devices in a mesh: gx: 16 (over z, x, core), sec: 2 (over y).
Axes of the slice: x: 2, y: 2, z: 4, core: 2. Of those that a mesh axis runs over, the one named last changes fastest.
Arguments:
- state_init: float32 [16, 128, 16, 128], P(None, 'gx', 'sec'), may hold values from -6 to 6
- rock_type: int32 [128, 1024], P('gx', 'sec'), may hold values from 0 to 15
- perm_table: float32 [3, 16], replicated, may hold values from 0.2 to 1
- well_cells: int32 [256], replicated, may hold values from 0 to 131071
- well_rate: float32 [16, 256], replicated, may hold values from -12 to 12
- basis_in: bfloat16 [128, 16, 128, 256], P(('gx', 'sec')), may hold values from -4 to 4
- singular: float32 [256], replicated, may hold values from 0.5 to 2
Outputs:
- state_out: float32 [16, 128, 16, 128], P(None, 'gx', 'sec')
- basis_out: bfloat16 [128, 16, 128, 256], P(('gx', 'sec'))
- singular_out: float32 [256], replicated
All inputs are finite; a program needn't handle non-finite values.
Results may differ from a plain program's by a relative error of at most 0.0059.
Values may be sent and summed in bfloat16 or wider, within the bound.
No kernel may reach another device: no remote copies, remote signals or barrier semaphores. Data moves between devices by JAX's collectives and lax.ppermute only.
A program may use at most 128 MiB of HBM per device.

v0:
```python
import jax
import jax.numpy as jnp
from jax import lax
from jax.experimental import pallas as pl
from jax.experimental.pallas import tpu as pltpu
from jax.sharding import PartitionSpec as P

MG = 8
STEPS = 4
GROUPS = 2

DT_PRESSURE = 0.12
DT_SATURATION = 0.06
DT_ADVECT = 0.15
HIGHEST = lax.Precision.HIGHEST
AXES = ("gx", "sec")
VMEM_LIMIT = 48 * 2**20


def place(wide_rows):
    sec_count = lax.axis_size("sec")
    rows = wide_rows - 2 * STEPS
    first = (lax.axis_index("gx") * sec_count + lax.axis_index("sec")) * rows - STEPS
    return first, rows * sec_count * lax.axis_size("gx")


def pack_kernel(state_ref, rock_ref, packed, outward, inward, rock_rows):
    across, entries, members, lanes = packed.shape
    along = entries - 1
    layers = lanes // 2
    rock_rows[...] = jnp.zeros_like(rock_rows)
    for y in range(along):
        chunk = rock_ref[:, y * layers : (y + 1) * layers].astype(jnp.float32)
        rock_rows[pl.ds(y, across, stride=members), :] = jnp.concatenate([chunk, chunk], 1)
    for x in range(across):
        for y in range(along):
            column = state_ref[pl.ds(x * along + y, members, stride=across * along), :]
            packed[x, y] = column.astype(jnp.bfloat16)
        packed[x, along] = rock_rows[x * members : (x + 1) * members].astype(jnp.bfloat16)
    if outward is not None:
        half = across // 2
        sec = lax.axis_index("sec")
        outward[...] = packed[pl.ds((1 - sec) * half, half)]
        inward[...] = packed[pl.ds(sec * half, half)]


def pack(state_init, rock_type, halves):
    members, across, along, lanes = state_init.shape
    shape = (along + 1, members, lanes)
    outs = [jax.ShapeDtypeStruct((across,) + shape, jnp.bfloat16)]
    if halves:
        outs += [jax.ShapeDtypeStruct((across // 2,) + shape, jnp.bfloat16)] * 2

    def kernel(state_ref, rock_ref, *refs):
        packed, outward, inward = refs[:3] if halves else (refs[0], None, None)
        pack_kernel(state_ref, rock_ref, packed, outward, inward, refs[-1])

    return pl.pallas_call(
        kernel,
        out_shape=outs,
        scratch_shapes=[pltpu.VMEM((across * members, lanes), jnp.float32)],
        compiler_params=pltpu.CompilerParams(vmem_limit_bytes=VMEM_LIMIT),
    )(state_init.reshape(-1, lanes), rock_type)


def inflow_kernel(cells_ref, rate_ref, out_ref):
    wide, total_y, group, lanes = out_ref.shape
    layers = lanes // 2
    wells = rate_ref.shape[1]
    first, _ = place(wide)
    out_ref[...] = jnp.zeros_like(out_ref)
    lane = lax.broadcasted_iota(jnp.int32, (group, lanes), 1)
    well = lax.broadcasted_iota(jnp.int32, rate_ref.shape, 1)

    def one(w, carry):
        cell = cells_ref[w]
        column = cell // layers
        z = cell - column * layers
        row = column // total_y
        y = column - row * total_y
        x = row - first

        @pl.when((x >= 0) & (x < wide))
        def _():
            rate = jnp.sum(jnp.where(well == w, rate_ref[...], 0.0), axis=1, keepdims=True) * DT_PRESSURE
            low = jnp.where(lane == z, rate[:group], 0.0)
            high = jnp.where(lane == z + layers, rate[group:], 0.0)
            out_ref[x, y] = out_ref[x, y] + low + high

        return carry

    lax.fori_loop(0, wells, one, 0)


def well_inflow(well_cells, well_rate, wide, total_y, lanes):
    return pl.pallas_call(
        inflow_kernel,
        out_shape=jax.ShapeDtypeStruct((wide, total_y, well_rate.shape[0] // 2, lanes), jnp.float32),
        in_specs=[pl.BlockSpec(memory_space=pltpu.SMEM), pl.BlockSpec(memory_space=pltpu.VMEM)],
        compiler_params=pltpu.CompilerParams(vmem_limit_bytes=VMEM_LIMIT),
    )(well_cells, well_rate)


def roll(value, shift):
    return pltpu.roll(value, shift, 1)


def halves_swap(low, high, left_lanes, layers):
    return (
        jnp.where(left_lanes, low, roll(high, layers)),
        jnp.where(left_lanes, roll(low, layers), high),
    )


def harmonic(left, right):
    total = left + right
    return jnp.where(total > 0.0, 2.0 * left * right / jnp.where(total > 0.0, total, 1.0), 0.0)


def face(w12, w06, p, s, p_next, s_next):
    push = w12 * (p_next - p)
    carried = push * jnp.where(push > 0.0, s_next, s)
    return push, w06 * (s_next - s) + (DT_ADVECT / DT_PRESSURE) * carried


def flux_kernel(fast, *refs):
    if fast:
        state_ref, packed, other, beside, cross = refs[:5]
        refs = refs[5:]
    else:
        slab = refs[0]
        refs = refs[1:]
    table, inflow, basis_hbm, snaps, inner_su, inner_ss, fin, send = refs[:8]
    press_a, sat_a, press_b, sat_b, rock, perm, w12, w06, carry, history, basis, sem = refs[8:]
    wide, total_y = inflow.shape[:2]
    group, lanes = inflow.shape[2:]
    layers = lanes // 2
    blocks, along = rock.shape[1:3]
    rows = wide - 2 * STEPS
    copy = pltpu.make_async_copy(basis_hbm, basis, sem)
    copy.start()
    lane = lax.broadcasted_iota(jnp.int32, (group, lanes), 1)
    left_lanes = lane < layers
    lane_y = lax.broadcasted_iota(jnp.int32, (along, lanes), 1)
    sec = lax.axis_index("sec")

    def put(x, y, low, high):
        p, s = halves_swap(low, high, left_lanes, layers)
        press_a[x, y] = p
        sat_a[x, y] = s

    def put_packed(ref, count, x_at, block):
        def row(x, c):
            for y in range(along):
                value = ref[x, y].astype(jnp.float32)
                put(x_at + x, block * along + y, value[:group], value[group:])
            rock[x_at + x, block] = ref[x, along].astype(jnp.float32)[:along]
            return c

        lax.fori_loop(0, count, row, 0)

    if fast:
        across = packed.shape[0]
        here, there = (1 - sec) * STEPS, sec * across

        def own(x, c):
            for y in range(along):
                at = x * along + y
                stride = across * along
                low = state_ref[pl.ds(at, group, stride=stride), :]
                high = state_ref[pl.ds(at + group * stride, group, stride=stride), :]
                put(here + x, sec * along + y, low, high)
            rock[here + x, sec] = packed[x, along].astype(jnp.float32)[:along]
            return c

        lax.fori_loop(0, across, own, 0)
        put_packed(other, across, here, 1 - sec)
        put_packed(beside, STEPS, there, sec)
        put_packed(cross, STEPS, there, 1 - sec)
    else:
        for block in range(blocks):
            put_packed(slab.at[:, block], wide, 0, block)
    zero = jnp.zeros((group, lanes), jnp.float32)
    for x in range(wide):
        for ref in (press_a, sat_a, press_b, sat_b):
            ref[x, total_y] = zero

    first, total_x = place(wide)

    def look_up(x, c):
        inside = ((first + x >= 0) & (first + x < total_x)).astype(jnp.float32)
        for block in range(blocks):
            kind = rock[x, block]
            for d in range(3):
                value = jnp.zeros((along, lanes), jnp.float32)
                for r in range(table.shape[1]):
                    value = jnp.where(kind == float(r), table[d, r], value)
                perm[d, x, pl.ds(block * along, along), :] = value * inside
        return c

    lax.fori_loop(0, wide, look_up, 0)
    for d in range(3):
        perm[d, wide] = jnp.zeros(perm.shape[2:], jnp.float32)
    perm[1, :, total_y:, :] = jnp.zeros((wide + 1, perm.shape[2] - total_y, lanes), jnp.float32)

    def weigh(x, c):
        for block in range(blocks):
            at = block * along
            here = [perm[d, x, pl.ds(at, along), :] for d in range(3)]
            z_next = jnp.where((lane_y == layers - 1) | (lane_y == lanes - 1), 0.0, roll(here[2], lanes - 1))
            beyond = (perm[0, x + 1, pl.ds(at, along), :], perm[1, x, pl.ds(at + 1, along), :], z_next)
            for d in range(3):
                weight = harmonic(here[d], beyond[d])
                w12[d, x, block] = DT_PRESSURE * weight
                w06[d, x, block] = DT_SATURATION * weight
        return c

    lax.fori_loop(0, wide, weigh, 0)

    def spread(ref, d, x, block, j):
        return jnp.broadcast_to(ref[d, x, block, j : j + 1, :], (group, lanes))

    def x_face(p_ref, s_ref, x, block, j):
        y = block * along + j
        return face(
            spread(w12, 0, x, block, j), spread(w06, 0, x, block, j),
            p_ref[x, y], s_ref[x, y], p_ref[x + 1, y], s_ref[x + 1, y],
        )

    buffers = [(press_a, sat_a), (press_b, sat_b)]
    for step in range(STEPS):
        (p_ref, s_ref), (p_new, s_new) = buffers[step % 2], buffers[(step + 1) % 2]

        def begin(block, c):
            for j in range(along):
                carry[0, block * along + j], carry[1, block * along + j] = x_face(p_ref, s_ref, step, block, j)
            return c

        lax.fori_loop(0, blocks, begin, 0)

        def one_row(x, c):
            def one_block(block, back):
                back_p, back_s = back
                for j in range(along):
                    y = block * along + j
                    p, s = p_ref[x, y], s_ref[x, y]
                    xp, xs = x_face(p_ref, s_ref, x, block, j)
                    yp, ys = face(
                        spread(w12, 1, x, block, j), spread(w06, 1, x, block, j),
                        p, s, p_ref[x, y + 1], s_ref[x, y + 1],
                    )
                    zp, zs = face(
                        spread(w12, 2, x, block, j), spread(w06, 2, x, block, j),
                        p, s, roll(p, lanes - 1), roll(s, lanes - 1),
                    )
                    p_new[x, y] = p + (xp - carry[0, y]) + (yp - back_p) + (zp - roll(zp, 1)) + inflow[x, y]
                    s_new[x, y] = s + (xs - carry[1, y]) + (ys - back_s) + (zs - roll(zs, 1))
                    carry[0, y] = xp
                    carry[1, y] = xs
                    back_p, back_s = yp, ys
                return back_p, back_s

            lax.fori_loop(0, blocks, one_block, (zero, zero))
            return c

        lax.fori_loop(step + 1, wide - 1 - step, one_row, 0)

        def save(at, c):
            x, block = at // blocks, at % blocks
            for j in range(along):
                y = block * along + j
                low, high = halves_swap(p_new[STEPS + x, y], s_new[STEPS + x, y], left_lanes, layers)
                history[x * total_y + y, step * group : (step + 1) * group] = low
                history[x * total_y + y, (STEPS + step) * group : (STEPS + step + 1) * group] = high
                if step == STEPS - 1 and not fast:
                    fin[x, block, j] = jnp.concatenate([low, high], 0)
            return c

        lax.fori_loop(0, rows * blocks, save, 0)

    if fast:
        last = slice((STEPS - 1) * group, STEPS * group)
        past = slice((2 * STEPS - 1) * group, 2 * STEPS * group)
        for ref, block in ((fin, sec), (send, 1 - sec)):
            for x in range(rows):
                for j in range(along):
                    at = x * total_y + block * along + j
                    ref[x, j, :group] = history[at, last]
                    ref[x, j, group:] = history[at, past]

    copy.wait()
    inner_su[...] = jnp.zeros_like(inner_su)
    inner_ss[...] = jnp.zeros_like(inner_ss)
    count = basis.shape[2]

    def add_pair(q, c):
        pair = [history[2 * q].astype(jnp.bfloat16), history[2 * q + 1].astype(jnp.bfloat16)]
        snaps[2 * q] = pair[0]
        snaps[2 * q + 1] = pair[1]
        both = jnp.concatenate(pair, 1)
        inner_su[...] += jnp.dot(both, basis[pl.ds(2 * q, 2)].reshape(2 * lanes, count), preferred_element_type=jnp.float32)
        inner_ss[...] += lax.dot_general(both, both, (((1,), (1,)), ((), ())), preferred_element_type=jnp.float32)
        return c

    lax.fori_loop(0, rows * total_y // 2, add_pair, 0)


def flux(fields, perm_table, inflow, basis_blocks, along):
    fast = len(fields) > 1
    wide, total_y, group, lanes = inflow.shape
    blocks = total_y // along
    rows = wide - 2 * STEPS
    count = basis_blocks.shape[-1]
    snaps = 2 * STEPS * group
    f32 = jnp.float32
    fin = (rows, along, 2 * group, lanes) if fast else (rows, blocks, along, 2 * group, lanes)
    outs = [
        jax.ShapeDtypeStruct((rows * total_y, snaps, lanes), jnp.bfloat16),
        jax.ShapeDtypeStruct((snaps, count), f32),
        jax.ShapeDtypeStruct((snaps, snaps), f32),
        jax.ShapeDtypeStruct(fin, f32),
        jax.ShapeDtypeStruct(fin if fast else (8, lanes), f32),
    ]
    state = pltpu.VMEM((wide, total_y + 1, group, lanes), f32)
    whole = pl.BlockSpec(memory_space=pltpu.VMEM)
    return pl.pallas_call(
        lambda *refs: flux_kernel(fast, *refs),
        out_shape=outs,
        in_specs=[whole] * len(fields)
        + [pl.BlockSpec(memory_space=pltpu.SMEM), whole, pl.BlockSpec(memory_space=pl.ANY)],
        scratch_shapes=[
            state, state, state, state,
            pltpu.VMEM((wide, blocks, along, lanes), f32),
            pltpu.VMEM((3, wide + 1, total_y + 8, lanes), f32),
            pltpu.VMEM((3, wide, blocks, along, lanes), f32),
            pltpu.VMEM((3, wide, blocks, along, lanes), f32),
            pltpu.VMEM((2, total_y, group, lanes), f32),
            pltpu.VMEM((rows * total_y, snaps, lanes), f32),
            pltpu.VMEM(basis_blocks.shape, jnp.bfloat16),
            pltpu.SemaphoreType.DMA,
        ],
        compiler_params=pltpu.CompilerParams(vmem_limit_bytes=VMEM_LIMIT),
    )(*fields, perm_table, inflow, basis_blocks)


def unpack_kernel(parts, *refs):
    out_ref = refs[-1]
    along = refs[0].shape[1]
    members = refs[0].shape[2]
    stride = out_ref.shape[0] // members
    sec = lax.axis_index("sec")
    for part in range(parts):
        rows = refs[part].shape[0]
        start = 0 if parts == 1 else (sec if part == 0 else 1 - sec) * rows
        for x in range(rows):
            for y in range(along):
                out_ref[pl.ds((start + x) * along + y, members, stride=stride), :] = refs[part][x, y]


def unpack(parts):
    rows, along, members, lanes = parts[0].shape
    across = rows * len(parts)
    out = pl.pallas_call(
        lambda *refs: unpack_kernel(len(parts), *refs),
        out_shape=jax.ShapeDtypeStruct((members * across * along, lanes), jnp.float32),
        compiler_params=pltpu.CompilerParams(vmem_limit_bytes=VMEM_LIMIT),
    )(*parts)
    return out.reshape(members, across, along, lanes)


def all_sum(value):
    for axis in AXES:
        count = lax.axis_size(axis)
        if count & (count - 1):
            value = lax.psum(value, axis)
            continue
        stride = 1
        while stride < count:
            value = value + lax.ppermute(value, axis, [(i, i ^ stride) for i in range(count)])
            stride *= 2
    return value


def to_bf16(value):
    return value.astype(jnp.bfloat16)


def hdot(a, b, left=1, right=0):
    return lax.dot_general(a, b, (((left,), (right,)), ((), ())), precision=HIGHEST, preferred_element_type=jnp.float32)

SUB = 8
PANEL = 32
LANE = 128

def eliminate(panel, column):
    groups = PANEL // SUB
    tiles = panel.shape[1] // LANE
    below = lax.broadcasted_iota(jnp.int32, (SUB, LANE), 0)
    strip = [[panel[h * SUB:(h + 1) * SUB, t * LANE:(t + 1) * LANE] for t in range(tiles)] for h in range(groups)]
    for g in range(groups):
        spread = {}
        for h in range(g, groups):
            for j in range(SUB):
                at = column + g * SUB + j
                tile, lane = at // LANE, at % LANE
                spread[h, j] = jnp.broadcast_to(strip[h][tile][:, lane:lane + 1], (SUB, LANE))
        scale = jnp.zeros((SUB, LANE), jnp.float32)
        for j in range(SUB):
            pivot = jnp.broadcast_to(spread[g, j][j:j + 1], (SUB, LANE))
            inverse = 1.0 / pivot
            scale = jnp.where(below == j, pivot, scale)
            factors = {}
            for h in range(g, groups):
                factors[h] = spread[h, j] * inverse
            factors[g] = jnp.where(below > j, factors[g], 0.0)
            for k in range(j + 1, SUB):
                row = jnp.broadcast_to(spread[g, k][j:j + 1], (SUB, LANE))
                for h in range(g, groups):
                    spread[h, k] = spread[h, k] - factors[h] * row
            for t in range(tiles):
                row = jnp.broadcast_to(strip[g][t][j:j + 1], (SUB, LANE))
                for h in range(g, groups):
                    strip[h][t] = strip[h][t] - factors[h] * row
        root = lax.rsqrt(scale)
        for t in range(tiles):
            strip[g][t] = strip[g][t] * root
    return jnp.concatenate([jnp.concatenate(s, 1) for s in strip], 0)

def solve(aug, count):
    width = aug.shape[1]
    for start in range(0, count, PANEL):
        first = start // LANE * LANE
        done = eliminate(aug[start:start + PANEL, first:], start - first)
        aug[start:start + PANEL, first:] = done
        rest = start + PANEL
        if rest < count:
            base = rest // LANE * LANE
            left = done[:, base - first:count - first]
            change = hdot(left, done[:, base - first:], 0, 0)
            aug[rest:, base:] = aug[rest:, base:] - change[rest - base:]

def small_kernel(gram_ref, sigma_ref, weight_ref, sigma_out, aug):
    count = sigma_ref.shape[1]
    snaps = (gram_ref.shape[0] - count) // 2
    eye = lax.broadcasted_iota(jnp.int32, (count, count), 0) == lax.broadcasted_iota(jnp.int32, (count, count), 1)
    pad = LANE - snaps
    sig2 = sigma_ref[...] * sigma_ref[...]
    prior = None
    for group in range(2):
        rows = gram_ref[count + group * snaps: count + (group + 1) * snaps]
        if group == 0:
            coeffs = rows[:, :count]
            own = rows[:, count:count + snaps]
        else:
            reach = count + snaps
            coeffs = hdot(rows[:, :reach], prior[:, :reach], 1, 1)
            own = rows[:, reach:reach + snaps]
        rounded = coeffs.astype(jnp.bfloat16).astype(jnp.float32)
        if group == 0:
            mapped = rounded
            known = gram_ref[:count, :count]
        else:
            mapped = hdot(rounded, prior[:, :reach])
            known = gram_ref[:reach, :reach]
        spread = hdot(mapped, known)
        gram = own - hdot(rounded, coeffs, 1, 1) - hdot(coeffs, rounded, 1, 1) + hdot(spread, mapped, 1, 1)
        lead = hdot(coeffs, coeffs, 0, 0) + jnp.where(eye, jnp.broadcast_to(sig2, eye.shape), 0.0)
        inner = hdot(lead, lead) + hdot(coeffs, hdot(gram, coeffs), 0, 0)
        aug[:, :count] = inner
        aug[:, count:2 * count] = lead
        aug[:, 2 * count:] = jnp.concatenate([coeffs, jnp.zeros((pad, count), jnp.float32)], 0).T
        solve(aug, count)
        turned = aug[:, count:2 * count]
        extra = aug[:, 2 * count:2 * count + snaps]
        energy = turned * turned * sig2
        ones = jnp.ones((8, count), jnp.float32)
        low = hdot(turned, coeffs, 1, 1) + hdot(extra, gram)
        sig2 = hdot(ones, energy, 1, 1)[:1] + hdot(ones[:, :snaps], low * low, 1, 1)[:1]
        step = turned.astype(jnp.bfloat16).astype(jnp.float32) - hdot(extra, rounded)
        if group == 0:
            prior = jnp.concatenate([step, aug[:, 2 * count:]], 1)
        else:
            weight_ref[:, :count + LANE] = hdot(step, prior)
            weight_ref[:, count + LANE:] = aug[:, 2 * count:]
    sigma_out[...] = jnp.sqrt(sig2)

def small(grams, sigma):
    count = sigma.shape[0]
    w, s = pl.pallas_call(
        small_kernel,
        out_shape=(jax.ShapeDtypeStruct((count, count + 2 * LANE), jnp.float32), jax.ShapeDtypeStruct((1, count), jnp.float32)),
        scratch_shapes=[pltpu.VMEM((count, 2 * count + LANE), jnp.float32)],
        compiler_params=pltpu.CompilerParams(vmem_limit_bytes=VMEM_LIMIT),
    )(grams, sigma.reshape(1, count))
    return w, s.reshape(count)


def body(state_init, rock_type, perm_table, well_cells, well_rate, basis_in, singular):
    members, across, along, lanes = state_init.shape
    gx_count = lax.axis_size("gx")
    sec_count = lax.axis_size("sec")
    rows = across // sec_count
    wide = rows + 2 * STEPS
    total_y = along * sec_count
    count = basis_in.shape[-1]
    fast = sec_count == 2 and across == 2 * STEPS
    inflow = well_inflow(well_cells, well_rate, wide, total_y, lanes)
    if fast:
        packed, outward, inward = pack(state_init, rock_type, True)
        straight, crossed = [], []
        for r in range(gx_count):
            if r > 0:
                straight.append((2 * (r - 1), 2 * r))
                crossed.append((2 * (r - 1) + 1, 2 * r))
            if r < gx_count - 1:
                straight.append((2 * (r + 1) + 1, 2 * r + 1))
                crossed.append((2 * (r + 1), 2 * r + 1))
        other = lax.ppermute(packed, "sec", [(0, 1), (1, 0)])
        cross = lax.ppermute(inward, AXES, crossed)
        beside = lax.ppermute(outward, AXES, straight)
        fields = (state_init.reshape(-1, lanes), packed, other, beside, cross)
    else:
        (packed,) = pack(state_init, rock_type, False)
        slab = lax.all_gather(packed, "sec", axis=1)
        low = lax.ppermute(slab[across - STEPS :], "gx", [(i, i + 1) for i in range(gx_count - 1)])
        high = lax.ppermute(slab[:STEPS], "gx", [(i + 1, i) for i in range(gx_count - 1)])
        padded = jnp.concatenate([low, slab, high], 0)
        fields = (lax.dynamic_slice_in_dim(padded, lax.axis_index("sec") * rows, wide, axis=0),)
    flat = basis_in.reshape(-1, count)
    rows_total = flat.shape[0] * gx_count * sec_count
    inner_uu = lax.dot_general(flat, flat, (((0,), (0,)), ((), ())), preferred_element_type=jnp.float32)
    snaps, inner_su, inner_ss, fin, send = flux(fields, perm_table, inflow, flat.reshape(-1, lanes, count), along)
    if fast:
        received = lax.ppermute(send, "sec", [(0, 1), (1, 0)])
        state_out = unpack((fin, received))
    else:
        moved = lax.all_to_all(fin, "sec", split_axis=1, concat_axis=0, tiled=True)
        state_out = unpack((moved.reshape(across, along, members, lanes),))

    snap_count = snaps.shape[1]
    grams = jnp.concatenate(
        [jnp.concatenate([inner_uu, inner_su.T], 1), jnp.concatenate([inner_su, inner_ss], 1)], 0
    )
    grams = all_sum(grams) / rows_total
    turned, sigma = small(grams, singular)
    half = snap_count // 2
    final_w = jnp.concatenate(
        [turned[:, :count], turned[:, count : count + half], turned[:, count + LANE : count + LANE + half]], 1
    ).T
    high = to_bf16(final_w)
    low = to_bf16(final_w - high.astype(jnp.float32))
    columns = jnp.moveaxis(snaps, 1, 2).reshape(-1, snap_count)
    both = jnp.concatenate([flat, columns], 1)
    fresh = jnp.dot(both, high, preferred_element_type=jnp.float32) + jnp.dot(
        both, low, preferred_element_type=jnp.float32
    )
    return state_out, to_bf16(fresh).reshape(basis_in.shape), sigma


def solution(mesh):
    return jax.shard_map(
        body,
        mesh=mesh,
        in_specs=(
            P(None, "gx", "sec", None),
            P("gx", "sec"),
            P(),
            P(),
            P(),
            P(("gx", "sec"), None, None, None),
            P(),
        ),
        out_specs=(P(None, "gx", "sec", None), P(("gx", "sec"), None, None, None), P()),
        check_vma=False,
    )
```

profile of v0, /device:TPU:25, one launch (start us, length us, event | category | flops | bytes accessed | tf_op | source)
XLA Modules:
  0.0 150.1 jit_solution(14670656679648674689)
XLA Ops:
  0.6 0.0 copy-start.5
  0.6 0.0 copy-start
  0.7 1.0 copy-done
  1.7 0.0 copy-start.2
  1.7 0.7 copy-done.2
  2.4 0.0 copy-start.3
  2.4 0.0 copy-start.1
  2.4 0.0 copy-start.4
  2.4 0.3 shard_map.94
  2.7 3.7 %collective-permute-start.1 = (bf16[4,9,16,128]{3,2,1,0:T(8,128)(2,1)S(1)}, bf16[4,9,16,128]{3,2,1,0:T(8,128)(2,1)S(1)}, u32[]{:S(2)}, u32[]{:S(2)}) collective-permute-start(bf16[4,9,16,128]{3,2,1,0:T(8,128)(2,1)S(1)} %get-tuple-element.14), channel_id=1, source_target_pairs={{3,1},{0,2},{5,3},{2,4},{7,5},{4,6},{9,7},{6,8},{11,9},{8,10},{13,... | collective-permute-start | bytes 442376 | tf_op jit(solution)/shard_map/ppermute | solution.py:520
  6.4 2.8 %collective-permute-start.2 = (bf16[4,9,16,128]{3,2,1,0:T(8,128)(2,1)S(1)}, bf16[4,9,16,128]{3,2,1,0:T(8,128)(2,1)S(1)}, u32[]{:S(2)}, u32[]{:S(2)}) collective-permute-start(bf16[4,9,16,128]{3,2,1,0:T(8,128)(2,1)S(1)} %get-tuple-element.15), channel_id=1, source_target_pairs={{2,1},{1,2},{4,3},{3,4},{6,5},{5,6},{8,7},{7,8},{10,9},{9,10},{12,... | collective-permute-start | bytes 442376 | tf_op jit(solution)/shard_map/ppermute | solution.py:519
  9.2 0.4 collective-permute-start
  9.6 4.7 %convolution_bitcast_fusion = f32[256,256]{1,0:T(8,128)S(1)} fusion(bf16[4,16,128,256]{3,2,1,0:T(8,128)(2,1)} %param.12), kind=kOutput, calls=%fused_computation.4 | convolution fusion | flops 1073741824 | bytes 4456448 | tf_op jit(solution)/shard_map/dot_general | solution.py:531
  14.4 0.0 copy-done.5
  14.4 0.0 copy-done.3
  14.4 7.8 %shard_map.95.refs_6_ = f32[12,16,8,128]{3,2,1,0:T(8,128)S(1)} custom-call(s32[256]{0:T(256)S(1)} %copy-done.5, f32[16,256]{1,0:T(8,128)S(1)} %copy-done.3), custom_call_target="tpu_custom_call" | custom-call | tf_op jit(solution)/shard_map/pallas_call | solution.py:96
  22.2 0.0 collective-permute-done.1.refs_3_
  22.2 0.0 collective-permute-done.2.refs_4_
  22.2 0.0 collective-permute-done.refs_2_
  22.2 0.0 copy-done.1
  22.3 0.0 copy-done.4
  22.3 21.5 %shard_map.96 = (bf16[64,64,128]{2,1,0:T(8,128)(2,1)S(1)}, f32[64,256]{1,0:T(8,128)S(1)}, f32[64,64]{1,0:T(8,128)S(1)}, f32[4,8,16,128]{3,2,1,0:T(8,128)S(1)}, f32[4,8,16,128]{3,2,1,0:T(8,128)S(1)}) custom-call(f32[1024,128]{1,0:T(8,128)S(1)} %bitcast.25, bf16[8,9,16,128]{3,2,1,0:T(8,128)(2,1)S(1)} %get-tuple-element.13.refs_1_, ...), custom_call_target="tpu_custom_call" | custom-call | tf_op jit(solution)/shard_map/pallas_call | solution.py:326
  43.8 0.1 copy.16
  43.9 0.0 copy-start.6
  43.9 1.0 collective-permute-start.4
  44.9 1.5 collective-permute-done.4
  46.4 0.1 fusion.8
  46.5 0.1 collective-permute-start.5
  46.6 12.4 %collective-permute-done.5 = f32[320,320]{1,0:T(8,128)S(1)} collective-permute-done((f32[320,320]{1,0:T(8,128)S(1)}, f32[320,320]{1,0:T(8,128)S(1)}, u32[]{:S(2)}, u32[]{:S(2)}) %collective-permute-start.5) | collective-permute-done | bytes 409632 | tf_op jit(solution)/shard_map/ppermute | solution.py:379
  59.0 0.1 add.19
  59.0 0.4 collective-permute-start.6
  59.4 11.2 %collective-permute-done.6 = f32[320,320]{1,0:T(8,128)S(1)} collective-permute-done((f32[320,320]{1,0:T(8,128)S(1)}, f32[320,320]{1,0:T(8,128)S(1)}, u32[]{:S(2)}, u32[]{:S(2)}) %collective-permute-start.6) | collective-permute-done | bytes 409632 | tf_op jit(solution)/shard_map/ppermute | solution.py:379
  70.6 0.1 add.20
  70.7 0.1 collective-permute-start.7
  70.8 24.5 %collective-permute-done.7 = f32[320,320]{1,0:T(8,128)S(1)} collective-permute-done((f32[320,320]{1,0:T(8,128)S(1)}, f32[320,320]{1,0:T(8,128)S(1)}, u32[]{:S(2)}, u32[]{:S(2)}) %collective-permute-start.7) | collective-permute-done | bytes 409632 | tf_op jit(solution)/shard_map/ppermute | solution.py:379
  95.3 0.1 add.21
  95.4 1.0 collective-permute-start.8
  96.3 0.6 collective-permute-start.3
  96.9 1.8 %copy.20 = bf16[64,128,64]{2,1,0:T(8,128)(2,1)} copy(bf16[64,128,64]{1,2,0:T(8,128)(2,1)S(1)} %bitcast.26) | data formatting | bytes 2097152 | tf_op jit(solution)/shard_map/reshape | solution.py:552
  98.6 14.7 %collective-permute-done.3.refs_1_ = f32[4,8,16,128]{3,2,1,0:T(8,128)S(1)} collective-permute-done((f32[4,8,16,128]{3,2,1,0:T(8,128)S(1)}, f32[4,8,16,128]{3,2,1,0:T(8,128)S(1)}, u32[]{:S(2)}, u32[]{:S(2)}) %collective-permute-start.3) | collective-permute-done | bytes 262176 | tf_op jit(solution)/shard_map/ppermute | solution.py:534
  113.3 1.1 shard_map.97
  114.4 0.0 collective-permute-done.8
  114.4 0.1 add_multiply_fusion.gram_ref
  114.5 0.0 copy-done.6
  114.5 26.3 %shard_map.98 = (f32[256,512]{1,0:T(8,128)S(1)}, f32[1,256]{1,0:T(1,128)}) custom-call(f32[320,320]{1,0:T(8,128)S(1)} %add_multiply_fusion.gram_ref, f32[1,256]{1,0:T(1,128)S(1)} %bitcast.27), custom_call_target="tpu_custom_call" | custom-call | tf_op jit(solution)/shard_map/pallas_call | solution.py:489
  140.8 0.0 copy-start.7
  140.8 0.0 copy-start.8
  140.8 5.2 %fusion.1 = f32[8192,256]{1,0:T(8,128)S(1)} fusion(bf16[8192,64]{1,0:T(8,128)(2,1)} %bitcast.31, bf16[8192,256]{1,0:T(8,128)(2,1)} %bitcast.29, f32[256,32]{1,0:T(8,128)S(1)} %slice.9, f32[256,288]{1,0:T(8,128)S(1)} %slice.8), kind=kOutput, calls=%fused_computation.3 | convolution fusion | flops 1352990720 | bytes 13959168 | tf_op jit(solution)/shard_map/dot_general | solution.py:554
  146.0 0.0 copy-done.7
  146.0 0.0 copy-done.8
  146.0 4.1 %fusion = bf16[8192,256]{1,0:T(8,128)(2,1)} fusion(f32[8192,256]{1,0:T(8,128)S(1)} %fusion.1, bf16[8192,64]{1,0:T(8,128)(2,1)S(1)} %bitcast.32, bf16[8192,256]{1,0:T(8,128)(2,1)S(1)} %bitcast.30, f32[256,32]{1,0:T(8,128)S(1)} %slice.9, f32[256,288]{1,0:T(8,128)S(1)} %slice.8), kind=kOutput, calls=%fused_computation.1 | convolution fusion | flops 1357266944 | bytes 18153472 | tf_op jit(solution)/shard_map/dot_general | solution.py:554
  (3 shorter events, 0.1 us)
Async XLA Ops:
  0.6 13.7 %copy-start.5 = (s32[256]{0:T(256)S(1)}, s32[256]{0:T(256)}, u32[]{:S(2)}) copy-start(s32[256]{0:T(256)} %cells_ref.1) | copy-start | bytes 3076
  0.6 1.0 copy-start
  1.7 0.7 copy-start.2
  2.4 12.0 %copy-start.3 = (f32[16,256]{1,0:T(8,128)S(1)}, f32[16,256]{1,0:T(8,128)}, u32[]{:S(2)}) copy-start(f32[16,256]{1,0:T(8,128)} %rate_ref.1) | copy-start | bytes 49156
  2.4 19.8 %copy-start.1 = (f32[16,8,8,128]{3,2,1,0:T(8,128)S(1)}, f32[16,8,8,128]{3,2,1,0:T(8,128)}, u32[]{:S(2)}) copy-start(f32[16,8,8,128]{3,2,1,0:T(8,128)} %param.7) | copy-start | bytes 1572868
  2.4 19.9 %copy-start.4 = (f32[3,16]{1,0:T(4,128)S(1)}, f32[3,16]{1,0:T(4,128)}, u32[]{:S(2)}) copy-start(f32[3,16]{1,0:T(4,128)} %refs_5_.1) | copy-start | bytes 580
  2.7 19.5 %collective-permute-start.1 = (bf16[4,9,16,128]{3,2,1,0:T(8,128)(2,1)S(1)}, bf16[4,9,16,128]{3,2,1,0:T(8,128)(2,1)S(1)}, u32[]{:S(2)}, u32[]{:S(2)}) collective-permute-start(bf16[4,9,16,128]{3,2,1,0:T(8,128)(2,1)S(1)} %get-tuple-element.14), channel_id=1, source_target_pairs={{3,1},{0,2},{5,3},{2,4},{7,5},{4,6},{9,7},{6,8},{11,9},{8,10},{13,... | collective-permute-start | bytes 442376 | tf_op jit(solution)/shard_map/ppermute | solution.py:520
  6.4 15.8 %collective-permute-start.2 = (bf16[4,9,16,128]{3,2,1,0:T(8,128)(2,1)S(1)}, bf16[4,9,16,128]{3,2,1,0:T(8,128)(2,1)S(1)}, u32[]{:S(2)}, u32[]{:S(2)}) collective-permute-start(bf16[4,9,16,128]{3,2,1,0:T(8,128)(2,1)S(1)} %get-tuple-element.15), channel_id=1, source_target_pairs={{2,1},{1,2},{4,3},{3,4},{6,5},{5,6},{8,7},{7,8},{10,9},{9,10},{12,... | collective-permute-start | bytes 442376 | tf_op jit(solution)/shard_map/ppermute | solution.py:519
  9.2 13.0 %collective-permute-start = (bf16[8,9,16,128]{3,2,1,0:T(8,128)(2,1)S(1)}, bf16[8,9,16,128]{3,2,1,0:T(8,128)(2,1)S(1)}, u32[]{:S(2)}, u32[]{:S(2)}) collective-permute-start(bf16[8,9,16,128]{3,2,1,0:T(8,128)(2,1)S(1)} %get-tuple-element.13.refs_1_), channel_id=1, source_target_pairs={{0,1},{1,0},{2,3},{3,2},{4,5},{5,4},{6,7},{7,6},{8,9},{9,8},{10,11... | collective-permute-start | bytes 884744 | tf_op jit(solution)/shard_map/ppermute | solution.py:518
  43.9 70.6 %copy-start.6 = (f32[256]{0:T(256)S(1)}, f32[256]{0:T(256)}, u32[]{:S(2)}) copy-start(f32[256]{0:T(256)} %param.13) | copy-start | bytes 3076
  43.9 2.5 %collective-permute-start.4 = (f32[320,320]{1,0:T(8,128)S(1)}, f32[320,320]{1,0:T(8,128)S(1)}, u32[]{:S(2)}, u32[]{:S(2)}) collective-permute-start(f32[320,320]{1,0:T(8,128)S(1)} %maximum_maximum_fusion), channel_id=1, source_target_pairs={{0,2},{2,0},{4,6},{6,4},{8,10},{10,8},{12,14},{14,12},{16,18},{18,... | collective-permute-start | bytes 1228808 | tf_op jit(solution)/shard_map/ppermute | solution.py:379
  46.5 12.5 %collective-permute-start.5 = (f32[320,320]{1,0:T(8,128)S(1)}, f32[320,320]{1,0:T(8,128)S(1)}, u32[]{:S(2)}, u32[]{:S(2)}) collective-permute-start(f32[320,320]{1,0:T(8,128)S(1)} %fusion.8), channel_id=1, source_target_pairs={{0,4},{2,6},{4,0},{6,2},{8,12},{10,14},{12,8},{14,10},{16,20},{18,... | collective-permute-start | bytes 1228808 | tf_op jit(solution)/shard_map/ppermute | solution.py:379
  59.0 11.6 %collective-permute-start.6 = (f32[320,320]{1,0:T(8,128)S(1)}, f32[320,320]{1,0:T(8,128)S(1)}, u32[]{:S(2)}, u32[]{:S(2)}) collective-permute-start(f32[320,320]{1,0:T(8,128)S(1)} %add.19), channel_id=1, source_target_pairs={{0,8},{2,10},{4,12},{6,14},{8,0},{10,2},{12,4},{14,6},{16,24},{18,... | collective-permute-start | bytes 1228808 | tf_op jit(solution)/shard_map/ppermute | solution.py:379
  70.7 24.6 %collective-permute-start.7 = (f32[320,320]{1,0:T(8,128)S(1)}, f32[320,320]{1,0:T(8,128)S(1)}, u32[]{:S(2)}, u32[]{:S(2)}) collective-permute-start(f32[320,320]{1,0:T(8,128)S(1)} %add.20), channel_id=1, source_target_pairs={{0,16},{2,18},{4,20},{6,22},{8,24},{10,26},{12,28},{14,30},{16,0},... | collective-permute-start | bytes 1228808 | tf_op jit(solution)/shard_map/ppermute | solution.py:379
  95.4 19.1 %collective-permute-start.8 = (f32[320,320]{1,0:T(8,128)S(1)}, f32[320,320]{1,0:T(8,128)S(1)}, u32[]{:S(2)}, u32[]{:S(2)}) collective-permute-start(f32[320,320]{1,0:T(8,128)S(1)} %add.21), channel_id=1, source_target_pairs={{0,1},{1,0},{2,3},{3,2},{4,5},{5,4},{6,7},{7,6},{8,9},{9,8},{10,11... | collective-permute-start | bytes 1228808 | tf_op jit(solution)/shard_map/ppermute | solution.py:379
  96.3 17.0 %collective-permute-start.3 = (f32[4,8,16,128]{3,2,1,0:T(8,128)S(1)}, f32[4,8,16,128]{3,2,1,0:T(8,128)S(1)}, u32[]{:S(2)}, u32[]{:S(2)}) collective-permute-start(f32[4,8,16,128]{3,2,1,0:T(8,128)S(1)} %get-tuple-element.17), channel_id=1, source_target_pairs={{0,1},{1,0},{2,3},{3,2},{4,5},{5,4},{6,7},{7,6},{8,9},{9,8},{10,11... | collective-permute-start | bytes 786440 | tf_op jit(solution)/shard_map/ppermute | solution.py:534
  140.8 5.2 %copy-start.7 = (bf16[4,16,128,256]{3,2,1,0:T(8,128)(2,1)S(1)}, bf16[4,16,128,256]{3,2,1,0:T(8,128)(2,1)}, u32[]{:S(2)}) copy-start(bf16[4,16,128,256]{3,2,1,0:T(8,128)(2,1)} %param.12) | copy-start | bytes 12582916
  140.8 5.2 %copy-start.8 = (bf16[64,128,64]{2,1,0:T(8,128)(2,1)S(1)}, bf16[64,128,64]{2,1,0:T(8,128)(2,1)}, u32[]{:S(2)}) copy-start(bf16[64,128,64]{2,1,0:T(8,128)(2,1)} %copy.20) | copy-start | bytes 3145732
where the time goes:
time: 152 us; the launch traced here: 150 us
  waiting for transfers between devices  64.3 us (42%)
  Pallas kernels  57 us (38%)
  matrix products  14 us (9%)
  starting transfers between devices  9.92 us (7%)
  local copies, waits for them, and re-layouts  3.7 us (2%)
    ppermute x5, waiting for transfers between devices, all_sum(): lax.ppermute(value, axis, [(i, i ^ stride) for i in range(count)])  49.7 us
    pallas_call x1, Pallas kernels, small(): pl.pallas_call(small_kernel, out_shape=(jax.ShapeDtypeStruct((count, coun...  26.3 us
    pallas_call x1, Pallas kernels, flux(): pl.pallas_call(lambda *refs: flux_kernel(fast, *refs), out_shape=outs, in...  21.5 us
    ppermute x1, waiting for transfers between devices, body(): received = lax.ppermute(send, 'sec', [(0, 1), (1, 0)])  14.7 us
    pallas_call x1, Pallas kernels, well_inflow(): pl.pallas_call(inflow_kernel, out_shape=jax.ShapeDtypeStruct((wide, total...  7.83 us
    dot_general x1, matrix products, body(): jnp.dot(both, high, preferred_element_type=jnp.float32)  5.17 us
    dot_general x1, matrix products, body(): lax.dot_general(flat, flat, (((0,), (0,)), ((), ())), preferred_element_t...  4.74 us
    dot_general x1, matrix products, body(): jnp.dot(both, low, preferred_element_type=jnp.float32)  4.07 us
  transfers between devices with their start and end apart: 9, of which 5 were waited for; matrix products, arithmetic and copies ran while one was open for 4% of the time, Pallas kernels for 6%

commit v1 on v0

--- a/solution.py
+++ b/solution.py
@@ -1,3 +1,5 @@
+import functools
+
 import jax
 import jax.numpy as jnp
 from jax import lax
@@ -24,17 +26,24 @@
     return first, rows * sec_count * lax.axis_size("gx")
 
 
-def pack_kernel(state_ref, rock_ref, packed, outward, inward, rock_rows):
+def pack_kernel(state_ref, rock_ref, own, packed, outward, inward, rock_rows):
     across, entries, members, lanes = packed.shape
     along = entries - 1
     layers = lanes // 2
+    group = members // 2
+    stride = across * along
+    left_lanes = lax.broadcasted_iota(jnp.int32, (group, lanes), 1) < layers
     rock_rows[...] = jnp.zeros_like(rock_rows)
     for y in range(along):
         chunk = rock_ref[:, y * layers : (y + 1) * layers].astype(jnp.float32)
         rock_rows[pl.ds(y, across, stride=members), :] = jnp.concatenate([chunk, chunk], 1)
     for x in range(across):
         for y in range(along):
-            column = state_ref[pl.ds(x * along + y, members, stride=across * along), :]
+            at = x * along + y
+            low = state_ref[pl.ds(at, group, stride=stride), :]
+            high = state_ref[pl.ds(at + group * stride, group, stride=stride), :]
+            column = jnp.concatenate(halves_swap(low, high, left_lanes, layers), 0)
+            own[x, y] = column
             packed[x, y] = column.astype(jnp.bfloat16)
         packed[x, along] = rock_rows[x * members : (x + 1) * members].astype(jnp.bfloat16)
     if outward is not None:
@@ -47,13 +56,17 @@
 def pack(state_init, rock_type, halves):
     members, across, along, lanes = state_init.shape
     shape = (along + 1, members, lanes)
-    outs = [jax.ShapeDtypeStruct((across,) + shape, jnp.bfloat16)]
+    outs = [
+        jax.ShapeDtypeStruct((across, along, members, lanes), jnp.float32),
+        jax.ShapeDtypeStruct((across,) + shape, jnp.bfloat16),
+    ]
     if halves:
         outs += [jax.ShapeDtypeStruct((across // 2,) + shape, jnp.bfloat16)] * 2
 
     def kernel(state_ref, rock_ref, *refs):
-        packed, outward, inward = refs[:3] if halves else (refs[0], None, None)
-        pack_kernel(state_ref, rock_ref, packed, outward, inward, refs[-1])
+        own, packed = refs[:2]
+        outward, inward = refs[2:4] if halves else (None, None)
+        pack_kernel(state_ref, rock_ref, own, packed, outward, inward, refs[-1])
 
     return pl.pallas_call(
         kernel,
@@ -63,42 +76,55 @@
     )(state_init.reshape(-1, lanes), rock_type)
 
 
+WELL_CHUNK = 8
+
+
 def inflow_kernel(cells_ref, rate_ref, out_ref):
     wide, total_y, group, lanes = out_ref.shape
     layers = lanes // 2
-    wells = rate_ref.shape[1]
+    wells = cells_ref.shape[0]
     first, _ = place(wide)
+    start = first * total_y * layers
+    size = wide * total_y * layers
     out_ref[...] = jnp.zeros_like(out_ref)
     lane = lax.broadcasted_iota(jnp.int32, (group, lanes), 1)
-    well = lax.broadcasted_iota(jnp.int32, rate_ref.shape, 1)
-
-    def one(w, carry):
-        cell = cells_ref[w]
-        column = cell // layers
-        z = cell - column * layers
-        row = column // total_y
-        y = column - row * total_y
-        x = row - first
-
-        @pl.when((x >= 0) & (x < wide))
+
+    def one(w):
+        near = cells_ref[w] - start
+
+        @pl.when((near >= 0) & (near < size))
         def _():
-            rate = jnp.sum(jnp.where(well == w, rate_ref[...], 0.0), axis=1, keepdims=True) * DT_PRESSURE
-            low = jnp.where(lane == z, rate[:group], 0.0)
-            high = jnp.where(lane == z + layers, rate[group:], 0.0)
-            out_ref[x, y] = out_ref[x, y] + low + high
-
+            column = lax.div(near, layers)
+            z = near - column * layers
+            x = lax.div(column, total_y)
+            y = column - x * total_y
+            rate = rate_ref[w] * DT_PRESSURE
+            out_ref[x, y] = out_ref[x, y] + jnp.where((lane == z) | (lane == z + layers), rate, 0.0)
+
+    def some(c, carry):
+        for i in range(WELL_CHUNK):
+            one(c * WELL_CHUNK + i)
         return carry
 
-    lax.fori_loop(0, wells, one, 0)
+    lax.fori_loop(0, wells // WELL_CHUNK, some, 0)
+    for w in range(wells // WELL_CHUNK * WELL_CHUNK, wells):
+        one(w)
 
 
 def well_inflow(well_cells, well_rate, wide, total_y, lanes):
+    members, wells = well_rate.shape
+    group = members // 2
+    layers = lanes // 2
+    rate = jnp.moveaxis(well_rate.reshape(2, group, wells), 2, 0)[..., None]
+    rate = jnp.broadcast_to(rate, (wells, 2, group, layers))
+    rate = jnp.concatenate([rate[:, 0], rate[:, 1]], -1)
     return pl.pallas_call(
         inflow_kernel,
-        out_shape=jax.ShapeDtypeStruct((wide, total_y, well_rate.shape[0] // 2, lanes), jnp.float32),
+        out_shape=jax.ShapeDtypeStruct((wide, total_y, group, lanes), jnp.float32),
         in_specs=[pl.BlockSpec(memory_space=pltpu.SMEM), pl.BlockSpec(memory_space=pltpu.VMEM)],
         compiler_params=pltpu.CompilerParams(vmem_limit_bytes=VMEM_LIMIT),
-    )(well_cells, well_rate)
+        cost_estimate=pl.CostEstimate(flops=2 * 10**9, bytes_accessed=2**20, transcendentals=0),
+    )(well_cells, rate)
 
 
 def roll(value, shift):
@@ -125,13 +151,13 @@
 
 def flux_kernel(fast, *refs):
     if fast:
-        state_ref, packed, other, beside, cross = refs[:5]
+        own_ref, packed, other, beside, cross = refs[:5]
         refs = refs[5:]
     else:
         slab = refs[0]
         refs = refs[1:]
-    table, inflow, basis_hbm, snaps, inner_su, inner_ss, fin, send = refs[:8]
-    press_a, sat_a, press_b, sat_b, rock, perm, w12, w06, carry, history, basis, sem = refs[8:]
+    table, inflow, inner_uu, basis_hbm, snaps, keep, give, fin, send = refs[:9]
+    press_a, sat_a, press_b, sat_b, rock, perm, w12, w06, carry, history, sums, basis, sem = refs[9:]
     wide, total_y = inflow.shape[:2]
     group, lanes = inflow.shape[2:]
     layers = lanes // 2
@@ -144,16 +170,12 @@
     lane_y = lax.broadcasted_iota(jnp.int32, (along, lanes), 1)
     sec = lax.axis_index("sec")
 
-    def put(x, y, low, high):
-        p, s = halves_swap(low, high, left_lanes, layers)
-        press_a[x, y] = p
-        sat_a[x, y] = s
-
     def put_packed(ref, count, x_at, block):
         def row(x, c):
             for y in range(along):
                 value = ref[x, y].astype(jnp.float32)
-                put(x_at + x, block * along + y, value[:group], value[group:])
+                press_a[x_at + x, block * along + y] = value[:group]
+                sat_a[x_at + x, block * along + y] = value[group:]
             rock[x_at + x, block] = ref[x, along].astype(jnp.float32)[:along]
             return c
 
@@ -165,11 +187,8 @@
 
         def own(x, c):
             for y in range(along):
-                at = x * along + y
-                stride = across * along
-                low = state_ref[pl.ds(at, group, stride=stride), :]
-                high = state_ref[pl.ds(at + group * stride, group, stride=stride), :]
-                put(here + x, sec * along + y, low, high)
+                press_a[here + x, sec * along + y] = own_ref[x, y, :group]
+                sat_a[here + x, sec * along + y] = own_ref[x, y, group:]
             rock[here + x, sec] = packed[x, along].astype(jnp.float32)[:along]
             return c
 
@@ -191,14 +210,15 @@
         inside = ((first + x >= 0) & (first + x < total_x)).astype(jnp.float32)
         for block in range(blocks):
             kind = rock[x, block]
+            values = [jnp.zeros((along, lanes), jnp.float32)] * 3
+            for r in range(table.shape[1]):
+                here = kind == float(r)
+                values = [jnp.where(here, table[d, r], values[d]) for d in range(3)]
             for d in range(3):
-                value = jnp.zeros((along, lanes), jnp.float32)
-                for r in range(table.shape[1]):
-                    value = jnp.where(kind == float(r), table[d, r], value)
-                perm[d, x, pl.ds(block * along, along), :] = value * inside
+                perm[d, x, pl.ds(block * along, along), :] = values[d] * inside
         return c
 
-    lax.fori_loop(0, wide, look_up, 0)
+    several(wide, look_up, 4)
     for d in range(3):
         perm[d, wide] = jnp.zeros(perm.shape[2:], jnp.float32)
     perm[1, :, total_y:, :] = jnp.zeros((wide + 1, perm.shape[2] - total_y, lanes), jnp.float32)
@@ -215,7 +235,7 @@
                 w06[d, x, block] = DT_SATURATION * weight
         return c
 
-    lax.fori_loop(0, wide, weigh, 0)
+    several(wide, weigh, 4)
 
     def spread(ref, d, x, block, j):
         return jnp.broadcast_to(ref[d, x, block, j : j + 1, :], (group, lanes))
@@ -228,55 +248,69 @@
         )
 
     buffers = [(press_a, sat_a), (press_b, sat_b)]
+    chunk = along * next(n for n in (2, 1) if blocks % n == 0)
+    chunks = total_y // chunk
+
+    def columns(c):
+        return [(c * chunk + i, c * (chunk // along) + i // along, i % along) for i in range(chunk)]
+
     for step in range(STEPS):
         (p_ref, s_ref), (p_new, s_new) = buffers[step % 2], buffers[(step + 1) % 2]
 
-        def begin(block, c):
-            for j in range(along):
-                carry[0, block * along + j], carry[1, block * along + j] = x_face(p_ref, s_ref, step, block, j)
-            return c
-
-        lax.fori_loop(0, blocks, begin, 0)
-
-        def one_row(x, c):
-            def one_block(block, back):
-                back_p, back_s = back
-                for j in range(along):
-                    y = block * along + j
-                    p, s = p_ref[x, y], s_ref[x, y]
-                    xp, xs = x_face(p_ref, s_ref, x, block, j)
-                    yp, ys = face(
-                        spread(w12, 1, x, block, j), spread(w06, 1, x, block, j),
-                        p, s, p_ref[x, y + 1], s_ref[x, y + 1],
-                    )
-                    zp, zs = face(
-                        spread(w12, 2, x, block, j), spread(w06, 2, x, block, j),
-                        p, s, roll(p, lanes - 1), roll(s, lanes - 1),
-                    )
-                    p_new[x, y] = p + (xp - carry[0, y]) + (yp - back_p) + (zp - roll(zp, 1)) + inflow[x, y]
-                    s_new[x, y] = s + (xs - carry[1, y]) + (ys - back_s) + (zs - roll(zs, 1))
-                    carry[0, y] = xp
-                    carry[1, y] = xs
-                    back_p, back_s = yp, ys
-                return back_p, back_s
-
-            lax.fori_loop(0, blocks, one_block, (zero, zero))
-            return c
-
-        lax.fori_loop(step + 1, wide - 1 - step, one_row, 0)
-
-        def save(at, c):
-            x, block = at // blocks, at % blocks
-            for j in range(along):
-                y = block * along + j
-                low, high = halves_swap(p_new[STEPS + x, y], s_new[STEPS + x, y], left_lanes, layers)
-                history[x * total_y + y, step * group : (step + 1) * group] = low
-                history[x * total_y + y, (STEPS + step) * group : (STEPS + step + 1) * group] = high
-                if step == STEPS - 1 and not fast:
-                    fin[x, block, j] = jnp.concatenate([low, high], 0)
-            return c
-
-        lax.fori_loop(0, rows * blocks, save, 0)
+        def begin(c, none):
+            for y, block, j in columns(c):
+                carry[0, y], carry[1, y] = x_face(p_ref, s_ref, step, block, j)
+            return none
+
+        lax.fori_loop(0, chunks, begin, 0)
+        span = wide - 2 - 2 * step
+        deep = 2 if span % 2 == 0 else 1
+
+        def some_rows(r, none):
+            x0 = step + 1 + r * deep
+
+            def one_chunk(c, back):
+                back = list(back)
+                for y, block, j in columns(c):
+                    before = carry[0, y], carry[1, y]
+                    for i in range(deep):
+                        x = x0 + i
+                        p, s = p_ref[x, y], s_ref[x, y]
+                        xp, xs = x_face(p_ref, s_ref, x, block, j)
+                        yp, ys = face(
+                            spread(w12, 1, x, block, j), spread(w06, 1, x, block, j),
+                            p, s, p_ref[x, y + 1], s_ref[x, y + 1],
+                        )
+                        zp, zs = face(
+                            spread(w12, 2, x, block, j), spread(w06, 2, x, block, j),
+                            p, s, roll(p, lanes - 1), roll(s, lanes - 1),
+                        )
+                        back_p, back_s = back[2 * i : 2 * i + 2]
+                        p_new[x, y] = p + (xp - before[0]) + (yp - back_p) + (zp - roll(zp, 1)) + inflow[x, y]
+                        s_new[x, y] = s + (xs - before[1]) + (ys - back_s) + (zs - roll(zs, 1))
+                        before = xp, xs
+                        back[2 * i : 2 * i + 2] = [yp, ys]
+                    carry[0, y], carry[1, y] = before
+                return tuple(back)
+
+            lax.fori_loop(0, chunks, one_chunk, (zero,) * (2 * deep))
+            return none
+
+        lax.fori_loop(0, span // deep, some_rows, 0)
+
+        def save(x, none):
+            def save_chunk(c, none):
+                for y, block, j in columns(c):
+                    low, high = halves_swap(p_new[STEPS + x, y], s_new[STEPS + x, y], left_lanes, layers)
+                    history[x * total_y + y, step * group : (step + 1) * group] = low
+                    history[x * total_y + y, (STEPS + step) * group : (STEPS + step + 1) * group] = high
+                    if step == STEPS - 1 and not fast:
+                        fin[x, block, j] = jnp.concatenate([low, high], 0)
+                return none
+
+            return lax.fori_loop(0, chunks, save_chunk, none)
+
+        several(rows, save, 2)
 
     if fast:
         last = slice((STEPS - 1) * group, STEPS * group)
@@ -289,35 +323,104 @@
                     ref[x, j, group:] = history[at, past]
 
     copy.wait()
-    inner_su[...] = jnp.zeros_like(inner_su)
-    inner_ss[...] = jnp.zeros_like(inner_ss)
     count = basis.shape[2]
-
-    def add_pair(q, c):
-        pair = [history[2 * q].astype(jnp.bfloat16), history[2 * q + 1].astype(jnp.bfloat16)]
-        snaps[2 * q] = pair[0]
-        snaps[2 * q + 1] = pair[1]
-        both = jnp.concatenate(pair, 1)
-        inner_su[...] += jnp.dot(both, basis[pl.ds(2 * q, 2)].reshape(2 * lanes, count), preferred_element_type=jnp.float32)
-        inner_ss[...] += lax.dot_general(both, both, (((1,), (1,)), ((), ())), preferred_element_type=jnp.float32)
-        return c
-
-    lax.fori_loop(0, rows * total_y // 2, add_pair, 0)
-
-
-def flux(fields, perm_table, inflow, basis_blocks, along):
+    cells = rows * total_y
+    snap_count = 2 * STEPS * group
+    run = next(n for n in (16, 8, 4, 2, 1) if cells % n == 0)
+    inner_su = jnp.zeros((snap_count, count), jnp.float32)
+    inner_ss = jnp.zeros((snap_count, snap_count), jnp.float32)
+    for q in range(0, cells, run):
+        part = [history[q + i].astype(jnp.bfloat16) for i in range(run)]
+        for i in range(run):
+            snaps[q + i] = part[i]
+        both = jnp.concatenate(part, 1)
+        inner_su += jnp.dot(both, basis[q : q + run].reshape(run * lanes, count), preferred_element_type=jnp.float32)
+        inner_ss += lax.dot_general(both, both, (((1,), (1,)), ((), ())), preferred_element_type=jnp.float32)
+    fold(sums, inner_uu, inner_su, inner_ss)
+    half = sums.shape[0] // 2
+    core = lax.rem(lax.axis_index("gx"), 2)
+    keep[...] = sums[pl.ds(pl.multiple_of(core * half, 8), half), :]
+    give[...] = sums[pl.ds(pl.multiple_of((1 - core) * half, 8), half), :]
+
+
+def several(total, one, most):
+    deep = next(n for n in range(most, 0, -1) if total % n == 0)
+
+    def some(r, none):
+        for i in range(deep):
+            one(r * deep + i, 0)
+        return none
+
+    lax.fori_loop(0, total // deep, some, 0)
+
+
+def folded_rows(count, snap_count):
+    used = count + snap_count * (count // LANE) + snap_count // 2 + 1
+    return -(-used // 16) * 16
+
+
+def lower_mask(side):
+    row = lax.broadcasted_iota(jnp.int32, (side, side), 0)
+    column = lax.broadcasted_iota(jnp.int32, (side, side), 1)
+    return row > column, row == column
+
+
+def fold(sums, inner_uu, inner_su, inner_ss):
+    below, on = lower_mask(LANE)
+    first = inner_uu[:LANE, :LANE]
+    sums[:LANE] = jnp.where(below, first, inner_uu[LANE:, LANE:])
+    sums[LANE : 2 * LANE] = inner_uu[LANE:, :LANE]
+    snap_count = inner_su.shape[0]
+    at = 2 * LANE
+    for tile in range(2):
+        sums[at : at + snap_count] = inner_su[:, tile * LANE : (tile + 1) * LANE]
+        at += snap_count
+    half = snap_count // 2
+    sums[at : at + half] = jnp.concatenate([inner_ss[:half], inner_ss[half:]], 1)
+    at += half
+    diagonal = jnp.sum(jnp.where(on, first, 0.0), axis=0, keepdims=True)
+    left = sums.shape[0] - at
+    sums[at:] = jnp.broadcast_to(diagonal, (left, LANE))
+
+
+def unfold(sums, grams, snap_count, scale):
+    count = 2 * LANE
+    below, on = lower_mask(LANE)
+    mixed = sums[:LANE] * scale
+    cross = sums[LANE : 2 * LANE] * scale
+    at = count + 2 * snap_count
+    half = snap_count // 2
+    diagonal = sums[at + half : at + half + 1] * scale
+    low = jnp.where(below, mixed, 0.0)
+    high = jnp.where(below, 0.0, mixed)
+    grams[:LANE, :LANE] = low + low.T + jnp.where(on, jnp.broadcast_to(diagonal, on.shape), 0.0)
+    grams[LANE:count, LANE:count] = high + jnp.where(on, 0.0, high).T
+    grams[LANE:count, :LANE] = cross
+    grams[:LANE, LANE:count] = cross.T
+    for tile in range(2):
+        part = sums[count + tile * snap_count : count + (tile + 1) * snap_count] * scale
+        grams[count : count + snap_count, tile * LANE : (tile + 1) * LANE] = part
+        wide = jnp.concatenate([part, jnp.zeros((LANE - snap_count, LANE), jnp.float32)], 0)
+        grams[tile * LANE : (tile + 1) * LANE, count:] = wide.T
+    folded = sums[at : at + half] * scale
+    grams[count : count + half, count : count + snap_count] = folded[:, :snap_count]
+    grams[count + half : count + snap_count, count : count + snap_count] = folded[:, snap_count:]
+
+
+def flux(fields, perm_table, inflow, inner_uu, basis_blocks, along):
     fast = len(fields) > 1
     wide, total_y, group, lanes = inflow.shape
     blocks = total_y // along
     rows = wide - 2 * STEPS
     count = basis_blocks.shape[-1]
     snaps = 2 * STEPS * group
+    folded = folded_rows(count, snaps)
     f32 = jnp.float32
     fin = (rows, along, 2 * group, lanes) if fast else (rows, blocks, along, 2 * group, lanes)
     outs = [
         jax.ShapeDtypeStruct((rows * total_y, snaps, lanes), jnp.bfloat16),
-        jax.ShapeDtypeStruct((snaps, count), f32),
-        jax.ShapeDtypeStruct((snaps, snaps), f32),
+        jax.ShapeDtypeStruct((folded // 2, LANE), f32),
+        jax.ShapeDtypeStruct((folded // 2, LANE), f32),
         jax.ShapeDtypeStruct(fin, f32),
         jax.ShapeDtypeStruct(fin if fast else (8, lanes), f32),
     ]
@@ -327,7 +430,7 @@
         lambda *refs: flux_kernel(fast, *refs),
         out_shape=outs,
         in_specs=[whole] * len(fields)
-        + [pl.BlockSpec(memory_space=pltpu.SMEM), whole, pl.BlockSpec(memory_space=pl.ANY)],
+        + [pl.BlockSpec(memory_space=pltpu.SMEM), whole, whole, pl.BlockSpec(memory_space=pl.ANY)],
         scratch_shapes=[
             state, state, state, state,
             pltpu.VMEM((wide, blocks, along, lanes), f32),
@@ -336,11 +439,12 @@
             pltpu.VMEM((3, wide, blocks, along, lanes), f32),
             pltpu.VMEM((2, total_y, group, lanes), f32),
             pltpu.VMEM((rows * total_y, snaps, lanes), f32),
+            pltpu.VMEM((folded, LANE), f32),
             pltpu.VMEM(basis_blocks.shape, jnp.bfloat16),
             pltpu.SemaphoreType.DMA,
         ],
         compiler_params=pltpu.CompilerParams(vmem_limit_bytes=VMEM_LIMIT),
-    )(*fields, perm_table, inflow, basis_blocks)
+    )(*fields, perm_table, inflow, inner_uu, basis_blocks)
 
 
 def unpack_kernel(parts, *refs):
@@ -368,17 +472,19 @@
     return out.reshape(members, across, along, lanes)
 
 
-def all_sum(value):
-    for axis in AXES:
-        count = lax.axis_size(axis)
-        if count & (count - 1):
-            value = lax.psum(value, axis)
-            continue
-        stride = 1
-        while stride < count:
-            value = value + lax.ppermute(value, axis, [(i, i ^ stride) for i in range(count)])
-            stride *= 2
-    return value
+def all_sum(keep, give):
+    counts = [lax.axis_size(axis) for axis in AXES]
+    total = counts[0] * counts[1]
+    pair = counts[1]
+    swap = [(i, i ^ pair) for i in range(total)]
+    value = keep + lax.ppermute(give, AXES, swap)
+    masks = [1 << b for b in range(total.bit_length() - 1) if 1 << b != pair]
+    turned = list(masks)
+    for i in range(0, len(masks) - 1, 2):
+        turned[i], turned[i + 1] = masks[i + 1], masks[i]
+    for even, odd in zip(masks, turned):
+        value = value + lax.ppermute(value, AXES, [(i, i ^ (odd if i & pair else even)) for i in range(total)])
+    return value, lax.ppermute(value, AXES, swap)
 
 
 def to_bf16(value):
@@ -439,9 +545,14 @@
             change = hdot(left, done[:, base - first:], 0, 0)
             aug[rest:, base:] = aug[rest:, base:] - change[rest - base:]
 
-def small_kernel(gram_ref, sigma_ref, weight_ref, sigma_out, aug):
+def small_kernel(scale, mine_ref, other_ref, sigma_ref, high_ref, low_ref, snap_ref, sigma_out, aug, sums, gram_ref):
     count = sigma_ref.shape[1]
     snaps = (gram_ref.shape[0] - count) // 2
+    half = sums.shape[0] // 2
+    core = lax.rem(lax.axis_index("gx"), 2)
+    sums[pl.ds(pl.multiple_of(core * half, 8), half), :] = mine_ref[...]
+    sums[pl.ds(pl.multiple_of((1 - core) * half, 8), half), :] = other_ref[...]
+    unfold(sums, gram_ref, 2 * snaps, scale)
     eye = lax.broadcasted_iota(jnp.int32, (count, count), 0) == lax.broadcasted_iota(jnp.int32, (count, count), 1)
     pad = LANE - snaps
     sig2 = sigma_ref[...] * sigma_ref[...]
@@ -480,19 +591,72 @@
         if group == 0:
             prior = jnp.concatenate([step, aug[:, 2 * count:]], 1)
         else:
-            weight_ref[:, :count + LANE] = hdot(step, prior)
-            weight_ref[:, count + LANE:] = aug[:, 2 * count:]
+            final = hdot(step, prior)
+            high = final[:, :count].astype(jnp.bfloat16)
+            high_ref[...] = high
+            low_ref[...] = (final[:, :count] - high.astype(jnp.float32)).astype(jnp.bfloat16)
+            both = jnp.concatenate([final[:, count:].T[:snaps], aug[:, 2 * count:].T[:snaps]], 0)
+            high = both.astype(jnp.bfloat16)
+            snap_ref[:2 * snaps] = high
+            snap_ref[2 * snaps:] = (both - high.astype(jnp.float32)).astype(jnp.bfloat16)
     sigma_out[...] = jnp.sqrt(sig2)
 
-def small(grams, sigma):
+def small(mine, other, sigma, snap_count, rows_total):
     count = sigma.shape[0]
-    w, s = pl.pallas_call(
-        small_kernel,
-        out_shape=(jax.ShapeDtypeStruct((count, count + 2 * LANE), jnp.float32), jax.ShapeDtypeStruct((1, count), jnp.float32)),
-        scratch_shapes=[pltpu.VMEM((count, 2 * count + LANE), jnp.float32)],
+    rows = count + snap_count
+    high, low, snap_weights, sigma_out = pl.pallas_call(
+        functools.partial(small_kernel, 1.0 / rows_total),
+        out_shape=(
+            jax.ShapeDtypeStruct((count, count), jnp.bfloat16),
+            jax.ShapeDtypeStruct((count, count), jnp.bfloat16),
+            jax.ShapeDtypeStruct((2 * snap_count, count), jnp.bfloat16),
+            jax.ShapeDtypeStruct((1, count), jnp.float32),
+        ),
+        scratch_shapes=[
+            pltpu.VMEM((count, 2 * count + LANE), jnp.float32),
+            pltpu.VMEM((2 * mine.shape[0], LANE), jnp.float32),
+            pltpu.VMEM((rows, count + LANE), jnp.float32),
+        ],
         compiler_params=pltpu.CompilerParams(vmem_limit_bytes=VMEM_LIMIT),
-    )(grams, sigma.reshape(1, count))
-    return w, s.reshape(count)
+        cost_estimate=pl.CostEstimate(flops=2 * 10**10, bytes_accessed=2**20, transcendentals=0),
+    )(mine, other, sigma.reshape(1, count))
+    return high, low, snap_weights, sigma_out.reshape(count)
+
+
+def renew_kernel(basis_ref, snaps_ref, high_ref, low_ref, snap_ref, out_ref):
+    lanes = snaps_ref.shape[2]
+    flat = basis_ref[...]
+    turned = (((1,), (1,)), ((), ()))
+    value = lax.dot_general(flat, high_ref[...], turned, preferred_element_type=jnp.float32)
+    value += lax.dot_general(flat, low_ref[...], turned, preferred_element_type=jnp.float32)
+    for q in range(snaps_ref.shape[0]):
+        part = snaps_ref[q]
+        part = lax.dot_general(
+            jnp.concatenate([part, part], 0), snap_ref[...], (((0,), (0,)), ((), ())),
+            preferred_element_type=jnp.float32,
+        )
+        out_ref[q * lanes : (q + 1) * lanes] = (value[q * lanes : (q + 1) * lanes] + part).astype(jnp.bfloat16)
+
+
+def renew(flat, snaps, high, low, snap_weights):
+    cells, snap_count, lanes = snaps.shape
+    count = flat.shape[1]
+    run = next(n for n in (8, 4, 2, 1) if cells % n == 0)
+    same = lambda i: (0, 0)
+    return pl.pallas_call(
+        renew_kernel,
+        out_shape=jax.ShapeDtypeStruct(flat.shape, jnp.bfloat16),
+        grid=(cells // run,),
+        in_specs=[
+            pl.BlockSpec((run * lanes, count), lambda i: (i, 0)),
+            pl.BlockSpec((run, snap_count, lanes), lambda i: (i, 0, 0)),
+            pl.BlockSpec((count, count), same),
+            pl.BlockSpec((count, count), same),
+            pl.BlockSpec((2 * snap_count, count), same),
+        ],
+        out_specs=pl.BlockSpec((run * lanes, count), lambda i: (i, 0)),
+        compiler_params=pltpu.CompilerParams(vmem_limit_bytes=VMEM_LIMIT),
+    )(flat, snaps, high, low, snap_weights)
 
 
 def body(state_init, rock_type, perm_table, well_cells, well_rate, basis_in, singular):
@@ -506,7 +670,7 @@
     fast = sec_count == 2 and across == 2 * STEPS
     inflow = well_inflow(well_cells, well_rate, wide, total_y, lanes)
     if fast:
-        packed, outward, inward = pack(state_init, rock_type, True)
+        own, packed, outward, inward = pack(state_init, rock_type, True)
         straight, crossed = [], []
         for r in range(gx_count):
             if r > 0:
@@ -518,9 +682,9 @@
         other = lax.ppermute(packed, "sec", [(0, 1), (1, 0)])
         cross = lax.ppermute(inward, AXES, crossed)
         beside = lax.ppermute(outward, AXES, straight)
-        fields = (state_init.reshape(-1, lanes), packed, other, beside, cross)
+        fields = (own, packed, other, beside, cross)
     else:
-        (packed,) = pack(state_init, rock_type, False)
+        _, packed = pack(state_init, rock_type, False)
         slab = lax.all_gather(packed, "sec", axis=1)
         low = lax.ppermute(slab[across - STEPS :], "gx", [(i, i + 1) for i in range(gx_count - 1)])
         high = lax.ppermute(slab[:STEPS], "gx", [(i + 1, i) for i in range(gx_count - 1)])
@@ -529,32 +693,21 @@
     flat = basis_in.reshape(-1, count)
     rows_total = flat.shape[0] * gx_count * sec_count
     inner_uu = lax.dot_general(flat, flat, (((0,), (0,)), ((), ())), preferred_element_type=jnp.float32)
-    snaps, inner_su, inner_ss, fin, send = flux(fields, perm_table, inflow, flat.reshape(-1, lanes, count), along)
+    snaps, keep, give, fin, send = flux(
+        fields, perm_table, inflow, inner_uu, flat.reshape(-1, lanes, count), along
+    )
+    mine, others = all_sum(keep, give)
     if fast:
+        send, mine = lax.optimization_barrier((send, mine))
         received = lax.ppermute(send, "sec", [(0, 1), (1, 0)])
+    high, low, snap_weights, sigma = small(mine, others, singular, snaps.shape[1], rows_total)
+    if fast:
         state_out = unpack((fin, received))
     else:
         moved = lax.all_to_all(fin, "sec", split_axis=1, concat_axis=0, tiled=True)
         state_out = unpack((moved.reshape(across, along, members, lanes),))
-
-    snap_count = snaps.shape[1]
-    grams = jnp.concatenate(
-        [jnp.concatenate([inner_uu, inner_su.T], 1), jnp.concatenate([inner_su, inner_ss], 1)], 0
-    )
-    grams = all_sum(grams) / rows_total
-    turned, sigma = small(grams, singular)
-    half = snap_count // 2
-    final_w = jnp.concatenate(
-        [turned[:, :count], turned[:, count : count + half], turned[:, count + LANE : count + LANE + half]], 1
-    ).T
-    high = to_bf16(final_w)
-    low = to_bf16(final_w - high.astype(jnp.float32))
-    columns = jnp.moveaxis(snaps, 1, 2).reshape(-1, snap_count)
-    both = jnp.concatenate([flat, columns], 1)
-    fresh = jnp.dot(both, high, preferred_element_type=jnp.float32) + jnp.dot(
-        both, low, preferred_element_type=jnp.float32
-    )
-    return state_out, to_bf16(fresh).reshape(basis_in.shape), sigma
+    fresh = renew(flat, snaps, high, low, snap_weights)
+    return state_out, fresh.reshape(basis_in.shape), sigma
 
 
 def solution(mesh):

time: 152 us -> 88 us (0.58); the launches traced: 150 us -> 87.7 us
  waiting for transfers between devices: 64.3 us -> 18 us
  Pallas kernels: 57 us -> 46.3 us
  matrix products: 14 us -> 4.74 us
  starting transfers between devices: 9.92 us -> 14.1 us
    ppermute x5 -> x6, waiting for transfers between devices: 49.7 us -> 18 us  [the longest x4 16.4 us: all_sum(): lax.ppermute(value, AXES, [(i, i ^ (odd if i & pair else even)) for i in...]
    ppermute x1, waiting for transfers between devices: 14.7 us -> 0.01 us  [body(): received = lax.ppermute(send, 'sec', [(0, 1), (1, 0)])]
    pallas_call x1, Pallas kernels: 21.5 us -> 8.16 us  [flux(): pl.pallas_call(lambda *refs: flux_kernel(fast, *refs), out_shape=outs, in...]
    dot_general x2 -> x0, matrix products: 9.24 us -> none  [the longest x1 5.17 us: body(): jnp.dot(both, high, preferred_element_type=jnp.float32)]
    pallas_call x1 -> x2, Pallas kernels: 26.3 us -> 33.1 us  [the longest x1 26.9 us: small(): pl.pallas_call(functools.partial(small_kernel, 1.0 / rows_total), out_sha...]
    ppermute x5 -> x6, starting transfers between devices: 2.5 us -> 6.97 us  [the longest x1 4.69 us: all_sum(): return (value, lax.ppermute(value, AXES, swap))]
    pallas_call x1, Pallas kernels: 7.83 us -> 3.48 us  [well_inflow(): pl.pallas_call(inflow_kernel, out_shape=jax.ShapeDtypeStruct((wide, total...]
  transfers between devices with their start and end apart: 9 -> 10, of which waited for: 5 -> 6; matrix products, arithmetic and copies ran while one was open for 4% -> 8% of each run, Pallas kernels for 6% -> 42%
where the time goes in v1:
time: 88 us; the launch traced here: 87.7 us
  Pallas kernels  46.3 us (53%)
  waiting for transfers between devices  18 us (20%)
  starting transfers between devices  14.1 us (16%)
  matrix products  4.74 us (5%)
  local copies, waits for them, and re-layouts  3.3 us (4%)
    pallas_call x1, Pallas kernels, small(): pl.pallas_call(functools.partial(small_kernel, 1.0 / rows_total), out_sha...  26.9 us
    ppermute x4, waiting for transfers between devices, all_sum(): lax.ppermute(value, AXES, [(i, i ^ (odd if i & pair else even)) for i in...  16.4 us
    pallas_call x1, Pallas kernels, flux(): pl.pallas_call(lambda *refs: flux_kernel(fast, *refs), out_shape=outs, in...  8.16 us
    pallas_call x1, Pallas kernels, renew(): pl.pallas_call(renew_kernel, out_shape=jax.ShapeDtypeStruct(flat.shape, j...  6.23 us
    dot_general x1, matrix products, body(): lax.dot_general(flat, flat, (((0,), (0,)), ((), ())), preferred_element_t...  4.74 us
    ppermute x1, starting transfers between devices, all_sum(): return (value, lax.ppermute(value, AXES, swap))  4.69 us
    ppermute x1, starting transfers between devices, body(): beside = lax.ppermute(outward, AXES, straight)  3.67 us
    pallas_call x1, Pallas kernels, well_inflow(): pl.pallas_call(inflow_kernel, out_shape=jax.ShapeDtypeStruct((wide, total...  3.48 us
  transfers between devices with their start and end apart: 10, of which 6 were waited for; matrix products, arithmetic and copies ran while one was open for 8% of the time, Pallas kernels for 42%

profile of v1, /device:TPU:25, one launch (start us, length us, event | category | flops | bytes accessed | tf_op | source)
XLA Modules:
  0.0 87.7 jit_solution(12654172742058976430)
XLA Ops:
  0.6 0.0 copy-start.1
  0.6 1.0 %copy-done.1 = f32[16,8,8,128]{3,2,1,0:T(8,128)S(1)} copy-done((f32[16,8,8,128]{3,2,1,0:T(8,128)S(1)}, f32[16,8,8,128]{3,2,1,0:T(8,128)}, u32[]{:S(2)}) %copy-start.1) | copy-done | bytes 524312
  1.7 0.0 copy-start.2
  1.7 0.7 copy-done.2
  2.4 0.4 shard_map.94
  2.8 3.7 %collective-permute-start.1 = (bf16[4,9,16,128]{3,2,1,0:T(8,128)(2,1)S(1)}, bf16[4,9,16,128]{3,2,1,0:T(8,128)(2,1)S(1)}, u32[]{:S(2)}, u32[]{:S(2)}) collective-permute-start(bf16[4,9,16,128]{3,2,1,0:T(8,128)(2,1)S(1)} %get-tuple-element.20), channel_id=1, source_target_pairs={{3,1},{0,2},{5,3},{2,4},{7,5},{4,6},{9,7},{6,8},{11,9},{8,10},{13,... | collective-permute-start | bytes 442376 | tf_op jit(solution)/shard_map/ppermute | solution.py:684
  6.5 2.7 %collective-permute-start.2 = (bf16[4,9,16,128]{3,2,1,0:T(8,128)(2,1)S(1)}, bf16[4,9,16,128]{3,2,1,0:T(8,128)(2,1)S(1)}, u32[]{:S(2)}, u32[]{:S(2)}) collective-permute-start(bf16[4,9,16,128]{3,2,1,0:T(8,128)(2,1)S(1)} %get-tuple-element.21), channel_id=1, source_target_pairs={{2,1},{1,2},{4,3},{3,4},{6,5},{5,6},{8,7},{7,8},{10,9},{9,10},{12,... | collective-permute-start | bytes 442376 | tf_op jit(solution)/shard_map/ppermute | solution.py:683
  9.3 0.4 collective-permute-start
  9.7 0.8 copy.10
  10.6 4.7 %convolution_bitcast_fusion.refs_7_ = f32[256,256]{1,0:T(8,128)S(1)} fusion(bf16[4,16,128,256]{3,2,1,0:T(8,128)(2,1)} %param.12), kind=kOutput, calls=%fused_computation | convolution fusion | flops 1073741824 | bytes 4456448 | tf_op jit(solution)/shard_map/dot_general | solution.py:695
  15.3 0.0 copy-start.4
  15.3 0.3 broadcast_in_dim.13
  15.7 0.3 broadcast_in_dim.15
  16.0 0.3 pad_maximum_fusion.rate_ref
  16.3 0.0 copy-done.4
  16.3 0.0 copy-start.3
  16.4 3.5 %shard_map.95.refs_6_ = f32[12,16,8,128]{3,2,1,0:T(8,128)S(1)} custom-call(s32[256]{0:T(256)S(1)} %copy-done.4, f32[256,8,128]{2,1,0:T(8,128)S(1)} %pad_maximum_fusion.rate_ref), custom_call_target="tpu_custom_call" | custom-call | flops 2000000000 | bytes 1048576 | tf_op jit(solution)/shard_map/pallas_call | solution.py:121
  19.9 0.0 copy-start.5
  19.9 0.0 collective-permute-done.1.refs_3_
  19.9 0.0 collective-permute-done.2.refs_4_
  19.9 0.0 collective-permute-done.refs_2_
  19.9 0.0 copy-done.3
  19.9 8.2 %shard_map.96 = (bf16[64,64,128]{2,1,0:T(8,128)(2,1)S(1)}, f32[216,128]{1,0:T(8,128)S(1)}, f32[216,128]{1,0:T(8,128)S(1)}, f32[4,8,16,128]{3,2,1,0:T(8,128)S(1)}, f32[4,8,16,128]{3,2,1,0:T(8,128)S(1)}) custom-call(f32[8,8,16,128]{3,2,1,0:T(8,128)S(1)} %get-tuple-element.18.refs_0_, bf16[8,9,16,128]{3,2,1,0:T(8,128)(2,1)S(1)} %get-tuple-element.19.refs_1_, ...), custom_call_target="tpu_custom_call" | custom-call | tf_op jit(solution)/shard_map/pallas_call | solution.py:429
  28.1 1.7 %collective-permute-start.3 = (f32[216,128]{1,0:T(8,128)S(1)}, f32[216,128]{1,0:T(8,128)S(1)}, u32[]{:S(2)}, u32[]{:S(2)}) collective-permute-start(f32[216,128]{1,0:T(8,128)S(1)} %get-tuple-element.25), channel_id=1, source_target_pairs={{0,2},{1,3},{2,0},{3,1},{4,6},{5,7},{6,4},{7,5},{8,10},{9,11},{10,... | collective-permute-start | bytes 331784 | tf_op jit(solution)/shard_map/ppermute | solution.py:480
  29.8 1.0 %collective-permute-done.3 = f32[216,128]{1,0:T(8,128)S(1)} collective-permute-done((f32[216,128]{1,0:T(8,128)S(1)}, f32[216,128]{1,0:T(8,128)S(1)}, u32[]{:S(2)}, u32[]{:S(2)}) %collective-permute-start.3) | collective-permute-done | bytes 110624 | tf_op jit(solution)/shard_map/ppermute | solution.py:480
  30.8 0.1 collective-permute-start.4
  30.8 3.9 %collective-permute-done.4 = f32[216,128]{1,0:T(8,128)S(1)} collective-permute-done((f32[216,128]{1,0:T(8,128)S(1)}, f32[216,128]{1,0:T(8,128)S(1)}, u32[]{:S(2)}, u32[]{:S(2)}) %collective-permute-start.4) | collective-permute-done | bytes 110624 | tf_op jit(solution)/shard_map/ppermute | solution.py:486
  34.7 0.3 collective-permute-start.5
  35.0 3.4 %collective-permute-done.5 = f32[216,128]{1,0:T(8,128)S(1)} collective-permute-done((f32[216,128]{1,0:T(8,128)S(1)}, f32[216,128]{1,0:T(8,128)S(1)}, u32[]{:S(2)}, u32[]{:S(2)}) %collective-permute-start.5) | collective-permute-done | bytes 110624 | tf_op jit(solution)/shard_map/ppermute | solution.py:486
  38.4 0.1 collective-permute-start.6
  38.5 5.5 %collective-permute-done.6 = f32[216,128]{1,0:T(8,128)S(1)} collective-permute-done((f32[216,128]{1,0:T(8,128)S(1)}, f32[216,128]{1,0:T(8,128)S(1)}, u32[]{:S(2)}, u32[]{:S(2)}) %collective-permute-start.6) | collective-permute-done | bytes 110624 | tf_op jit(solution)/shard_map/ppermute | solution.py:486
  44.1 0.1 collective-permute-start.7
  44.2 3.6 %collective-permute-done.7 = f32[216,128]{1,0:T(8,128)S(1)} collective-permute-done((f32[216,128]{1,0:T(8,128)S(1)}, f32[216,128]{1,0:T(8,128)S(1)}, u32[]{:S(2)}, u32[]{:S(2)}) %collective-permute-start.7) | collective-permute-done | bytes 110624 | tf_op jit(solution)/shard_map/ppermute | solution.py:486
  47.8 4.7 %collective-permute-start.9 = (f32[216,128]{1,0:T(8,128)S(1)}, f32[216,128]{1,0:T(8,128)S(1)}, u32[]{:S(2)}, u32[]{:S(2)}) collective-permute-start(f32[216,128]{1,0:T(8,128)S(1)} %add.19.mine_ref), channel_id=1, source_target_pairs={{0,2},{1,3},{2,0},{3,1},{4,6},{5,7},{6,4},{7,5},{8,10},{9,11},{10,... | collective-permute-start | bytes 331784 | tf_op jit(solution)/shard_map/ppermute | solution.py:487
  52.5 0.3 collective-permute-start.8
  52.8 0.7 collective-permute-done.9.other_ref
  53.4 0.0 copy-done.5
  53.5 0.0 copy-start
  53.5 26.9 %shard_map.98 = (bf16[256,256]{1,0:T(8,128)(2,1)S(1)}, bf16[256,256]{1,0:T(8,128)(2,1)S(1)}, bf16[128,256]{1,0:T(8,128)(2,1)S(1)}, f32[1,256]{1,0:T(1,128)}) custom-call(f32[216,128]{1,0:T(8,128)S(1)} %add.19.mine_ref, f32[216,128]{1,0:T(8,128)S(1)} %collective-permute-done.9.other_ref, f32[1,256]{1,0:T(1,128)S(1)} %bitcast.22), custom_call_target="tpu_custom_call" | custom-call | flops 20000000000 | bytes 1048576 | tf_op jit(solution)/shard_map/pallas_call | solution.py:607
  80.4 0.0 copy-done
  80.4 6.2 %shard_map.99 = bf16[8192,256]{1,0:T(8,128)(2,1)} custom-call(bf16[8192,256]{1,0:T(8,128)(2,1)S(1)} %bitcast.20, bf16[64,64,128]{2,1,0:T(8,128)(2,1)S(1)} %get-tuple-element.27.snaps_ref, bf16[256,256]{1,0:T(8,128)(2,1)S(1)} %get-tuple-element.29.high_ref, bf16[256,256]{1,0:T(8,128)(2,1)S(1)} %get-tuple-element.30.low_ref, ...), custom_call_target="tpu_custom_call" | custom-call | tf_op jit(solution)/shard_map/pallas_call | solution.py:646
  86.6 0.0 collective-permute-done.8.refs_1_
  86.6 1.1 %shard_map.97 = f32[1024,128]{1,0:T(8,128)} custom-call(f32[4,8,16,128]{3,2,1,0:T(8,128)S(1)} %get-tuple-element.22.refs_0_, f32[4,8,16,128]{3,2,1,0:T(8,128)S(1)} %collective-permute-done.8.refs_1_), custom_call_target="tpu_custom_call" | custom-call | tf_op jit(solution)/shard_map/pallas_call | solution.py:467
  (6 shorter events, 0.1 us)
Async XLA Ops:
  0.6 1.0 %copy-start.1 = (f32[16,8,8,128]{3,2,1,0:T(8,128)S(1)}, f32[16,8,8,128]{3,2,1,0:T(8,128)}, u32[]{:S(2)}) copy-start(f32[16,8,8,128]{3,2,1,0:T(8,128)} %param.7) | copy-start | bytes 1572868
  1.7 0.7 copy-start.2
  2.8 17.0 %collective-permute-start.1 = (bf16[4,9,16,128]{3,2,1,0:T(8,128)(2,1)S(1)}, bf16[4,9,16,128]{3,2,1,0:T(8,128)(2,1)S(1)}, u32[]{:S(2)}, u32[]{:S(2)}) collective-permute-start(bf16[4,9,16,128]{3,2,1,0:T(8,128)(2,1)S(1)} %get-tuple-element.20), channel_id=1, source_target_pairs={{3,1},{0,2},{5,3},{2,4},{7,5},{4,6},{9,7},{6,8},{11,9},{8,10},{13,... | collective-permute-start | bytes 442376 | tf_op jit(solution)/shard_map/ppermute | solution.py:684
  6.5 13.4 %collective-permute-start.2 = (bf16[4,9,16,128]{3,2,1,0:T(8,128)(2,1)S(1)}, bf16[4,9,16,128]{3,2,1,0:T(8,128)(2,1)S(1)}, u32[]{:S(2)}, u32[]{:S(2)}) collective-permute-start(bf16[4,9,16,128]{3,2,1,0:T(8,128)(2,1)S(1)} %get-tuple-element.21), channel_id=1, source_target_pairs={{2,1},{1,2},{4,3},{3,4},{6,5},{5,6},{8,7},{7,8},{10,9},{9,10},{12,... | collective-permute-start | bytes 442376 | tf_op jit(solution)/shard_map/ppermute | solution.py:683
  9.3 10.6 %collective-permute-start = (bf16[8,9,16,128]{3,2,1,0:T(8,128)(2,1)S(1)}, bf16[8,9,16,128]{3,2,1,0:T(8,128)(2,1)S(1)}, u32[]{:S(2)}, u32[]{:S(2)}) collective-permute-start(bf16[8,9,16,128]{3,2,1,0:T(8,128)(2,1)S(1)} %get-tuple-element.19.refs_1_), channel_id=1, source_target_pairs={{0,1},{1,0},{2,3},{3,2},{4,5},{5,4},{6,7},{7,6},{8,9},{9,8},{10,11... | collective-permute-start | bytes 884744 | tf_op jit(solution)/shard_map/ppermute | solution.py:682
  15.3 1.0 %copy-start.4 = (s32[256]{0:T(256)S(1)}, s32[256]{0:T(256)}, u32[]{:S(2)}) copy-start(s32[256]{0:T(256)} %cells_ref.1) | copy-start | bytes 3076
  16.3 3.5 %copy-start.3 = (f32[3,16]{1,0:T(4,128)S(1)}, f32[3,16]{1,0:T(4,128)}, u32[]{:S(2)}) copy-start(f32[3,16]{1,0:T(4,128)} %refs_5_.1) | copy-start | bytes 580
  19.9 33.6 %copy-start.5 = (f32[256]{0:T(256)S(1)}, f32[256]{0:T(256)}, u32[]{:S(2)}) copy-start(f32[256]{0:T(256)} %param.13) | copy-start | bytes 3076
  28.1 2.7 %collective-permute-start.3 = (f32[216,128]{1,0:T(8,128)S(1)}, f32[216,128]{1,0:T(8,128)S(1)}, u32[]{:S(2)}, u32[]{:S(2)}) collective-permute-start(f32[216,128]{1,0:T(8,128)S(1)} %get-tuple-element.25), channel_id=1, source_target_pairs={{0,2},{1,3},{2,0},{3,1},{4,6},{5,7},{6,4},{7,5},{8,10},{9,11},{10,... | collective-permute-start | bytes 331784 | tf_op jit(solution)/shard_map/ppermute | solution.py:480
  30.8 4.0 %collective-permute-start.4 = (f32[216,128]{1,0:T(8,128)S(1)}, f32[216,128]{1,0:T(8,128)S(1)}, u32[]{:S(2)}, u32[]{:S(2)}) collective-permute-start(f32[216,128]{1,0:T(8,128)S(1)} %add.15), channel_id=1, source_target_pairs={{0,1},{1,0},{2,6},{3,7},{4,5},{5,4},{6,2},{7,3},{8,9},{9,8},{10,14... | collective-permute-start | bytes 331784 | tf_op jit(solution)/shard_map/ppermute | solution.py:486
  34.7 3.7 %collective-permute-start.5 = (f32[216,128]{1,0:T(8,128)S(1)}, f32[216,128]{1,0:T(8,128)S(1)}, u32[]{:S(2)}, u32[]{:S(2)}) collective-permute-start(f32[216,128]{1,0:T(8,128)S(1)} %add.16), channel_id=1, source_target_pairs={{0,4},{1,5},{2,3},{3,2},{4,0},{5,1},{6,7},{7,6},{8,12},{9,13},{10,... | collective-permute-start | bytes 331784 | tf_op jit(solution)/shard_map/ppermute | solution.py:486
  38.4 5.7 %collective-permute-start.6 = (f32[216,128]{1,0:T(8,128)S(1)}, f32[216,128]{1,0:T(8,128)S(1)}, u32[]{:S(2)}, u32[]{:S(2)}) collective-permute-start(f32[216,128]{1,0:T(8,128)S(1)} %add.17), channel_id=1, source_target_pairs={{0,8},{1,9},{2,18},{3,19},{4,12},{5,13},{6,22},{7,23},{8,0},{9,1},... | collective-permute-start | bytes 331784 | tf_op jit(solution)/shard_map/ppermute | solution.py:486
  44.1 3.7 %collective-permute-start.7 = (f32[216,128]{1,0:T(8,128)S(1)}, f32[216,128]{1,0:T(8,128)S(1)}, u32[]{:S(2)}, u32[]{:S(2)}) collective-permute-start(f32[216,128]{1,0:T(8,128)S(1)} %add.18), channel_id=1, source_target_pairs={{0,16},{1,17},{2,10},{3,11},{4,20},{5,21},{6,14},{7,15},{8,24},{9,... | collective-permute-start | bytes 331784 | tf_op jit(solution)/shard_map/ppermute | solution.py:486
  47.8 5.7 %collective-permute-start.9 = (f32[216,128]{1,0:T(8,128)S(1)}, f32[216,128]{1,0:T(8,128)S(1)}, u32[]{:S(2)}, u32[]{:S(2)}) collective-permute-start(f32[216,128]{1,0:T(8,128)S(1)} %add.19.mine_ref), channel_id=1, source_target_pairs={{0,2},{1,3},{2,0},{3,1},{4,6},{5,7},{6,4},{7,5},{8,10},{9,11},{10,... | collective-permute-start | bytes 331784 | tf_op jit(solution)/shard_map/ppermute | solution.py:487
  52.5 34.1 %collective-permute-start.8 = (f32[4,8,16,128]{3,2,1,0:T(8,128)S(1)}, f32[4,8,16,128]{3,2,1,0:T(8,128)S(1)}, u32[]{:S(2)}, u32[]{:S(2)}) collective-permute-start(f32[4,8,16,128]{3,2,1,0:T(8,128)S(1)} %get-tuple-element.26), channel_id=1, source_target_pairs={{0,1},{1,0},{2,3},{3,2},{4,5},{5,4},{6,7},{7,6},{8,9},{9,8},{10,11... | collective-permute-start | bytes 786440 | tf_op jit(solution)/shard_map/ppermute | solution.py:702
  53.5 26.9 %copy-start = (bf16[4,16,128,256]{3,2,1,0:T(8,128)(2,1)S(1)}, bf16[4,16,128,256]{3,2,1,0:T(8,128)(2,1)}, u32[]{:S(2)}) copy-start(bf16[4,16,128,256]{3,2,1,0:T(8,128)(2,1)} %param.12) | copy-start | bytes 12582916

commit v2 on v1

--- a/solution.py
+++ b/solution.py
@@ -26,7 +26,7 @@
     return first, rows * sec_count * lax.axis_size("gx")
 
 
-def pack_kernel(state_ref, rock_ref, own, packed, outward, inward, rock_rows):
+def pack_kernel(state_ref, rock_ref, own, packed, rock_rows):
     across, entries, members, lanes = packed.shape
     along = entries - 1
     layers = lanes // 2
@@ -46,85 +46,114 @@
             own[x, y] = column
             packed[x, y] = column.astype(jnp.bfloat16)
         packed[x, along] = rock_rows[x * members : (x + 1) * members].astype(jnp.bfloat16)
-    if outward is not None:
-        half = across // 2
-        sec = lax.axis_index("sec")
-        outward[...] = packed[pl.ds((1 - sec) * half, half)]
-        inward[...] = packed[pl.ds(sec * half, half)]
-
-
-def pack(state_init, rock_type, halves):
+
+
+def pack(state_init, rock_type):
     members, across, along, lanes = state_init.shape
     shape = (along + 1, members, lanes)
     outs = [
         jax.ShapeDtypeStruct((across, along, members, lanes), jnp.float32),
         jax.ShapeDtypeStruct((across,) + shape, jnp.bfloat16),
     ]
-    if halves:
-        outs += [jax.ShapeDtypeStruct((across // 2,) + shape, jnp.bfloat16)] * 2
-
-    def kernel(state_ref, rock_ref, *refs):
+
+    def kernel(state_hbm, rock_hbm, *refs):
         own, packed = refs[:2]
-        outward, inward = refs[2:4] if halves else (None, None)
-        pack_kernel(state_ref, rock_ref, own, packed, outward, inward, refs[-1])
+        rock_rows, state_ref, rock_ref, state_sem, rock_sem = refs[-5:]
+        state_copy = pltpu.make_async_copy(state_hbm, state_ref, state_sem)
+        rock_copy = pltpu.make_async_copy(rock_hbm, rock_ref, rock_sem)
+        state_copy.start()
+        rock_copy.start()
+        rock_copy.wait()
+        state_copy.wait()
+        pack_kernel(state_ref, rock_ref, own, packed, rock_rows)
 
     return pl.pallas_call(
         kernel,
         out_shape=outs,
-        scratch_shapes=[pltpu.VMEM((across * members, lanes), jnp.float32)],
+        in_specs=[pl.BlockSpec(memory_space=pl.ANY)] * 2,
+        scratch_shapes=[
+            pltpu.VMEM((across * members, lanes), jnp.float32),
+            pltpu.VMEM((members * across * along, lanes), jnp.float32),
+            pltpu.VMEM(rock_type.shape, jnp.int32),
+            pltpu.SemaphoreType.DMA,
+            pltpu.SemaphoreType.DMA,
+        ],
         compiler_params=pltpu.CompilerParams(vmem_limit_bytes=VMEM_LIMIT),
     )(state_init.reshape(-1, lanes), rock_type)
 
 
-WELL_CHUNK = 8
-
-
-def inflow_kernel(cells_ref, rate_ref, out_ref):
-    wide, total_y, group, lanes = out_ref.shape
+def split_kernel(packed, outward, inward):
+    half = packed.shape[0] // 2
+    sec = lax.axis_index("sec")
+    outward[...] = packed[pl.ds((1 - sec) * half, half)]
+    inward[...] = packed[pl.ds(sec * half, half)]
+
+
+def split(packed):
+    half = jax.ShapeDtypeStruct((packed.shape[0] // 2,) + packed.shape[1:], packed.dtype)
+    return pl.pallas_call(
+        split_kernel, out_shape=(half, half), compiler_params=pltpu.CompilerParams(vmem_limit_bytes=VMEM_LIMIT)
+    )(packed)
+
+
+def inflow_rows(cell_row, rate_ref, out_ref, wide, total_y):
+    columns = wide * total_y
+    members, wells = rate_ref.shape
+    group = members // 2
+    lanes = out_ref.shape[1]
     layers = lanes // 2
-    wells = cells_ref.shape[0]
     first, _ = place(wide)
-    start = first * total_y * layers
-    size = wide * total_y * layers
-    out_ref[...] = jnp.zeros_like(out_ref)
-    lane = lax.broadcasted_iota(jnp.int32, (group, lanes), 1)
-
-    def one(w):
-        near = cells_ref[w] - start
-
-        @pl.when((near >= 0) & (near < size))
-        def _():
-            column = lax.div(near, layers)
-            z = near - column * layers
-            x = lax.div(column, total_y)
-            y = column - x * total_y
-            rate = rate_ref[w] * DT_PRESSURE
-            out_ref[x, y] = out_ref[x, y] + jnp.where((lane == z) | (lane == z + layers), rate, 0.0)
-
-    def some(c, carry):
-        for i in range(WELL_CHUNK):
-            one(c * WELL_CHUNK + i)
-        return carry
-
-    lax.fori_loop(0, wells // WELL_CHUNK, some, 0)
-    for w in range(wells // WELL_CHUNK * WELL_CHUNK, wells):
-        one(w)
-
-
-def well_inflow(well_cells, well_rate, wide, total_y, lanes):
+    start = first * total_y
+    row = lax.broadcasted_iota(jnp.int32, (columns, wells), 0)
+    near = lax.div(cell_row[...], layers) - start
+    picks = jnp.where(row == near, 1.0, 0.0).astype(jnp.bfloat16)
+    layer = lax.rem(jnp.broadcast_to(cell_row[...], (lanes, wells)).T, layers)
+    lane = lax.broadcasted_iota(jnp.int32, (wells, lanes), 1)
+    left_lanes = lane < layers
+    at = jnp.where(left_lanes, lane, lane - layers) == layer
+    short = jnp.zeros((lanes - members, wells), jnp.float32)
+    rate = (jnp.concatenate([rate_ref[...], short], 0) * DT_PRESSURE).T
+    for m in range(group):
+        value = jnp.where(left_lanes, rate[:, m : m + 1], rate[:, m + group : m + group + 1])
+        value = jnp.where(at, value, 0.0)
+        sums = [jnp.dot(picks, t, preferred_element_type=jnp.float32) for t in terms(value)]
+        out_ref[pl.ds(m, columns, stride=group), :] = (sums[2] + sums[1]) + sums[0]
+
+
+def prepare_kernel(wide, total_y, parts, cell_row, rate_ref, basis_hbm, inflow, inner_uu, basis, sems):
+    run = basis.shape[0] // parts
+    copies = [
+        pltpu.make_async_copy(basis_hbm.at[pl.ds(i * run, run)], basis.at[pl.ds(i * run, run)], sems.at[i])
+        for i in range(parts)
+    ]
+    for copy in copies:
+        copy.start()
+    inflow_rows(cell_row, rate_ref, inflow, wide, total_y)
+    total = jnp.zeros(inner_uu.shape, jnp.float32)
+    for i, copy in enumerate(copies):
+        copy.wait()
+        rows = basis[i * run : (i + 1) * run]
+        total += lax.dot_general(rows, rows, (((0,), (0,)), ((), ())), preferred_element_type=jnp.float32)
+    inner_uu[...] = total
+
+
+def prepare(well_cells, well_rate, flat, wide, total_y, lanes):
     members, wells = well_rate.shape
-    group = members // 2
-    layers = lanes // 2
-    rate = jnp.moveaxis(well_rate.reshape(2, group, wells), 2, 0)[..., None]
-    rate = jnp.broadcast_to(rate, (wells, 2, group, layers))
-    rate = jnp.concatenate([rate[:, 0], rate[:, 1]], -1)
-    return pl.pallas_call(
-        inflow_kernel,
-        out_shape=jax.ShapeDtypeStruct((wide, total_y, group, lanes), jnp.float32),
-        in_specs=[pl.BlockSpec(memory_space=pltpu.SMEM), pl.BlockSpec(memory_space=pltpu.VMEM)],
+    count = flat.shape[1]
+    parts = next(n for n in (4, 2, 1) if flat.shape[0] % (16 * n) == 0)
+    whole = pl.BlockSpec(memory_space=pltpu.VMEM)
+    inflow, inner_uu = pl.pallas_call(
+        functools.partial(prepare_kernel, wide, total_y, parts),
+        out_shape=(
+            jax.ShapeDtypeStruct((wide * total_y * members // 2, lanes), jnp.float32),
+            jax.ShapeDtypeStruct((count, count), jnp.float32),
+        ),
+        in_specs=[whole, whole, pl.BlockSpec(memory_space=pl.ANY)],
+        scratch_shapes=[pltpu.VMEM(flat.shape, jnp.bfloat16), pltpu.SemaphoreType.DMA((parts,))],
         compiler_params=pltpu.CompilerParams(vmem_limit_bytes=VMEM_LIMIT),
-        cost_estimate=pl.CostEstimate(flops=2 * 10**9, bytes_accessed=2**20, transcendentals=0),
-    )(well_cells, rate)
+        cost_estimate=pl.CostEstimate(flops=4 * 10**9, bytes_accessed=2**20, transcendentals=0),
+    )(well_cells.reshape(1, wells), well_rate, flat)
+    return inflow.reshape(wide, total_y, members // 2, lanes), inner_uu
 
 
 def roll(value, shift):
@@ -472,7 +501,8 @@
     return out.reshape(members, across, along, lanes)
 
 
-def all_sum(keep, give):
+def all_sum(keep, give, beside=None):
+    swapped = None
     counts = [lax.axis_size(axis) for axis in AXES]
     total = counts[0] * counts[1]
     pair = counts[1]
@@ -482,9 +512,12 @@
     turned = list(masks)
     for i in range(0, len(masks) - 1, 2):
         turned[i], turned[i + 1] = masks[i + 1], masks[i]
-    for even, odd in zip(masks, turned):
+    for hop, (even, odd) in enumerate(zip(masks, turned)):
         value = value + lax.ppermute(value, AXES, [(i, i ^ (odd if i & pair else even)) for i in range(total)])
-    return value, lax.ppermute(value, AXES, swap)
+        if hop == 1 and beside is not None:
+            beside, value = lax.optimization_barrier((beside, value))
+            swapped = lax.ppermute(beside, "sec", [(0, 1), (1, 0)])
+    return value, lax.ppermute(value, AXES, swap), swapped
 
 
 def to_bf16(value):
@@ -498,42 +531,75 @@
 PANEL = 32
 LANE = 128
 
+def row_of(value, j):
+    return jnp.broadcast_to(value[j:j + 1], (SUB, LANE))
+
 def eliminate(panel, column):
     groups = PANEL // SUB
     tiles = panel.shape[1] // LANE
-    below = lax.broadcasted_iota(jnp.int32, (SUB, LANE), 0)
+    row = lax.broadcasted_iota(jnp.int32, (SUB, LANE), 0)
     strip = [[panel[h * SUB:(h + 1) * SUB, t * LANE:(t + 1) * LANE] for t in range(tiles)] for h in range(groups)]
+    spread = {}
+
+    def expand(g, first_group):
+        for h in range(first_group, groups):
+            for j in range(g * SUB, (g + 1) * SUB):
+                tile, lane = (column + j) // LANE, (column + j) % LANE
+                spread[h, j] = jnp.broadcast_to(strip[h][tile][:, lane:lane + 1], (SUB, LANE))
+
+    expand(0, 0)
     for g in range(groups):
-        spread = {}
-        for h in range(g, groups):
-            for j in range(SUB):
-                at = column + g * SUB + j
-                tile, lane = at // LANE, at % LANE
-                spread[h, j] = jnp.broadcast_to(strip[h][tile][:, lane:lane + 1], (SUB, LANE))
+        if g + 1 < groups:
+            expand(g + 1, g)
         scale = jnp.zeros((SUB, LANE), jnp.float32)
-        for j in range(SUB):
-            pivot = jnp.broadcast_to(spread[g, j][j:j + 1], (SUB, LANE))
-            inverse = 1.0 / pivot
-            scale = jnp.where(below == j, pivot, scale)
-            factors = {}
+        for j in range(0, SUB, 2):
+            left, right = spread[g, g * SUB + j], spread[g, g * SUB + j + 1]
+            a, b, c = row_of(left, j), row_of(right, j), row_of(right, j + 1)
+            det = a * c - b * b
+            inv_a, inv_det = 1.0 / a, 1.0 / det
+            slope = b * inv_a
+            second = a * inv_det
+            scale = jnp.where(row == j, a, jnp.where(row == j + 1, det * inv_a, scale))
+            one, two = {}, {}
             for h in range(g, groups):
-                factors[h] = spread[h, j] * inverse
-            factors[g] = jnp.where(below > j, factors[g], 0.0)
-            for k in range(j + 1, SUB):
-                row = jnp.broadcast_to(spread[g, k][j:j + 1], (SUB, LANE))
+                one[h] = spread[h, g * SUB + j] * inv_a
+                two[h] = (spread[h, g * SUB + j + 1] - one[h] * b) * second
+            one[g] = jnp.where(row > j, one[g], 0.0)
+            two[g] = jnp.where(row > j + 1, two[g], 0.0)
+            for k in range(g * SUB + j + 2, min(g + 2, groups) * SUB):
+                first = row_of(spread[g, k], j)
+                next_ = row_of(spread[g, k], j + 1) - slope * first
                 for h in range(g, groups):
-                    spread[h, k] = spread[h, k] - factors[h] * row
+                    spread[h, k] = spread[h, k] - one[h] * first - two[h] * next_
             for t in range(tiles):
-                row = jnp.broadcast_to(strip[g][t][j:j + 1], (SUB, LANE))
+                first = row_of(strip[g][t], j)
+                next_ = row_of(strip[g][t], j + 1) - slope * first
                 for h in range(g, groups):
-                    strip[h][t] = strip[h][t] - factors[h] * row
+                    strip[h][t] = strip[h][t] - one[h] * first - two[h] * next_
         root = lax.rsqrt(scale)
         for t in range(tiles):
             strip[g][t] = strip[g][t] * root
     return jnp.concatenate([jnp.concatenate(s, 1) for s in strip], 0)
 
+def terms(value):
+    high = value.astype(jnp.bfloat16)
+    rest = value - high.astype(jnp.float32)
+    middle = rest.astype(jnp.bfloat16)
+    return high, middle, (rest - middle.astype(jnp.float32)).astype(jnp.bfloat16)
+
+def left_stack(t):
+    return jnp.concatenate([t[0], t[0], t[1], t[1], t[0], t[2]], 0)
+
+def right_stack(t):
+    return jnp.concatenate([t[0], t[1], t[0], t[1], t[2], t[0]], 0)
+
+def stacked_dot(left, right):
+    return lax.dot_general(left, right, (((0,), (0,)), ((), ())), preferred_element_type=jnp.float32)
+
+def tdot(a, b):
+    return stacked_dot(left_stack(terms(a)), right_stack(terms(b)))
+
 def solve(aug, count):
-    width = aug.shape[1]
     for start in range(0, count, PANEL):
         first = start // LANE * LANE
         done = eliminate(aug[start:start + PANEL, first:], start - first)
@@ -541,11 +607,21 @@
         rest = start + PANEL
         if rest < count:
             base = rest // LANE * LANE
-            left = done[:, base - first:count - first]
-            change = hdot(left, done[:, base - first:], 0, 0)
+            parts = terms(done[:, base - first:])
+            left, right = left_stack(parts), right_stack(parts)
+            change = stacked_dot(left[:, :count - base], right)
             aug[rest:, base:] = aug[rest:, base:] - change[rest - base:]
 
-def small_kernel(scale, mine_ref, other_ref, sigma_ref, high_ref, low_ref, snap_ref, sigma_out, aug, sums, gram_ref):
+def small_kernel(
+    scale, mine_ref, other_ref, sigma_ref, snaps_hbm, basis_hbm, fresh_hbm, sigma_out,
+    aug, sums, gram_ref, weights, snaps_ref, basis, fresh, in_sems, out_sems,
+):
+    copies = [
+        pltpu.make_async_copy(basis_hbm, basis, in_sems.at[0]),
+        pltpu.make_async_copy(snaps_hbm, snaps_ref, in_sems.at[1]),
+    ]
+    for copy in copies:
+        copy.start()
     count = sigma_ref.shape[1]
     snaps = (gram_ref.shape[0] - count) // 2
     half = sums.shape[0] // 2
@@ -575,8 +651,8 @@
             known = gram_ref[:reach, :reach]
         spread = hdot(mapped, known)
         gram = own - hdot(rounded, coeffs, 1, 1) - hdot(coeffs, rounded, 1, 1) + hdot(spread, mapped, 1, 1)
-        lead = hdot(coeffs, coeffs, 0, 0) + jnp.where(eye, jnp.broadcast_to(sig2, eye.shape), 0.0)
-        inner = hdot(lead, lead) + hdot(coeffs, hdot(gram, coeffs), 0, 0)
+        lead = tdot(coeffs, coeffs) + jnp.where(eye, jnp.broadcast_to(sig2, eye.shape), 0.0)
+        inner = hdot(lead, lead) + tdot(coeffs, hdot(gram, coeffs))
         aug[:, :count] = inner
         aug[:, count:2 * count] = lead
         aug[:, 2 * count:] = jnp.concatenate([coeffs, jnp.zeros((pad, count), jnp.float32)], 0).T
@@ -593,70 +669,82 @@
         else:
             final = hdot(step, prior)
             high = final[:, :count].astype(jnp.bfloat16)
-            high_ref[...] = high
-            low_ref[...] = (final[:, :count] - high.astype(jnp.float32)).astype(jnp.bfloat16)
+            low = (final[:, :count] - high.astype(jnp.float32)).astype(jnp.bfloat16)
+            weights[:count] = high.T
+            weights[count:2 * count] = low.T
             both = jnp.concatenate([final[:, count:].T[:snaps], aug[:, 2 * count:].T[:snaps]], 0)
             high = both.astype(jnp.bfloat16)
-            snap_ref[:2 * snaps] = high
-            snap_ref[2 * snaps:] = (both - high.astype(jnp.float32)).astype(jnp.bfloat16)
+            weights[2 * count:2 * count + 2 * snaps] = high
+            weights[2 * count + 2 * snaps:] = (both - high.astype(jnp.float32)).astype(jnp.bfloat16)
     sigma_out[...] = jnp.sqrt(sig2)
-
-def small(mine, other, sigma, snap_count, rows_total):
+    for copy in copies:
+        copy.wait()
+    renew(weights, snaps_ref, basis, fresh, fresh_hbm, out_sems)
+
+
+def renew(weights, snaps_ref, basis, fresh, fresh_hbm, out_sems):
+    parts = out_sems.shape[0]
+    cells, _, lanes = snaps_ref.shape
+    run = cells // parts
+
+    def out(i):
+        rows = pl.ds(pl.multiple_of(i * run * lanes, run * lanes), run * lanes)
+        return pltpu.make_async_copy(fresh.at[rows], fresh_hbm.at[rows], out_sems.at[i])
+
+    def part(i, none):
+        at = pl.multiple_of(i * run * lanes, run * lanes)
+        flat = basis[pl.ds(at, run * lanes), :]
+        turned = []
+        for q in range(run):
+            one = snaps_ref[i * run + q]
+            turned.append(jnp.concatenate([one, one], 0).T)
+        value = jnp.dot(
+            jnp.concatenate([flat, flat, jnp.concatenate(turned, 0)], 1), weights[...],
+            preferred_element_type=jnp.float32,
+        )
+        fresh[pl.ds(at, run * lanes), :] = value.astype(jnp.bfloat16)
+        out(i).start()
+        return none
+
+    lax.fori_loop(0, parts, part, 0)
+
+    def finish(i, none):
+        out(i).wait()
+        return none
+
+    lax.fori_loop(0, parts, finish, 0)
+
+
+def small(mine, other, sigma, snaps, flat, rows_total):
     count = sigma.shape[0]
+    cells, snap_count, lanes = snaps.shape
     rows = count + snap_count
-    high, low, snap_weights, sigma_out = pl.pallas_call(
+    parts = next(n for n in (8, 4, 2, 1) if cells % n == 0)
+    whole = pl.BlockSpec(memory_space=pltpu.VMEM)
+    outside = pl.BlockSpec(memory_space=pl.ANY)
+    fresh, sigma_out = pl.pallas_call(
         functools.partial(small_kernel, 1.0 / rows_total),
         out_shape=(
-            jax.ShapeDtypeStruct((count, count), jnp.bfloat16),
-            jax.ShapeDtypeStruct((count, count), jnp.bfloat16),
-            jax.ShapeDtypeStruct((2 * snap_count, count), jnp.bfloat16),
+            jax.ShapeDtypeStruct(flat.shape, jnp.bfloat16),
             jax.ShapeDtypeStruct((1, count), jnp.float32),
         ),
+        in_specs=[whole, whole, whole, outside, outside],
+        out_specs=(outside, whole),
         scratch_shapes=[
             pltpu.VMEM((count, 2 * count + LANE), jnp.float32),
             pltpu.VMEM((2 * mine.shape[0], LANE), jnp.float32),
             pltpu.VMEM((rows, count + LANE), jnp.float32),
+            pltpu.VMEM((2 * count + 2 * snap_count, count), jnp.bfloat16),
+            pltpu.VMEM(snaps.shape, jnp.bfloat16),
+            pltpu.VMEM(flat.shape, jnp.bfloat16),
+            pltpu.VMEM(flat.shape, jnp.bfloat16),
+            pltpu.SemaphoreType.DMA((2,)),
+            pltpu.SemaphoreType.DMA((parts,)),
         ],
         compiler_params=pltpu.CompilerParams(vmem_limit_bytes=VMEM_LIMIT),
         cost_estimate=pl.CostEstimate(flops=2 * 10**10, bytes_accessed=2**20, transcendentals=0),
-    )(mine, other, sigma.reshape(1, count))
-    return high, low, snap_weights, sigma_out.reshape(count)
-
-
-def renew_kernel(basis_ref, snaps_ref, high_ref, low_ref, snap_ref, out_ref):
-    lanes = snaps_ref.shape[2]
-    flat = basis_ref[...]
-    turned = (((1,), (1,)), ((), ()))
-    value = lax.dot_general(flat, high_ref[...], turned, preferred_element_type=jnp.float32)
-    value += lax.dot_general(flat, low_ref[...], turned, preferred_element_type=jnp.float32)
-    for q in range(snaps_ref.shape[0]):
-        part = snaps_ref[q]
-        part = lax.dot_general(
-            jnp.concatenate([part, part], 0), snap_ref[...], (((0,), (0,)), ((), ())),
-            preferred_element_type=jnp.float32,
-        )
-        out_ref[q * lanes : (q + 1) * lanes] = (value[q * lanes : (q + 1) * lanes] + part).astype(jnp.bfloat16)
-
-
-def renew(flat, snaps, high, low, snap_weights):
-    cells, snap_count, lanes = snaps.shape
-    count = flat.shape[1]
-    run = next(n for n in (8, 4, 2, 1) if cells % n == 0)
-    same = lambda i: (0, 0)
-    return pl.pallas_call(
-        renew_kernel,
-        out_shape=jax.ShapeDtypeStruct(flat.shape, jnp.bfloat16),
-        grid=(cells // run,),
-        in_specs=[
-            pl.BlockSpec((run * lanes, count), lambda i: (i, 0)),
-            pl.BlockSpec((run, snap_count, lanes), lambda i: (i, 0, 0)),
-            pl.BlockSpec((count, count), same),
-            pl.BlockSpec((count, count), same),
-            pl.BlockSpec((2 * snap_count, count), same),
-        ],
-        out_specs=pl.BlockSpec((run * lanes, count), lambda i: (i, 0)),
-        compiler_params=pltpu.CompilerParams(vmem_limit_bytes=VMEM_LIMIT),
-    )(flat, snaps, high, low, snap_weights)
+    )(mine, other, sigma.reshape(1, count), snaps, flat)
+    return fresh, sigma_out.reshape(count)
 
 
 def body(state_init, rock_type, perm_table, well_cells, well_rate, basis_in, singular):
@@ -668,9 +756,9 @@
     total_y = along * sec_count
     count = basis_in.shape[-1]
     fast = sec_count == 2 and across == 2 * STEPS
-    inflow = well_inflow(well_cells, well_rate, wide, total_y, lanes)
     if fast:
-        own, packed, outward, inward = pack(state_init, rock_type, True)
+        own, packed = pack(state_init, rock_type)
+        outward, inward = split(packed)
         straight, crossed = [], []
         for r in range(gx_count):
             if r > 0:
@@ -684,7 +772,7 @@
         beside = lax.ppermute(outward, AXES, straight)
         fields = (own, packed, other, beside, cross)
     else:
-        _, packed = pack(state_init, rock_type, False)
+        _, packed = pack(state_init, rock_type)
         slab = lax.all_gather(packed, "sec", axis=1)
         low = lax.ppermute(slab[across - STEPS :], "gx", [(i, i + 1) for i in range(gx_count - 1)])
         high = lax.ppermute(slab[:STEPS], "gx", [(i + 1, i) for i in range(gx_count - 1)])
@@ -692,21 +780,18 @@
         fields = (lax.dynamic_slice_in_dim(padded, lax.axis_index("sec") * rows, wide, axis=0),)
     flat = basis_in.reshape(-1, count)
     rows_total = flat.shape[0] * gx_count * sec_count
-    inner_uu = lax.dot_general(flat, flat, (((0,), (0,)), ((), ())), preferred_element_type=jnp.float32)
+    inflow, inner_uu = prepare(well_cells, well_rate, flat, wide, total_y, lanes)
     snaps, keep, give, fin, send = flux(
         fields, perm_table, inflow, inner_uu, flat.reshape(-1, lanes, count), along
     )
-    mine, others = all_sum(keep, give)
-    if fast:
-        send, mine = lax.optimization_barrier((send, mine))
-        received = lax.ppermute(send, "sec", [(0, 1), (1, 0)])
-    high, low, snap_weights, sigma = small(mine, others, singular, snaps.shape[1], rows_total)
+    mine, others, received = all_sum(keep, give, send if fast else None)
     if fast:
         state_out = unpack((fin, received))
+        state_out, mine = lax.optimization_barrier((state_out, mine))
     else:
         moved = lax.all_to_all(fin, "sec", split_axis=1, concat_axis=0, tiled=True)
         state_out = unpack((moved.reshape(across, along, members, lanes),))
-    fresh = renew(flat, snaps, high, low, snap_weights)
+    fresh, sigma = small(mine, others, singular, snaps, flat, rows_total)
     return state_out, fresh.reshape(basis_in.shape), sigma
 
 

time: 88 us -> 77.3 us (0.88)
  Pallas kernels: 46.3 us -> 39.8 us
  matrix products: 4.74 us -> 0 us
  waiting for transfers between devices: 18 us -> 14.4 us
  local copies, waits for them, and re-layouts: 3.3 us -> 5.35 us
  starting transfers between devices: 14.1 us -> 15.8 us
    pallas_call x3, Pallas kernels: 10.2 us -> 4.61 us  [the longest x1 4.12 us: prepare(): pl.pallas_call(functools.partial(prepare_kernel, wide, total_y, parts), o...]
    dot_general x1 -> x0, matrix products: 4.74 us -> none  [body(): lax.dot_general(flat, flat, (((0,), (0,)), ((), ())), preferred_element_t...]
    unnamed x12 -> x16, local copies, waits for them, and re-layouts: 1.77 us -> 5.35 us
    ppermute x4, waiting for transfers between devices: 16.4 us -> 13.3 us  [all_sum(): lax.ppermute(value, AXES, [(i, i ^ (odd if i & pair else even)) for i in...]
    ppermute x4, starting transfers between devices: 0.56 us -> 2.15 us  [all_sum(): lax.ppermute(value, AXES, [(i, i ^ (odd if i & pair else even)) for i in...]
    ppermute x1, starting transfers between devices: 1.72 us -> 0.39 us  [all_sum(): value = keep + lax.ppermute(give, AXES, swap)]
    ppermute x2, starting transfers between devices: 4.99 us -> 6.11 us  [the longest x1 4.63 us: all_sum(): return (value, lax.ppermute(value, AXES, swap), swapped)]
    ppermute x1, starting transfers between devices: 0.42 us -> 1.3 us  [body(): other = lax.ppermute(packed, 'sec', [(0, 1), (1, 0)])]
  transfers between devices with their start and end apart: 10 -> 10, of which waited for: 6 -> 5; matrix products, arithmetic and copies ran while one was open for 8% -> 0% of each run, Pallas kernels for 42% -> 7%
where the time goes in v2:
time: 77.3 us; the launch traced here: 76.4 us
  Pallas kernels  39.8 us (51%)
  starting transfers between devices  15.8 us (20%)
  waiting for transfers between devices  14.4 us (19%)
  local copies, waits for them, and re-layouts  5.35 us (7%)
  between operations  0.96 us (1%)
    pallas_call x1, Pallas kernels, small(): pl.pallas_call(functools.partial(small_kernel, 1.0 / rows_total), out_sha...  26.1 us
    ppermute x4, waiting for transfers between devices, all_sum(): lax.ppermute(value, AXES, [(i, i ^ (odd if i & pair else even)) for i in...  13.3 us
    pallas_call x1, Pallas kernels, flux(): pl.pallas_call(lambda *refs: flux_kernel(fast, *refs), out_shape=outs, in...  8.05 us
    unnamed x16, local copies, waits for them, and re-layouts  5.35 us
    ppermute x1, starting transfers between devices, all_sum(): return (value, lax.ppermute(value, AXES, swap), swapped)  4.63 us
    pallas_call x1, Pallas kernels, prepare(): pl.pallas_call(functools.partial(prepare_kernel, wide, total_y, parts), o...  4.12 us
    ppermute x1, starting transfers between devices, body(): beside = lax.ppermute(outward, AXES, straight)  3.96 us
    ppermute x4, starting transfers between devices, all_sum(): lax.ppermute(value, AXES, [(i, i ^ (odd if i & pair else even)) for i in...  2.15 us
  transfers between devices with their start and end apart: 10, of which 5 were waited for; matrix products, arithmetic and copies ran while one was open for 0% of the time, Pallas kernels for 7%

profile of v2, /device:TPU:25, one launch (start us, length us, event | category | flops | bytes accessed | tf_op | source)
XLA Modules:
  0.0 76.4 jit_solution(1766251903556620729)
XLA Ops:
  0.6 0.0 copy-start.2
  0.6 1.0 %copy-done.2 = f32[16,8,8,128]{3,2,1,0:T(8,128)S(1)} copy-done((f32[16,8,8,128]{3,2,1,0:T(8,128)S(1)}, f32[16,8,8,128]{3,2,1,0:T(8,128)}, u32[]{:S(2)}) %copy-start.2) | copy-done | bytes 524312
  1.7 0.0 copy-start.3
  1.7 0.7 copy-done.3
  2.4 0.5 shard_map.94
  2.9 1.3 %collective-permute-start = (bf16[8,9,16,128]{3,2,1,0:T(8,128)(2,1)S(1)}, bf16[8,9,16,128]{3,2,1,0:T(8,128)(2,1)S(1)}, u32[]{:S(2)}, u32[]{:S(2)}) collective-permute-start(bf16[8,9,16,128]{3,2,1,0:T(8,128)(2,1)S(1)} %get-tuple-element.21.packed.refs_1_), channel_id=1, source_target_pairs={{0,1},{1,0},{2,3},{3,2},{4,5},{5,4},{6,7},{7,6},{8,9},{9,8},{10,11... | collective-permute-start | bytes 884744 | tf_op jit(solution)/shard_map/ppermute | solution.py:770
  4.2 4.0 %collective-permute-start.1 = (bf16[4,9,16,128]{3,2,1,0:T(8,128)(2,1)S(1)}, bf16[4,9,16,128]{3,2,1,0:T(8,128)(2,1)S(1)}, u32[]{:S(2)}, u32[]{:S(2)}) collective-permute-start(bf16[4,9,16,128]{3,2,1,0:T(8,128)(2,1)S(1)} %get-tuple-element.22), channel_id=1, source_target_pairs={{3,1},{0,2},{5,3},{2,4},{7,5},{4,6},{9,7},{6,8},{11,9},{8,10},{13,... | collective-permute-start | bytes 442376 | tf_op jit(solution)/shard_map/ppermute | solution.py:772
  8.2 1.9 %collective-permute-start.2 = (bf16[4,9,16,128]{3,2,1,0:T(8,128)(2,1)S(1)}, bf16[4,9,16,128]{3,2,1,0:T(8,128)(2,1)S(1)}, u32[]{:S(2)}, u32[]{:S(2)}) collective-permute-start(bf16[4,9,16,128]{3,2,1,0:T(8,128)(2,1)S(1)} %get-tuple-element.23), channel_id=1, source_target_pairs={{2,1},{1,2},{4,3},{3,4},{6,5},{5,6},{8,7},{7,8},{10,9},{9,10},{12,... | collective-permute-start | bytes 442376 | tf_op jit(solution)/shard_map/ppermute | solution.py:771
  10.1 0.0 copy-start
  10.1 2.2 %copy-done = bf16[4,16,128,256]{3,2,1,0:T(8,128)(2,1)S(1)} copy-done((bf16[4,16,128,256]{3,2,1,0:T(8,128)(2,1)S(1)}, bf16[4,16,128,256]{3,2,1,0:T(8,128)(2,1)}, u32[]{:S(2)}) %copy-start) | copy-done | bytes 4194328
  12.3 0.0 copy-start.5
  12.3 0.7 copy-done.5
  13.0 0.0 copy-start.6
  13.0 0.7 copy-done.6
  13.7 0.0 copy-start.4
  13.7 4.1 %shard_map.96 = (f32[1536,128]{1,0:T(8,128)S(1)}, f32[256,256]{1,0:T(8,128)S(1)}) custom-call(s32[1,256]{1,0:T(1,128)S(1)} %bitcast.14, f32[16,256]{1,0:T(8,128)S(1)} %copy-done.5, bf16[8192,256]{1,0:T(8,128)(2,1)S(1)} %bitcast.10), custom_call_target="tpu_custom_call" | custom-call | flops 4000000000 | bytes 1048576 | tf_op jit(solution)/shard_map/pallas_call | solution.py:145
  17.8 0.0 collective-permute-done.1.refs_3_
  17.8 0.0 collective-permute-done.2.refs_4_
  17.8 0.0 collective-permute-done.refs_2_
  17.8 0.0 copy-done.4
  17.8 0.0 copy-start.1
  17.9 0.0 copy-start.7
  17.9 8.1 %shard_map.97 = (bf16[64,64,128]{2,1,0:T(8,128)(2,1)S(1)}, f32[216,128]{1,0:T(8,128)S(1)}, f32[216,128]{1,0:T(8,128)S(1)}, f32[4,8,16,128]{3,2,1,0:T(8,128)S(1)}, f32[4,8,16,128]{3,2,1,0:T(8,128)S(1)}) custom-call(f32[8,8,16,128]{3,2,1,0:T(8,128)S(1)} %get-tuple-element.20.refs_0_, bf16[8,9,16,128]{3,2,1,0:T(8,128)(2,1)S(1)} %get-tuple-element.21.packed.refs_1_, ...), custom_call_target="tpu_custom_call" | custom-call | tf_op jit(solution)/shard_map/pallas_call | solution.py:458
  25.9 0.4 collective-permute-start.3
  26.3 1.0 %collective-permute-done.3 = f32[216,128]{1,0:T(8,128)S(1)} collective-permute-done((f32[216,128]{1,0:T(8,128)S(1)}, f32[216,128]{1,0:T(8,128)S(1)}, u32[]{:S(2)}, u32[]{:S(2)}) %collective-permute-start.3) | collective-permute-done | bytes 110624 | tf_op jit(solution)/shard_map/ppermute | solution.py:510
  27.3 0.4 collective-permute-start.4
  27.7 3.6 %collective-permute-done.4 = f32[216,128]{1,0:T(8,128)S(1)} collective-permute-done((f32[216,128]{1,0:T(8,128)S(1)}, f32[216,128]{1,0:T(8,128)S(1)}, u32[]{:S(2)}, u32[]{:S(2)}) %collective-permute-start.4) | collective-permute-done | bytes 110624 | tf_op jit(solution)/shard_map/ppermute | solution.py:516
  31.3 1.6 %collective-permute-start.5 = (f32[216,128]{1,0:T(8,128)S(1)}, f32[216,128]{1,0:T(8,128)S(1)}, u32[]{:S(2)}, u32[]{:S(2)}) collective-permute-start(f32[216,128]{1,0:T(8,128)S(1)} %add.16), channel_id=1, source_target_pairs={{0,4},{1,5},{2,3},{3,2},{4,0},{5,1},{6,7},{7,6},{8,12},{9,13},{10,... | collective-permute-start | bytes 331784 | tf_op jit(solution)/shard_map/ppermute | solution.py:516
  32.9 2.1 %collective-permute-done.5 = f32[216,128]{1,0:T(8,128)S(1)} collective-permute-done((f32[216,128]{1,0:T(8,128)S(1)}, f32[216,128]{1,0:T(8,128)S(1)}, u32[]{:S(2)}, u32[]{:S(2)}) %collective-permute-start.5) | collective-permute-done | bytes 110624 | tf_op jit(solution)/shard_map/ppermute | solution.py:516
  35.0 0.1 collective-permute-start.7
  35.1 1.5 %collective-permute-start.6 = (f32[4,8,16,128]{3,2,1,0:T(8,128)S(1)}, f32[4,8,16,128]{3,2,1,0:T(8,128)S(1)}, u32[]{:S(2)}, u32[]{:S(2)}) collective-permute-start(f32[4,8,16,128]{3,2,1,0:T(8,128)S(1)} %get-tuple-element.30), channel_id=1, source_target_pairs={{0,1},{1,0},{2,3},{3,2},{4,5},{5,4},{6,7},{7,6},{8,9},{9,8},{10,11... | collective-permute-start | bytes 786440 | tf_op jit(solution)/shard_map/ppermute | solution.py:519
  36.6 4.1 %collective-permute-done.7 = f32[216,128]{1,0:T(8,128)S(1)} collective-permute-done((f32[216,128]{1,0:T(8,128)S(1)}, f32[216,128]{1,0:T(8,128)S(1)}, u32[]{:S(2)}, u32[]{:S(2)}) %collective-permute-start.7) | collective-permute-done | bytes 110624 | tf_op jit(solution)/shard_map/ppermute | solution.py:516
  40.7 0.1 collective-permute-start.8
  40.8 3.6 %collective-permute-done.8 = f32[216,128]{1,0:T(8,128)S(1)} collective-permute-done((f32[216,128]{1,0:T(8,128)S(1)}, f32[216,128]{1,0:T(8,128)S(1)}, u32[]{:S(2)}, u32[]{:S(2)}) %collective-permute-start.8) | collective-permute-done | bytes 110624 | tf_op jit(solution)/shard_map/ppermute | solution.py:516
  44.4 4.6 %collective-permute-start.9 = (f32[216,128]{1,0:T(8,128)S(1)}, f32[216,128]{1,0:T(8,128)S(1)}, u32[]{:S(2)}, u32[]{:S(2)}) collective-permute-start(f32[216,128]{1,0:T(8,128)S(1)} %add.19.mine_ref), channel_id=1, source_target_pairs={{0,2},{1,3},{2,0},{3,1},{4,6},{5,7},{6,4},{7,5},{8,10},{9,11},{10,... | collective-permute-start | bytes 331784 | tf_op jit(solution)/shard_map/ppermute | solution.py:520
  49.0 0.0 collective-permute-done.6.refs_1_
  49.0 1.1 %shard_map.98 = f32[1024,128]{1,0:T(8,128)} custom-call(f32[4,8,16,128]{3,2,1,0:T(8,128)S(1)} %get-tuple-element.26.refs_0_, f32[4,8,16,128]{3,2,1,0:T(8,128)S(1)} %collective-permute-done.6.refs_1_), custom_call_target="tpu_custom_call" | custom-call | tf_op jit(solution)/shard_map/pallas_call | solution.py:496
  50.1 0.0 collective-permute-done.9.other_ref
  50.1 0.0 copy-done.1
  50.1 0.0 copy-done.7
  50.1 26.1 %shard_map.99 = (bf16[8192,256]{1,0:T(8,128)(2,1)}, f32[1,256]{1,0:T(1,128)}) custom-call(f32[216,128]{1,0:T(8,128)S(1)} %add.19.mine_ref, f32[216,128]{1,0:T(8,128)S(1)} %collective-permute-done.9.other_ref, f32[1,256]{1,0:T(1,128)S(1)} %bitcast.15, bf16[64,64,128]{2,1,0:T(8,128)(2,1)S(1)} %get-tuple-element.34.snaps_hbm, bf16[8192,256]{1,0:T(8,128)(2,1)S(1)} %bitcast.11), custom_call_target="tpu_custom_call" | custom-call | flops 20000000000 | bytes 1048576 | tf_op jit(solution)/shard_map/pallas_call | solution.py:725
  (6 shorter events, 0.1 us)
Async XLA Ops:
  0.6 1.0 %copy-start.2 = (f32[16,8,8,128]{3,2,1,0:T(8,128)S(1)}, f32[16,8,8,128]{3,2,1,0:T(8,128)}, u32[]{:S(2)}) copy-start(f32[16,8,8,128]{3,2,1,0:T(8,128)} %param.7) | copy-start | bytes 1572868
  1.7 0.7 copy-start.3
  2.9 15.0 %collective-permute-start = (bf16[8,9,16,128]{3,2,1,0:T(8,128)(2,1)S(1)}, bf16[8,9,16,128]{3,2,1,0:T(8,128)(2,1)S(1)}, u32[]{:S(2)}, u32[]{:S(2)}) collective-permute-start(bf16[8,9,16,128]{3,2,1,0:T(8,128)(2,1)S(1)} %get-tuple-element.21.packed.refs_1_), channel_id=1, source_target_pairs={{0,1},{1,0},{2,3},{3,2},{4,5},{5,4},{6,7},{7,6},{8,9},{9,8},{10,11... | collective-permute-start | bytes 884744 | tf_op jit(solution)/shard_map/ppermute | solution.py:770
  4.2 13.6 %collective-permute-start.1 = (bf16[4,9,16,128]{3,2,1,0:T(8,128)(2,1)S(1)}, bf16[4,9,16,128]{3,2,1,0:T(8,128)(2,1)S(1)}, u32[]{:S(2)}, u32[]{:S(2)}) collective-permute-start(bf16[4,9,16,128]{3,2,1,0:T(8,128)(2,1)S(1)} %get-tuple-element.22), channel_id=1, source_target_pairs={{3,1},{0,2},{5,3},{2,4},{7,5},{4,6},{9,7},{6,8},{11,9},{8,10},{13,... | collective-permute-start | bytes 442376 | tf_op jit(solution)/shard_map/ppermute | solution.py:772
  8.2 9.7 %collective-permute-start.2 = (bf16[4,9,16,128]{3,2,1,0:T(8,128)(2,1)S(1)}, bf16[4,9,16,128]{3,2,1,0:T(8,128)(2,1)S(1)}, u32[]{:S(2)}, u32[]{:S(2)}) collective-permute-start(bf16[4,9,16,128]{3,2,1,0:T(8,128)(2,1)S(1)} %get-tuple-element.23), channel_id=1, source_target_pairs={{2,1},{1,2},{4,3},{3,4},{6,5},{5,6},{8,7},{7,8},{10,9},{9,10},{12,... | collective-permute-start | bytes 442376 | tf_op jit(solution)/shard_map/ppermute | solution.py:771
  10.1 2.2 %copy-start = (bf16[4,16,128,256]{3,2,1,0:T(8,128)(2,1)S(1)}, bf16[4,16,128,256]{3,2,1,0:T(8,128)(2,1)}, u32[]{:S(2)}) copy-start(bf16[4,16,128,256]{3,2,1,0:T(8,128)(2,1)} %param.12) | copy-start | bytes 12582916
  12.3 0.7 copy-start.5
  13.0 0.7 copy-start.6
  13.7 4.2 %copy-start.4 = (f32[3,16]{1,0:T(4,128)S(1)}, f32[3,16]{1,0:T(4,128)}, u32[]{:S(2)}) copy-start(f32[3,16]{1,0:T(4,128)} %refs_5_.1) | copy-start | bytes 580
  17.8 32.3 %copy-start.1 = (bf16[4,16,128,256]{3,2,1,0:T(8,128)(2,1)S(1)}, bf16[4,16,128,256]{3,2,1,0:T(8,128)(2,1)}, u32[]{:S(2)}) copy-start(bf16[4,16,128,256]{3,2,1,0:T(8,128)(2,1)} %param.12) | copy-start | bytes 12582916
  17.9 32.3 %copy-start.7 = (f32[256]{0:T(256)S(1)}, f32[256]{0:T(256)}, u32[]{:S(2)}) copy-start(f32[256]{0:T(256)} %param.13) | copy-start | bytes 3076
  25.9 1.4 %collective-permute-start.3 = (f32[216,128]{1,0:T(8,128)S(1)}, f32[216,128]{1,0:T(8,128)S(1)}, u32[]{:S(2)}, u32[]{:S(2)}) collective-permute-start(f32[216,128]{1,0:T(8,128)S(1)} %get-tuple-element.29), channel_id=1, source_target_pairs={{0,2},{1,3},{2,0},{3,1},{4,6},{5,7},{6,4},{7,5},{8,10},{9,11},{10,... | collective-permute-start | bytes 331784 | tf_op jit(solution)/shard_map/ppermute | solution.py:510
  27.3 4.0 %collective-permute-start.4 = (f32[216,128]{1,0:T(8,128)S(1)}, f32[216,128]{1,0:T(8,128)S(1)}, u32[]{:S(2)}, u32[]{:S(2)}) collective-permute-start(f32[216,128]{1,0:T(8,128)S(1)} %add.15), channel_id=1, source_target_pairs={{0,1},{1,0},{2,6},{3,7},{4,5},{5,4},{6,2},{7,3},{8,9},{9,8},{10,14... | collective-permute-start | bytes 331784 | tf_op jit(solution)/shard_map/ppermute | solution.py:516
  31.3 3.7 %collective-permute-start.5 = (f32[216,128]{1,0:T(8,128)S(1)}, f32[216,128]{1,0:T(8,128)S(1)}, u32[]{:S(2)}, u32[]{:S(2)}) collective-permute-start(f32[216,128]{1,0:T(8,128)S(1)} %add.16), channel_id=1, source_target_pairs={{0,4},{1,5},{2,3},{3,2},{4,0},{5,1},{6,7},{7,6},{8,12},{9,13},{10,... | collective-permute-start | bytes 331784 | tf_op jit(solution)/shard_map/ppermute | solution.py:516
  35.0 5.7 %collective-permute-start.7 = (f32[216,128]{1,0:T(8,128)S(1)}, f32[216,128]{1,0:T(8,128)S(1)}, u32[]{:S(2)}, u32[]{:S(2)}) collective-permute-start(f32[216,128]{1,0:T(8,128)S(1)} %add.17), channel_id=1, source_target_pairs={{0,8},{1,9},{2,18},{3,19},{4,12},{5,13},{6,22},{7,23},{8,0},{9,1},... | collective-permute-start | bytes 331784 | tf_op jit(solution)/shard_map/ppermute | solution.py:516
  35.1 13.9 %collective-permute-start.6 = (f32[4,8,16,128]{3,2,1,0:T(8,128)S(1)}, f32[4,8,16,128]{3,2,1,0:T(8,128)S(1)}, u32[]{:S(2)}, u32[]{:S(2)}) collective-permute-start(f32[4,8,16,128]{3,2,1,0:T(8,128)S(1)} %get-tuple-element.30), channel_id=1, source_target_pairs={{0,1},{1,0},{2,3},{3,2},{4,5},{5,4},{6,7},{7,6},{8,9},{9,8},{10,11... | collective-permute-start | bytes 786440 | tf_op jit(solution)/shard_map/ppermute | solution.py:519
  40.7 3.7 %collective-permute-start.8 = (f32[216,128]{1,0:T(8,128)S(1)}, f32[216,128]{1,0:T(8,128)S(1)}, u32[]{:S(2)}, u32[]{:S(2)}) collective-permute-start(f32[216,128]{1,0:T(8,128)S(1)} %add.18), channel_id=1, source_target_pairs={{0,16},{1,17},{2,10},{3,11},{4,20},{5,21},{6,14},{7,15},{8,24},{9,... | collective-permute-start | bytes 331784 | tf_op jit(solution)/shard_map/ppermute | solution.py:516
  44.4 5.7 %collective-permute-start.9 = (f32[216,128]{1,0:T(8,128)S(1)}, f32[216,128]{1,0:T(8,128)S(1)}, u32[]{:S(2)}, u32[]{:S(2)}) collective-permute-start(f32[216,128]{1,0:T(8,128)S(1)} %add.19.mine_ref), channel_id=1, source_target_pairs={{0,2},{1,3},{2,0},{3,1},{4,6},{5,7},{6,4},{7,5},{8,10},{9,11},{10,... | collective-permute-start | bytes 331784 | tf_op jit(solution)/shard_map/ppermute | solution.py:520

commit v3 on v2

--- a/solution.py
+++ b/solution.py
@@ -120,40 +120,25 @@
         out_ref[pl.ds(m, columns, stride=group), :] = (sums[2] + sums[1]) + sums[0]
 
 
-def prepare_kernel(wide, total_y, parts, cell_row, rate_ref, basis_hbm, inflow, inner_uu, basis, sems):
-    run = basis.shape[0] // parts
-    copies = [
-        pltpu.make_async_copy(basis_hbm.at[pl.ds(i * run, run)], basis.at[pl.ds(i * run, run)], sems.at[i])
-        for i in range(parts)
-    ]
-    for copy in copies:
-        copy.start()
-    inflow_rows(cell_row, rate_ref, inflow, wide, total_y)
-    total = jnp.zeros(inner_uu.shape, jnp.float32)
-    for i, copy in enumerate(copies):
-        copy.wait()
-        rows = basis[i * run : (i + 1) * run]
-        total += lax.dot_general(rows, rows, (((0,), (0,)), ((), ())), preferred_element_type=jnp.float32)
-    inner_uu[...] = total
-
-
-def prepare(well_cells, well_rate, flat, wide, total_y, lanes):
+def before_flux(well_cells, well_rate, perm_table, wide, total_y, lanes):
     members, wells = well_rate.shape
-    count = flat.shape[1]
-    parts = next(n for n in (4, 2, 1) if flat.shape[0] % (16 * n) == 0)
-    whole = pl.BlockSpec(memory_space=pltpu.VMEM)
-    inflow, inner_uu = pl.pallas_call(
-        functools.partial(prepare_kernel, wide, total_y, parts),
+
+    def kernel(cell_row, rate_ref, table_ref, out_ref, table_out):
+        inflow_rows(cell_row, rate_ref, out_ref, wide, total_y)
+        for d in range(table_ref.shape[0]):
+            for r in range(table_ref.shape[1]):
+                table_out[d, r : r + 1, :] = jnp.full((1, lanes), table_ref[d, r], jnp.float32)
+
+    inflow, table = pl.pallas_call(
+        kernel,
         out_shape=(
             jax.ShapeDtypeStruct((wide * total_y * members // 2, lanes), jnp.float32),
-            jax.ShapeDtypeStruct((count, count), jnp.float32),
+            jax.ShapeDtypeStruct(perm_table.shape + (lanes,), jnp.float32),
         ),
-        in_specs=[whole, whole, pl.BlockSpec(memory_space=pl.ANY)],
-        scratch_shapes=[pltpu.VMEM(flat.shape, jnp.bfloat16), pltpu.SemaphoreType.DMA((parts,))],
+        in_specs=[pl.BlockSpec(memory_space=pltpu.VMEM)] * 2 + [pl.BlockSpec(memory_space=pltpu.SMEM)],
         compiler_params=pltpu.CompilerParams(vmem_limit_bytes=VMEM_LIMIT),
-        cost_estimate=pl.CostEstimate(flops=4 * 10**9, bytes_accessed=2**20, transcendentals=0),
-    )(well_cells.reshape(1, wells), well_rate, flat)
-    return inflow.reshape(wide, total_y, members // 2, lanes), inner_uu
+    )(well_cells.reshape(1, wells), well_rate, perm_table)
+    return inflow.reshape(wide, total_y, members // 2, lanes), table
 
 
 def roll(value, shift):
@@ -185,15 +170,25 @@
     else:
         slab = refs[0]
         refs = refs[1:]
-    table, inflow, inner_uu, basis_hbm, snaps, keep, give, fin, send = refs[:9]
-    press_a, sat_a, press_b, sat_b, rock, perm, w12, w06, carry, history, sums, basis, sem = refs[9:]
+    table, inflow, basis_hbm, snaps, keep, give, fin, send = refs[:8]
+    press_a, sat_a, press_b, sat_b, rock, perm, w12, w06, carry, history, sums, inner_uu, basis, sems = refs[8:]
     wide, total_y = inflow.shape[:2]
     group, lanes = inflow.shape[2:]
     layers = lanes // 2
     blocks, along = rock.shape[1:3]
     rows = wide - 2 * STEPS
-    copy = pltpu.make_async_copy(basis_hbm, basis, sem)
-    copy.start()
+    parts = sems.shape[0]
+    cells = rows * total_y
+    copies = [
+        pltpu.make_async_copy(
+            basis_hbm.at[pl.ds(i * (cells // parts), cells // parts)],
+            basis.at[pl.ds(i * (cells // parts), cells // parts)],
+            sems.at[i],
+        )
+        for i in range(parts)
+    ]
+    for copy in copies:
+        copy.start()
     lane = lax.broadcasted_iota(jnp.int32, (group, lanes), 1)
     left_lanes = lane < layers
     lane_y = lax.broadcasted_iota(jnp.int32, (along, lanes), 1)
@@ -242,7 +237,7 @@
             values = [jnp.zeros((along, lanes), jnp.float32)] * 3
             for r in range(table.shape[1]):
                 here = kind == float(r)
-                values = [jnp.where(here, table[d, r], values[d]) for d in range(3)]
+                values = [jnp.where(here, jnp.broadcast_to(table[d, r : r + 1, :], here.shape), values[d]) for d in range(3)]
             for d in range(3):
                 perm[d, x, pl.ds(block * along, along), :] = values[d] * inside
         return c
@@ -351,14 +346,17 @@
                     ref[x, j, :group] = history[at, last]
                     ref[x, j, group:] = history[at, past]
 
-    copy.wait()
+    for copy in copies:
+        copy.wait()
     count = basis.shape[2]
-    cells = rows * total_y
     snap_count = 2 * STEPS * group
     run = next(n for n in (16, 8, 4, 2, 1) if cells % n == 0)
     inner_su = jnp.zeros((snap_count, count), jnp.float32)
     inner_ss = jnp.zeros((snap_count, snap_count), jnp.float32)
+    inner_uu[...] = jnp.zeros_like(inner_uu)
     for q in range(0, cells, run):
+        rows_q = basis[q : q + run].reshape(run * lanes, count)
+        inner_uu[...] += lax.dot_general(rows_q, rows_q, (((0,), (0,)), ((), ())), preferred_element_type=jnp.float32)
         part = [history[q + i].astype(jnp.bfloat16) for i in range(run)]
         for i in range(run):
             snaps[q + i] = part[i]
@@ -436,7 +434,7 @@
     grams[count + half : count + snap_count, count : count + snap_count] = folded[:, snap_count:]
 
 
-def flux(fields, perm_table, inflow, inner_uu, basis_blocks, along):
+def flux(fields, table, inflow, basis_blocks, along):
     fast = len(fields) > 1
     wide, total_y, group, lanes = inflow.shape
     blocks = total_y // along
@@ -459,7 +457,7 @@
         lambda *refs: flux_kernel(fast, *refs),
         out_shape=outs,
         in_specs=[whole] * len(fields)
-        + [pl.BlockSpec(memory_space=pltpu.SMEM), whole, whole, pl.BlockSpec(memory_space=pl.ANY)],
+        + [whole, whole, pl.BlockSpec(memory_space=pl.ANY)],
         scratch_shapes=[
             state, state, state, state,
             pltpu.VMEM((wide, blocks, along, lanes), f32),
@@ -469,11 +467,12 @@
             pltpu.VMEM((2, total_y, group, lanes), f32),
             pltpu.VMEM((rows * total_y, snaps, lanes), f32),
             pltpu.VMEM((folded, LANE), f32),
+            pltpu.VMEM((count, count), f32),
             pltpu.VMEM(basis_blocks.shape, jnp.bfloat16),
-            pltpu.SemaphoreType.DMA,
+            pltpu.SemaphoreType.DMA((next(n for n in (4, 2, 1) if rows * total_y % n == 0),)),
         ],
         compiler_params=pltpu.CompilerParams(vmem_limit_bytes=VMEM_LIMIT),
-    )(*fields, perm_table, inflow, inner_uu, basis_blocks)
+    )(*fields, table, inflow, basis_blocks)
 
 
 def unpack_kernel(parts, *refs):
@@ -669,13 +668,11 @@
         else:
             final = hdot(step, prior)
             high = final[:, :count].astype(jnp.bfloat16)
-            low = (final[:, :count] - high.astype(jnp.float32)).astype(jnp.bfloat16)
             weights[:count] = high.T
-            weights[count:2 * count] = low.T
             both = jnp.concatenate([final[:, count:].T[:snaps], aug[:, 2 * count:].T[:snaps]], 0)
             high = both.astype(jnp.bfloat16)
-            weights[2 * count:2 * count + 2 * snaps] = high
-            weights[2 * count + 2 * snaps:] = (both - high.astype(jnp.float32)).astype(jnp.bfloat16)
+            weights[count:count + 2 * snaps] = high
+            weights[count + 2 * snaps:] = (both - high.astype(jnp.float32)).astype(jnp.bfloat16)
     sigma_out[...] = jnp.sqrt(sig2)
     for copy in copies:
         copy.wait()
@@ -688,31 +685,27 @@
     run = cells // parts
 
     def out(i):
-        rows = pl.ds(pl.multiple_of(i * run * lanes, run * lanes), run * lanes)
+        rows = pl.ds(i * run * lanes, run * lanes)
         return pltpu.make_async_copy(fresh.at[rows], fresh_hbm.at[rows], out_sems.at[i])
 
-    def part(i, none):
-        at = pl.multiple_of(i * run * lanes, run * lanes)
+    def part(i):
+        at = i * run * lanes
         flat = basis[pl.ds(at, run * lanes), :]
         turned = []
         for q in range(run):
             one = snaps_ref[i * run + q]
             turned.append(jnp.concatenate([one, one], 0).T)
         value = jnp.dot(
-            jnp.concatenate([flat, flat, jnp.concatenate(turned, 0)], 1), weights[...],
+            jnp.concatenate([flat, jnp.concatenate(turned, 0)], 1), weights[...],
             preferred_element_type=jnp.float32,
         )
         fresh[pl.ds(at, run * lanes), :] = value.astype(jnp.bfloat16)
         out(i).start()
-        return none
-
-    lax.fori_loop(0, parts, part, 0)
-
-    def finish(i, none):
+
+    for i in range(parts):
+        part(i)
+    for i in range(parts):
         out(i).wait()
-        return none
-
-    lax.fori_loop(0, parts, finish, 0)
 
 
 def small(mine, other, sigma, snaps, flat, rows_total):
@@ -734,7 +727,7 @@
             pltpu.VMEM((count, 2 * count + LANE), jnp.float32),
             pltpu.VMEM((2 * mine.shape[0], LANE), jnp.float32),
             pltpu.VMEM((rows, count + LANE), jnp.float32),
-            pltpu.VMEM((2 * count + 2 * snap_count, count), jnp.bfloat16),
+            pltpu.VMEM((count + 2 * snap_count, count), jnp.bfloat16),
             pltpu.VMEM(snaps.shape, jnp.bfloat16),
             pltpu.VMEM(flat.shape, jnp.bfloat16),
             pltpu.VMEM(flat.shape, jnp.bfloat16),
@@ -780,9 +773,9 @@
         fields = (lax.dynamic_slice_in_dim(padded, lax.axis_index("sec") * rows, wide, axis=0),)
     flat = basis_in.reshape(-1, count)
     rows_total = flat.shape[0] * gx_count * sec_count
-    inflow, inner_uu = prepare(well_cells, well_rate, flat, wide, total_y, lanes)
+    inflow, table = before_flux(well_cells, well_rate, perm_table, wide, total_y, lanes)
     snaps, keep, give, fin, send = flux(
-        fields, perm_table, inflow, inner_uu, flat.reshape(-1, lanes, count), along
+        fields, table, inflow, flat.reshape(-1, lanes, count), along
     )
     mine, others, received = all_sum(keep, give, send if fast else None)
     if fast:

time: 77.3 us -> 73.4 us (0.950)
  waiting for transfers between devices: 14.4 us -> 19.8 us
  Pallas kernels: 39.8 us -> 35.9 us
  starting transfers between devices: 15.8 us -> 12.4 us
  local copies, waits for them, and re-layouts: 5.35 us -> 3.83 us
    ppermute x4, waiting for transfers between devices: 13.3 us -> 16.2 us  [all_sum(): lax.ppermute(value, AXES, [(i, i ^ (odd if i & pair else even)) for i in...]
    pallas_call x1, Pallas kernels: 4.12 us -> 1.75 us  [before_flux(): pl.pallas_call(kernel, out_shape=(jax.ShapeDtypeStruct((wide * total_y *...]
    ppermute x1, waiting for transfers between devices: 0.01 us -> 2.26 us  [body(): cross = lax.ppermute(inward, AXES, crossed)]
    pallas_call x1, Pallas kernels: 26.1 us -> 24 us  [small(): pl.pallas_call(functools.partial(small_kernel, 1.0 / rows_total), out_sha...]
    ppermute x4, starting transfers between devices: 2.15 us -> 0.53 us  [all_sum(): lax.ppermute(value, AXES, [(i, i ^ (odd if i & pair else even)) for i in...]
    unnamed x16 -> x14, local copies, waits for them, and re-layouts: 5.35 us -> 3.83 us
    ppermute x1, starting transfers between devices: 1.48 us -> 0.19 us  [all_sum(): swapped = lax.ppermute(beside, 'sec', [(0, 1), (1, 0)])]
  transfers between devices with their start and end apart: 10 -> 10, of which waited for: 5 -> 6; matrix products, arithmetic and copies ran while one was open for 0% -> 0% of each run, Pallas kernels for 7% -> 4%
where the time goes in v3:
time: 73.4 us; the launch traced here: 73 us
  Pallas kernels  35.9 us (49%)
  waiting for transfers between devices  19.8 us (27%)
  starting transfers between devices  12.4 us (17%)
  local copies, waits for them, and re-layouts  3.83 us (5%)
  between operations  0.93 us (1%)
    pallas_call x1, Pallas kernels, small(): pl.pallas_call(functools.partial(small_kernel, 1.0 / rows_total), out_sha...  24 us
    ppermute x4, waiting for transfers between devices, all_sum(): lax.ppermute(value, AXES, [(i, i ^ (odd if i & pair else even)) for i in...  16.2 us
    pallas_call x1, Pallas kernels, flux(): pl.pallas_call(lambda *refs: flux_kernel(fast, *refs), out_shape=outs, in...  8.59 us
    ppermute x1, starting transfers between devices, all_sum(): return (value, lax.ppermute(value, AXES, swap), swapped)  4.46 us
    ppermute x1, starting transfers between devices, body(): beside = lax.ppermute(outward, AXES, straight)  3.96 us
    unnamed x14, local copies, waits for them, and re-layouts  3.83 us
    ppermute x1, waiting for transfers between devices, body(): cross = lax.ppermute(inward, AXES, crossed)  2.26 us
    ppermute x1, starting transfers between devices, body(): cross = lax.ppermute(inward, AXES, crossed)  1.92 us
  transfers between devices with their start and end apart: 10, of which 6 were waited for; matrix products, arithmetic and copies ran while one was open for 0% of the time, Pallas kernels for 4%

profile of v3, /device:TPU:25, one launch (start us, length us, event | category | flops | bytes accessed | tf_op | source)
XLA Modules:
  0.0 73.0 jit_solution(10618353041579514934)
XLA Ops:
  0.6 0.0 copy-start.1
  0.6 1.0 %copy-done.1 = f32[16,8,8,128]{3,2,1,0:T(8,128)S(1)} copy-done((f32[16,8,8,128]{3,2,1,0:T(8,128)S(1)}, f32[16,8,8,128]{3,2,1,0:T(8,128)}, u32[]{:S(2)}) %copy-start.1) | copy-done | bytes 524312
  1.7 0.0 copy-start.2
  1.7 0.7 copy-done.2
  2.4 0.5 shard_map.94
  2.9 1.3 %collective-permute-start = (bf16[8,9,16,128]{3,2,1,0:T(8,128)(2,1)S(1)}, bf16[8,9,16,128]{3,2,1,0:T(8,128)(2,1)S(1)}, u32[]{:S(2)}, u32[]{:S(2)}) collective-permute-start(bf16[8,9,16,128]{3,2,1,0:T(8,128)(2,1)S(1)} %get-tuple-element.21.packed.refs_1_), channel_id=1, source_target_pairs={{0,1},{1,0},{2,3},{3,2},{4,5},{5,4},{6,7},{7,6},{8,9},{9,8},{10,11... | collective-permute-start | bytes 884744 | tf_op jit(solution)/shard_map/ppermute | solution.py:763
  4.2 4.0 %collective-permute-start.1 = (bf16[4,9,16,128]{3,2,1,0:T(8,128)(2,1)S(1)}, bf16[4,9,16,128]{3,2,1,0:T(8,128)(2,1)S(1)}, u32[]{:S(2)}, u32[]{:S(2)}) collective-permute-start(bf16[4,9,16,128]{3,2,1,0:T(8,128)(2,1)S(1)} %get-tuple-element.22), channel_id=1, source_target_pairs={{3,1},{0,2},{5,3},{2,4},{7,5},{4,6},{9,7},{6,8},{11,9},{8,10},{13,... | collective-permute-start | bytes 442376 | tf_op jit(solution)/shard_map/ppermute | solution.py:765
  8.2 1.9 %collective-permute-start.2 = (bf16[4,9,16,128]{3,2,1,0:T(8,128)(2,1)S(1)}, bf16[4,9,16,128]{3,2,1,0:T(8,128)(2,1)S(1)}, u32[]{:S(2)}, u32[]{:S(2)}) collective-permute-start(bf16[4,9,16,128]{3,2,1,0:T(8,128)(2,1)S(1)} %get-tuple-element.23), channel_id=1, source_target_pairs={{2,1},{1,2},{4,3},{3,4},{6,5},{5,6},{8,7},{7,8},{10,9},{9,10},{12,... | collective-permute-start | bytes 442376 | tf_op jit(solution)/shard_map/ppermute | solution.py:764
  10.1 0.0 copy-start.3
  10.1 0.7 copy-done.3
  10.8 0.0 copy-start.4
  10.8 0.7 copy-done.4
  11.5 0.0 copy-start.5
  11.5 0.7 copy-done.5
  12.2 1.8 %shard_map.96 = (f32[1536,128]{1,0:T(8,128)S(1)}, f32[3,16,128]{2,1,0:T(8,128)S(1)}) custom-call(s32[1,256]{1,0:T(1,128)S(1)} %bitcast.13, f32[16,256]{1,0:T(8,128)S(1)} %copy-done.3, f32[3,16]{1,0:T(4,128)S(1)} %copy-done.4), custom_call_target="tpu_custom_call" | custom-call | tf_op jit(solution)/shard_map/pallas_call | solution.py:132
  13.9 0.0 collective-permute-done.1.refs_3_
  13.9 2.3 %collective-permute-done.2.refs_4_ = bf16[4,9,16,128]{3,2,1,0:T(8,128)(2,1)S(1)} collective-permute-done((bf16[4,9,16,128]{3,2,1,0:T(8,128)(2,1)S(1)}, bf16[4,9,16,128]{3,2,1,0:T(8,128)(2,1)S(1)}, u32[]{:S(2)}, u32[]{:S(2)}) %collective-permute-start.2) | collective-permute-done | bytes 147488 | tf_op jit(solution)/shard_map/ppermute | solution.py:764
  16.2 0.0 collective-permute-done.refs_2_
  16.2 0.0 copy-start
  16.2 0.0 copy-start.6
  16.2 8.6 %shard_map.97 = (bf16[64,64,128]{2,1,0:T(8,128)(2,1)S(1)}, f32[216,128]{1,0:T(8,128)S(1)}, f32[216,128]{1,0:T(8,128)S(1)}, f32[4,8,16,128]{3,2,1,0:T(8,128)S(1)}, f32[4,8,16,128]{3,2,1,0:T(8,128)S(1)}) custom-call(f32[8,8,16,128]{3,2,1,0:T(8,128)S(1)} %get-tuple-element.20.refs_0_, bf16[8,9,16,128]{3,2,1,0:T(8,128)(2,1)S(1)} %get-tuple-element.21.packed.refs_1_, ...), custom_call_target="tpu_custom_call" | custom-call | tf_op jit(solution)/shard_map/pallas_call | solution.py:456
  24.8 0.1 collective-permute-start.3
  24.9 1.3 %collective-permute-done.3 = f32[216,128]{1,0:T(8,128)S(1)} collective-permute-done((f32[216,128]{1,0:T(8,128)S(1)}, f32[216,128]{1,0:T(8,128)S(1)}, u32[]{:S(2)}, u32[]{:S(2)}) %collective-permute-start.3) | collective-permute-done | bytes 110624 | tf_op jit(solution)/shard_map/ppermute | solution.py:509
  26.2 0.1 collective-permute-start.4
  26.3 3.9 %collective-permute-done.4 = f32[216,128]{1,0:T(8,128)S(1)} collective-permute-done((f32[216,128]{1,0:T(8,128)S(1)}, f32[216,128]{1,0:T(8,128)S(1)}, u32[]{:S(2)}, u32[]{:S(2)}) %collective-permute-start.4) | collective-permute-done | bytes 110624 | tf_op jit(solution)/shard_map/ppermute | solution.py:515
  30.2 0.3 collective-permute-start.5
  30.4 3.4 %collective-permute-done.5 = f32[216,128]{1,0:T(8,128)S(1)} collective-permute-done((f32[216,128]{1,0:T(8,128)S(1)}, f32[216,128]{1,0:T(8,128)S(1)}, u32[]{:S(2)}, u32[]{:S(2)}) %collective-permute-start.5) | collective-permute-done | bytes 110624 | tf_op jit(solution)/shard_map/ppermute | solution.py:515
  33.9 0.1 collective-permute-start.7
  34.0 0.2 collective-permute-start.6
  34.2 5.4 %collective-permute-done.7 = f32[216,128]{1,0:T(8,128)S(1)} collective-permute-done((f32[216,128]{1,0:T(8,128)S(1)}, f32[216,128]{1,0:T(8,128)S(1)}, u32[]{:S(2)}, u32[]{:S(2)}) %collective-permute-start.7) | collective-permute-done | bytes 110624 | tf_op jit(solution)/shard_map/ppermute | solution.py:515
  39.6 0.1 collective-permute-start.8
  39.6 3.6 %collective-permute-done.8 = f32[216,128]{1,0:T(8,128)S(1)} collective-permute-done((f32[216,128]{1,0:T(8,128)S(1)}, f32[216,128]{1,0:T(8,128)S(1)}, u32[]{:S(2)}, u32[]{:S(2)}) %collective-permute-start.8) | collective-permute-done | bytes 110624 | tf_op jit(solution)/shard_map/ppermute | solution.py:515
  43.2 4.5 %collective-permute-start.9 = (f32[216,128]{1,0:T(8,128)S(1)}, f32[216,128]{1,0:T(8,128)S(1)}, u32[]{:S(2)}, u32[]{:S(2)}) collective-permute-start(f32[216,128]{1,0:T(8,128)S(1)} %add.19.mine_ref), channel_id=1, source_target_pairs={{0,2},{1,3},{2,0},{3,1},{4,6},{5,7},{6,4},{7,5},{8,10},{9,11},{10,... | collective-permute-start | bytes 331784 | tf_op jit(solution)/shard_map/ppermute | solution.py:519
  47.7 0.0 collective-permute-done.6.refs_1_
  47.7 1.1 %shard_map.98 = f32[1024,128]{1,0:T(8,128)} custom-call(f32[4,8,16,128]{3,2,1,0:T(8,128)S(1)} %get-tuple-element.26.refs_0_, f32[4,8,16,128]{3,2,1,0:T(8,128)S(1)} %collective-permute-done.6.refs_1_), custom_call_target="tpu_custom_call" | custom-call | tf_op jit(solution)/shard_map/pallas_call | solution.py:495
  48.8 0.0 collective-permute-done.9.other_ref
  48.8 0.0 copy-done
  48.8 0.0 copy-done.6
  48.8 24.0 %shard_map.99 = (bf16[8192,256]{1,0:T(8,128)(2,1)}, f32[1,256]{1,0:T(1,128)}) custom-call(f32[216,128]{1,0:T(8,128)S(1)} %add.19.mine_ref, f32[216,128]{1,0:T(8,128)S(1)} %collective-permute-done.9.other_ref, f32[1,256]{1,0:T(1,128)S(1)} %bitcast.14, bf16[64,64,128]{2,1,0:T(8,128)(2,1)S(1)} %get-tuple-element.34.snaps_hbm, bf16[8192,256]{1,0:T(8,128)(2,1)S(1)} %bitcast.10), custom_call_target="tpu_custom_call" | custom-call | flops 20000000000 | bytes 1048576 | tf_op jit(solution)/shard_map/pallas_call | solution.py:718
  (6 shorter events, 0.1 us)
Async XLA Ops:
  0.6 1.0 %copy-start.1 = (f32[16,8,8,128]{3,2,1,0:T(8,128)S(1)}, f32[16,8,8,128]{3,2,1,0:T(8,128)}, u32[]{:S(2)}) copy-start(f32[16,8,8,128]{3,2,1,0:T(8,128)} %param.7) | copy-start | bytes 1572868
  1.7 0.7 copy-start.2
  2.9 13.3 %collective-permute-start = (bf16[8,9,16,128]{3,2,1,0:T(8,128)(2,1)S(1)}, bf16[8,9,16,128]{3,2,1,0:T(8,128)(2,1)S(1)}, u32[]{:S(2)}, u32[]{:S(2)}) collective-permute-start(bf16[8,9,16,128]{3,2,1,0:T(8,128)(2,1)S(1)} %get-tuple-element.21.packed.refs_1_), channel_id=1, source_target_pairs={{0,1},{1,0},{2,3},{3,2},{4,5},{5,4},{6,7},{7,6},{8,9},{9,8},{10,11... | collective-permute-start | bytes 884744 | tf_op jit(solution)/shard_map/ppermute | solution.py:763
  4.2 9.7 %collective-permute-start.1 = (bf16[4,9,16,128]{3,2,1,0:T(8,128)(2,1)S(1)}, bf16[4,9,16,128]{3,2,1,0:T(8,128)(2,1)S(1)}, u32[]{:S(2)}, u32[]{:S(2)}) collective-permute-start(bf16[4,9,16,128]{3,2,1,0:T(8,128)(2,1)S(1)} %get-tuple-element.22), channel_id=1, source_target_pairs={{3,1},{0,2},{5,3},{2,4},{7,5},{4,6},{9,7},{6,8},{11,9},{8,10},{13,... | collective-permute-start | bytes 442376 | tf_op jit(solution)/shard_map/ppermute | solution.py:765
  8.2 8.0 %collective-permute-start.2 = (bf16[4,9,16,128]{3,2,1,0:T(8,128)(2,1)S(1)}, bf16[4,9,16,128]{3,2,1,0:T(8,128)(2,1)S(1)}, u32[]{:S(2)}, u32[]{:S(2)}) collective-permute-start(bf16[4,9,16,128]{3,2,1,0:T(8,128)(2,1)S(1)} %get-tuple-element.23), channel_id=1, source_target_pairs={{2,1},{1,2},{4,3},{3,4},{6,5},{5,6},{8,7},{7,8},{10,9},{9,10},{12,... | collective-permute-start | bytes 442376 | tf_op jit(solution)/shard_map/ppermute | solution.py:764
  10.1 0.7 copy-start.3
  10.8 0.7 copy-start.4
  11.5 0.7 copy-start.5
  16.2 32.6 %copy-start = (bf16[4,16,128,256]{3,2,1,0:T(8,128)(2,1)S(1)}, bf16[4,16,128,256]{3,2,1,0:T(8,128)(2,1)}, u32[]{:S(2)}) copy-start(bf16[4,16,128,256]{3,2,1,0:T(8,128)(2,1)} %param.12) | copy-start | bytes 12582916
  16.2 32.6 %copy-start.6 = (f32[256]{0:T(256)S(1)}, f32[256]{0:T(256)}, u32[]{:S(2)}) copy-start(f32[256]{0:T(256)} %param.13) | copy-start | bytes 3076
  24.8 1.4 %collective-permute-start.3 = (f32[216,128]{1,0:T(8,128)S(1)}, f32[216,128]{1,0:T(8,128)S(1)}, u32[]{:S(2)}, u32[]{:S(2)}) collective-permute-start(f32[216,128]{1,0:T(8,128)S(1)} %get-tuple-element.29), channel_id=1, source_target_pairs={{0,2},{1,3},{2,0},{3,1},{4,6},{5,7},{6,4},{7,5},{8,10},{9,11},{10,... | collective-permute-start | bytes 331784 | tf_op jit(solution)/shard_map/ppermute | solution.py:509
  26.2 4.0 %collective-permute-start.4 = (f32[216,128]{1,0:T(8,128)S(1)}, f32[216,128]{1,0:T(8,128)S(1)}, u32[]{:S(2)}, u32[]{:S(2)}) collective-permute-start(f32[216,128]{1,0:T(8,128)S(1)} %add.15), channel_id=1, source_target_pairs={{0,1},{1,0},{2,6},{3,7},{4,5},{5,4},{6,2},{7,3},{8,9},{9,8},{10,14... | collective-permute-start | bytes 331784 | tf_op jit(solution)/shard_map/ppermute | solution.py:515
  30.2 3.7 %collective-permute-start.5 = (f32[216,128]{1,0:T(8,128)S(1)}, f32[216,128]{1,0:T(8,128)S(1)}, u32[]{:S(2)}, u32[]{:S(2)}) collective-permute-start(f32[216,128]{1,0:T(8,128)S(1)} %add.16), channel_id=1, source_target_pairs={{0,4},{1,5},{2,3},{3,2},{4,0},{5,1},{6,7},{7,6},{8,12},{9,13},{10,... | collective-permute-start | bytes 331784 | tf_op jit(solution)/shard_map/ppermute | solution.py:515
  33.9 5.7 %collective-permute-start.7 = (f32[216,128]{1,0:T(8,128)S(1)}, f32[216,128]{1,0:T(8,128)S(1)}, u32[]{:S(2)}, u32[]{:S(2)}) collective-permute-start(f32[216,128]{1,0:T(8,128)S(1)} %add.17), channel_id=1, source_target_pairs={{0,8},{1,9},{2,18},{3,19},{4,12},{5,13},{6,22},{7,23},{8,0},{9,1},... | collective-permute-start | bytes 331784 | tf_op jit(solution)/shard_map/ppermute | solution.py:515
  34.0 13.7 %collective-permute-start.6 = (f32[4,8,16,128]{3,2,1,0:T(8,128)S(1)}, f32[4,8,16,128]{3,2,1,0:T(8,128)S(1)}, u32[]{:S(2)}, u32[]{:S(2)}) collective-permute-start(f32[4,8,16,128]{3,2,1,0:T(8,128)S(1)} %get-tuple-element.30), channel_id=1, source_target_pairs={{0,1},{1,0},{2,3},{3,2},{4,5},{5,4},{6,7},{7,6},{8,9},{9,8},{10,11... | collective-permute-start | bytes 786440 | tf_op jit(solution)/shard_map/ppermute | solution.py:518
  39.6 3.7 %collective-permute-start.8 = (f32[216,128]{1,0:T(8,128)S(1)}, f32[216,128]{1,0:T(8,128)S(1)}, u32[]{:S(2)}, u32[]{:S(2)}) collective-permute-start(f32[216,128]{1,0:T(8,128)S(1)} %add.18), channel_id=1, source_target_pairs={{0,16},{1,17},{2,10},{3,11},{4,20},{5,21},{6,14},{7,15},{8,24},{9,... | collective-permute-start | bytes 331784 | tf_op jit(solution)/shard_map/ppermute | solution.py:515
  43.2 5.6 %collective-permute-start.9 = (f32[216,128]{1,0:T(8,128)S(1)}, f32[216,128]{1,0:T(8,128)S(1)}, u32[]{:S(2)}, u32[]{:S(2)}) collective-permute-start(f32[216,128]{1,0:T(8,128)S(1)} %add.19.mine_ref), channel_id=1, source_target_pairs={{0,2},{1,3},{2,0},{3,1},{4,6},{5,7},{6,4},{7,5},{8,10},{9,11},{10,... | collective-permute-start | bytes 331784 | tf_op jit(solution)/shard_map/ppermute | solution.py:519

commit v4 on v3

--- a/solution.py
+++ b/solution.py
@@ -610,6 +610,13 @@
             left, right = left_stack(parts), right_stack(parts)
             change = stacked_dot(left[:, :count - base], right)
             aug[rest:, base:] = aug[rest:, base:] - change[rest - base:]
+
+def next_squares(turned, extra, coeffs, gram, sig2):
+    energy = turned * turned * sig2
+    ones = jnp.ones((8, turned.shape[0]), jnp.float32)
+    low = hdot(turned, coeffs, 1, 1) + hdot(extra, gram)
+    return hdot(ones, energy, 1, 1)[:1] + hdot(ones[:, : low.shape[1]], low * low, 1, 1)[:1]
+
 
 def small_kernel(
     scale, mine_ref, other_ref, sigma_ref, snaps_hbm, basis_hbm, fresh_hbm, sigma_out,
@@ -658,12 +665,9 @@
         solve(aug, count)
         turned = aug[:, count:2 * count]
         extra = aug[:, 2 * count:2 * count + snaps]
-        energy = turned * turned * sig2
-        ones = jnp.ones((8, count), jnp.float32)
-        low = hdot(turned, coeffs, 1, 1) + hdot(extra, gram)
-        sig2 = hdot(ones, energy, 1, 1)[:1] + hdot(ones[:, :snaps], low * low, 1, 1)[:1]
         step = turned.astype(jnp.bfloat16).astype(jnp.float32) - hdot(extra, rounded)
         if group == 0:
+            sig2 = next_squares(turned, extra, coeffs, gram, sig2)
             prior = jnp.concatenate([step, aug[:, 2 * count:]], 1)
         else:
             final = hdot(step, prior)
@@ -673,10 +677,11 @@
             high = both.astype(jnp.bfloat16)
             weights[count:count + 2 * snaps] = high
             weights[count + 2 * snaps:] = (both - high.astype(jnp.float32)).astype(jnp.bfloat16)
-    sigma_out[...] = jnp.sqrt(sig2)
     for copy in copies:
         copy.wait()
-    renew(weights, snaps_ref, basis, fresh, fresh_hbm, out_sems)
+    wait_all = renew(weights, snaps_ref, basis, fresh, fresh_hbm, out_sems)
+    sigma_out[...] = jnp.sqrt(next_squares(turned, extra, coeffs, gram, sig2))
+    wait_all()
 
 
 def renew(weights, snaps_ref, basis, fresh, fresh_hbm, out_sems):
@@ -704,8 +709,12 @@
 
     for i in range(parts):
         part(i)
-    for i in range(parts):
-        out(i).wait()
+
+    def wait_all():
+        for i in range(parts):
+            out(i).wait()
+
+    return wait_all
 
 
 def small(mine, other, sigma, snaps, flat, rows_total):

time: 73.4 us -> 72.6 us (0.989)
  Pallas kernels: 35.9 us -> 35.1 us
    pallas_call x1, Pallas kernels: 24 us -> 23.2 us  [small(): pl.pallas_call(functools.partial(small_kernel, 1.0 / rows_total), out_sha...]
where the time goes in v4:
time: 72.6 us; the launch traced here: 72.2 us
  Pallas kernels  35.1 us (48%)
  waiting for transfers between devices  19.8 us (27%)
  starting transfers between devices  12.4 us (17%)
  local copies, waits for them, and re-layouts  3.83 us (5%)
  between operations  0.93 us (1%)
    pallas_call x1, Pallas kernels, small(): pl.pallas_call(functools.partial(small_kernel, 1.0 / rows_total), out_sha...  23.2 us
    ppermute x4, waiting for transfers between devices, all_sum(): lax.ppermute(value, AXES, [(i, i ^ (odd if i & pair else even)) for i in...  16.2 us
    pallas_call x1, Pallas kernels, flux(): pl.pallas_call(lambda *refs: flux_kernel(fast, *refs), out_shape=outs, in...  8.59 us
    ppermute x1, starting transfers between devices, all_sum(): return (value, lax.ppermute(value, AXES, swap), swapped)  4.46 us
    ppermute x1, starting transfers between devices, body(): beside = lax.ppermute(outward, AXES, straight)  3.96 us
    unnamed x14, local copies, waits for them, and re-layouts  3.83 us
    ppermute x1, waiting for transfers between devices, body(): cross = lax.ppermute(inward, AXES, crossed)  2.26 us
    ppermute x1, starting transfers between devices, body(): cross = lax.ppermute(inward, AXES, crossed)  1.92 us
  transfers between devices with their start and end apart: 10, of which 6 were waited for; matrix products, arithmetic and copies ran while one was open for 0% of the time, Pallas kernels for 4%

profile of v4, /device:TPU:25, one launch (start us, length us, event | category | flops | bytes accessed | tf_op | source)
XLA Modules:
  0.0 72.2 jit_solution(13069563062036115643)
XLA Ops:
  0.6 0.0 copy-start.1
  0.6 1.0 %copy-done.1 = f32[16,8,8,128]{3,2,1,0:T(8,128)S(1)} copy-done((f32[16,8,8,128]{3,2,1,0:T(8,128)S(1)}, f32[16,8,8,128]{3,2,1,0:T(8,128)}, u32[]{:S(2)}) %copy-start.1) | copy-done | bytes 524312
  1.7 0.0 copy-start.2
  1.7 0.7 copy-done.2
  2.4 0.5 shard_map.94
  2.9 1.3 %collective-permute-start = (bf16[8,9,16,128]{3,2,1,0:T(8,128)(2,1)S(1)}, bf16[8,9,16,128]{3,2,1,0:T(8,128)(2,1)S(1)}, u32[]{:S(2)}, u32[]{:S(2)}) collective-permute-start(bf16[8,9,16,128]{3,2,1,0:T(8,128)(2,1)S(1)} %get-tuple-element.21.packed.refs_1_), channel_id=1, source_target_pairs={{0,1},{1,0},{2,3},{3,2},{4,5},{5,4},{6,7},{7,6},{8,9},{9,8},{10,11... | collective-permute-start | bytes 884744 | tf_op jit(solution)/shard_map/ppermute | solution.py:772
  4.2 4.0 %collective-permute-start.1 = (bf16[4,9,16,128]{3,2,1,0:T(8,128)(2,1)S(1)}, bf16[4,9,16,128]{3,2,1,0:T(8,128)(2,1)S(1)}, u32[]{:S(2)}, u32[]{:S(2)}) collective-permute-start(bf16[4,9,16,128]{3,2,1,0:T(8,128)(2,1)S(1)} %get-tuple-element.22), channel_id=1, source_target_pairs={{3,1},{0,2},{5,3},{2,4},{7,5},{4,6},{9,7},{6,8},{11,9},{8,10},{13,... | collective-permute-start | bytes 442376 | tf_op jit(solution)/shard_map/ppermute | solution.py:774
  8.2 1.9 %collective-permute-start.2 = (bf16[4,9,16,128]{3,2,1,0:T(8,128)(2,1)S(1)}, bf16[4,9,16,128]{3,2,1,0:T(8,128)(2,1)S(1)}, u32[]{:S(2)}, u32[]{:S(2)}) collective-permute-start(bf16[4,9,16,128]{3,2,1,0:T(8,128)(2,1)S(1)} %get-tuple-element.23), channel_id=1, source_target_pairs={{2,1},{1,2},{4,3},{3,4},{6,5},{5,6},{8,7},{7,8},{10,9},{9,10},{12,... | collective-permute-start | bytes 442376 | tf_op jit(solution)/shard_map/ppermute | solution.py:773
  10.1 0.0 copy-start.3
  10.1 0.7 copy-done.3
  10.8 0.0 copy-start.4
  10.8 0.7 copy-done.4
  11.5 0.0 copy-start.5
  11.5 0.7 copy-done.5
  12.2 1.8 %shard_map.96 = (f32[1536,128]{1,0:T(8,128)S(1)}, f32[3,16,128]{2,1,0:T(8,128)S(1)}) custom-call(s32[1,256]{1,0:T(1,128)S(1)} %bitcast.13, f32[16,256]{1,0:T(8,128)S(1)} %copy-done.3, f32[3,16]{1,0:T(4,128)S(1)} %copy-done.4), custom_call_target="tpu_custom_call" | custom-call | tf_op jit(solution)/shard_map/pallas_call | solution.py:132
  13.9 0.0 collective-permute-done.1.refs_3_
  13.9 2.3 %collective-permute-done.2.refs_4_ = bf16[4,9,16,128]{3,2,1,0:T(8,128)(2,1)S(1)} collective-permute-done((bf16[4,9,16,128]{3,2,1,0:T(8,128)(2,1)S(1)}, bf16[4,9,16,128]{3,2,1,0:T(8,128)(2,1)S(1)}, u32[]{:S(2)}, u32[]{:S(2)}) %collective-permute-start.2) | collective-permute-done | bytes 147488 | tf_op jit(solution)/shard_map/ppermute | solution.py:773
  16.2 0.0 collective-permute-done.refs_2_
  16.2 0.0 copy-start
  16.2 0.0 copy-start.6
  16.2 8.6 %shard_map.97 = (bf16[64,64,128]{2,1,0:T(8,128)(2,1)S(1)}, f32[216,128]{1,0:T(8,128)S(1)}, f32[216,128]{1,0:T(8,128)S(1)}, f32[4,8,16,128]{3,2,1,0:T(8,128)S(1)}, f32[4,8,16,128]{3,2,1,0:T(8,128)S(1)}) custom-call(f32[8,8,16,128]{3,2,1,0:T(8,128)S(1)} %get-tuple-element.20.refs_0_, bf16[8,9,16,128]{3,2,1,0:T(8,128)(2,1)S(1)} %get-tuple-element.21.packed.refs_1_, ...), custom_call_target="tpu_custom_call" | custom-call | tf_op jit(solution)/shard_map/pallas_call | solution.py:456
  24.8 0.1 collective-permute-start.3
  24.9 1.3 %collective-permute-done.3 = f32[216,128]{1,0:T(8,128)S(1)} collective-permute-done((f32[216,128]{1,0:T(8,128)S(1)}, f32[216,128]{1,0:T(8,128)S(1)}, u32[]{:S(2)}, u32[]{:S(2)}) %collective-permute-start.3) | collective-permute-done | bytes 110624 | tf_op jit(solution)/shard_map/ppermute | solution.py:509
  26.2 0.1 collective-permute-start.4
  26.3 3.9 %collective-permute-done.4 = f32[216,128]{1,0:T(8,128)S(1)} collective-permute-done((f32[216,128]{1,0:T(8,128)S(1)}, f32[216,128]{1,0:T(8,128)S(1)}, u32[]{:S(2)}, u32[]{:S(2)}) %collective-permute-start.4) | collective-permute-done | bytes 110624 | tf_op jit(solution)/shard_map/ppermute | solution.py:515
  30.2 0.3 collective-permute-start.5
  30.4 3.4 %collective-permute-done.5 = f32[216,128]{1,0:T(8,128)S(1)} collective-permute-done((f32[216,128]{1,0:T(8,128)S(1)}, f32[216,128]{1,0:T(8,128)S(1)}, u32[]{:S(2)}, u32[]{:S(2)}) %collective-permute-start.5) | collective-permute-done | bytes 110624 | tf_op jit(solution)/shard_map/ppermute | solution.py:515
  33.9 0.1 collective-permute-start.7
  34.0 0.2 collective-permute-start.6
  34.2 5.4 %collective-permute-done.7 = f32[216,128]{1,0:T(8,128)S(1)} collective-permute-done((f32[216,128]{1,0:T(8,128)S(1)}, f32[216,128]{1,0:T(8,128)S(1)}, u32[]{:S(2)}, u32[]{:S(2)}) %collective-permute-start.7) | collective-permute-done | bytes 110624 | tf_op jit(solution)/shard_map/ppermute | solution.py:515
  39.6 0.1 collective-permute-start.8
  39.6 3.6 %collective-permute-done.8 = f32[216,128]{1,0:T(8,128)S(1)} collective-permute-done((f32[216,128]{1,0:T(8,128)S(1)}, f32[216,128]{1,0:T(8,128)S(1)}, u32[]{:S(2)}, u32[]{:S(2)}) %collective-permute-start.8) | collective-permute-done | bytes 110624 | tf_op jit(solution)/shard_map/ppermute | solution.py:515
  43.2 4.5 %collective-permute-start.9 = (f32[216,128]{1,0:T(8,128)S(1)}, f32[216,128]{1,0:T(8,128)S(1)}, u32[]{:S(2)}, u32[]{:S(2)}) collective-permute-start(f32[216,128]{1,0:T(8,128)S(1)} %add.19.mine_ref), channel_id=1, source_target_pairs={{0,2},{1,3},{2,0},{3,1},{4,6},{5,7},{6,4},{7,5},{8,10},{9,11},{10,... | collective-permute-start | bytes 331784 | tf_op jit(solution)/shard_map/ppermute | solution.py:519
  47.7 0.0 collective-permute-done.6.refs_1_
  47.7 1.1 %shard_map.98 = f32[1024,128]{1,0:T(8,128)} custom-call(f32[4,8,16,128]{3,2,1,0:T(8,128)S(1)} %get-tuple-element.26.refs_0_, f32[4,8,16,128]{3,2,1,0:T(8,128)S(1)} %collective-permute-done.6.refs_1_), custom_call_target="tpu_custom_call" | custom-call | tf_op jit(solution)/shard_map/pallas_call | solution.py:495
  48.8 0.0 collective-permute-done.9.other_ref
  48.8 0.0 copy-done
  48.8 0.0 copy-done.6
  48.8 23.2 %shard_map.99 = (bf16[8192,256]{1,0:T(8,128)(2,1)}, f32[1,256]{1,0:T(1,128)}) custom-call(f32[216,128]{1,0:T(8,128)S(1)} %add.19.mine_ref, f32[216,128]{1,0:T(8,128)S(1)} %collective-permute-done.9.other_ref, f32[1,256]{1,0:T(1,128)S(1)} %bitcast.14, bf16[64,64,128]{2,1,0:T(8,128)(2,1)S(1)} %get-tuple-element.34.snaps_hbm, bf16[8192,256]{1,0:T(8,128)(2,1)S(1)} %bitcast.10), custom_call_target="tpu_custom_call" | custom-call | flops 20000000000 | bytes 1048576 | tf_op jit(solution)/shard_map/pallas_call | solution.py:727
  (6 shorter events, 0.1 us)
Async XLA Ops:
  0.6 1.0 %copy-start.1 = (f32[16,8,8,128]{3,2,1,0:T(8,128)S(1)}, f32[16,8,8,128]{3,2,1,0:T(8,128)}, u32[]{:S(2)}) copy-start(f32[16,8,8,128]{3,2,1,0:T(8,128)} %param.7) | copy-start | bytes 1572868
  1.7 0.7 copy-start.2
  2.9 13.3 %collective-permute-start = (bf16[8,9,16,128]{3,2,1,0:T(8,128)(2,1)S(1)}, bf16[8,9,16,128]{3,2,1,0:T(8,128)(2,1)S(1)}, u32[]{:S(2)}, u32[]{:S(2)}) collective-permute-start(bf16[8,9,16,128]{3,2,1,0:T(8,128)(2,1)S(1)} %get-tuple-element.21.packed.refs_1_), channel_id=1, source_target_pairs={{0,1},{1,0},{2,3},{3,2},{4,5},{5,4},{6,7},{7,6},{8,9},{9,8},{10,11... | collective-permute-start | bytes 884744 | tf_op jit(solution)/shard_map/ppermute | solution.py:772
  4.2 9.7 %collective-permute-start.1 = (bf16[4,9,16,128]{3,2,1,0:T(8,128)(2,1)S(1)}, bf16[4,9,16,128]{3,2,1,0:T(8,128)(2,1)S(1)}, u32[]{:S(2)}, u32[]{:S(2)}) collective-permute-start(bf16[4,9,16,128]{3,2,1,0:T(8,128)(2,1)S(1)} %get-tuple-element.22), channel_id=1, source_target_pairs={{3,1},{0,2},{5,3},{2,4},{7,5},{4,6},{9,7},{6,8},{11,9},{8,10},{13,... | collective-permute-start | bytes 442376 | tf_op jit(solution)/shard_map/ppermute | solution.py:774
  8.2 8.0 %collective-permute-start.2 = (bf16[4,9,16,128]{3,2,1,0:T(8,128)(2,1)S(1)}, bf16[4,9,16,128]{3,2,1,0:T(8,128)(2,1)S(1)}, u32[]{:S(2)}, u32[]{:S(2)}) collective-permute-start(bf16[4,9,16,128]{3,2,1,0:T(8,128)(2,1)S(1)} %get-tuple-element.23), channel_id=1, source_target_pairs={{2,1},{1,2},{4,3},{3,4},{6,5},{5,6},{8,7},{7,8},{10,9},{9,10},{12,... | collective-permute-start | bytes 442376 | tf_op jit(solution)/shard_map/ppermute | solution.py:773
  10.1 0.7 copy-start.3
  10.8 0.7 copy-start.4
  11.5 0.7 copy-start.5
  16.2 32.6 %copy-start = (bf16[4,16,128,256]{3,2,1,0:T(8,128)(2,1)S(1)}, bf16[4,16,128,256]{3,2,1,0:T(8,128)(2,1)}, u32[]{:S(2)}) copy-start(bf16[4,16,128,256]{3,2,1,0:T(8,128)(2,1)} %param.12) | copy-start | bytes 12582916
  16.2 32.6 %copy-start.6 = (f32[256]{0:T(256)S(1)}, f32[256]{0:T(256)}, u32[]{:S(2)}) copy-start(f32[256]{0:T(256)} %param.13) | copy-start | bytes 3076
  24.8 1.4 %collective-permute-start.3 = (f32[216,128]{1,0:T(8,128)S(1)}, f32[216,128]{1,0:T(8,128)S(1)}, u32[]{:S(2)}, u32[]{:S(2)}) collective-permute-start(f32[216,128]{1,0:T(8,128)S(1)} %get-tuple-element.29), channel_id=1, source_target_pairs={{0,2},{1,3},{2,0},{3,1},{4,6},{5,7},{6,4},{7,5},{8,10},{9,11},{10,... | collective-permute-start | bytes 331784 | tf_op jit(solution)/shard_map/ppermute | solution.py:509
  26.2 4.0 %collective-permute-start.4 = (f32[216,128]{1,0:T(8,128)S(1)}, f32[216,128]{1,0:T(8,128)S(1)}, u32[]{:S(2)}, u32[]{:S(2)}) collective-permute-start(f32[216,128]{1,0:T(8,128)S(1)} %add.15), channel_id=1, source_target_pairs={{0,1},{1,0},{2,6},{3,7},{4,5},{5,4},{6,2},{7,3},{8,9},{9,8},{10,14... | collective-permute-start | bytes 331784 | tf_op jit(solution)/shard_map/ppermute | solution.py:515
  30.2 3.7 %collective-permute-start.5 = (f32[216,128]{1,0:T(8,128)S(1)}, f32[216,128]{1,0:T(8,128)S(1)}, u32[]{:S(2)}, u32[]{:S(2)}) collective-permute-start(f32[216,128]{1,0:T(8,128)S(1)} %add.16), channel_id=1, source_target_pairs={{0,4},{1,5},{2,3},{3,2},{4,0},{5,1},{6,7},{7,6},{8,12},{9,13},{10,... | collective-permute-start | bytes 331784 | tf_op jit(solution)/shard_map/ppermute | solution.py:515
  33.9 5.7 %collective-permute-start.7 = (f32[216,128]{1,0:T(8,128)S(1)}, f32[216,128]{1,0:T(8,128)S(1)}, u32[]{:S(2)}, u32[]{:S(2)}) collective-permute-start(f32[216,128]{1,0:T(8,128)S(1)} %add.17), channel_id=1, source_target_pairs={{0,8},{1,9},{2,18},{3,19},{4,12},{5,13},{6,22},{7,23},{8,0},{9,1},... | collective-permute-start | bytes 331784 | tf_op jit(solution)/shard_map/ppermute | solution.py:515
  34.0 13.7 %collective-permute-start.6 = (f32[4,8,16,128]{3,2,1,0:T(8,128)S(1)}, f32[4,8,16,128]{3,2,1,0:T(8,128)S(1)}, u32[]{:S(2)}, u32[]{:S(2)}) collective-permute-start(f32[4,8,16,128]{3,2,1,0:T(8,128)S(1)} %get-tuple-element.30), channel_id=1, source_target_pairs={{0,1},{1,0},{2,3},{3,2},{4,5},{5,4},{6,7},{7,6},{8,9},{9,8},{10,11... | collective-permute-start | bytes 786440 | tf_op jit(solution)/shard_map/ppermute | solution.py:518
  39.6 3.7 %collective-permute-start.8 = (f32[216,128]{1,0:T(8,128)S(1)}, f32[216,128]{1,0:T(8,128)S(1)}, u32[]{:S(2)}, u32[]{:S(2)}) collective-permute-start(f32[216,128]{1,0:T(8,128)S(1)} %add.18), channel_id=1, source_target_pairs={{0,16},{1,17},{2,10},{3,11},{4,20},{5,21},{6,14},{7,15},{8,24},{9,... | collective-permute-start | bytes 331784 | tf_op jit(solution)/shard_map/ppermute | solution.py:515
  43.2 5.6 %collective-permute-start.9 = (f32[216,128]{1,0:T(8,128)S(1)}, f32[216,128]{1,0:T(8,128)S(1)}, u32[]{:S(2)}, u32[]{:S(2)}) collective-permute-start(f32[216,128]{1,0:T(8,128)S(1)} %add.19.mine_ref), channel_id=1, source_target_pairs={{0,2},{1,3},{2,0},{3,1},{4,6},{5,7},{6,4},{7,5},{8,10},{9,11},{10,... | collective-permute-start | bytes 331784 | tf_op jit(solution)/shard_map/ppermute | solution.py:519

commit v5 on v4

--- a/solution.py
+++ b/solution.py
@@ -242,7 +242,7 @@
                 perm[d, x, pl.ds(block * along, along), :] = values[d] * inside
         return c
 
-    several(wide, look_up, 4)
+    several(wide, look_up, 6)
     for d in range(3):
         perm[d, wide] = jnp.zeros(perm.shape[2:], jnp.float32)
     perm[1, :, total_y:, :] = jnp.zeros((wide + 1, perm.shape[2] - total_y, lanes), jnp.float32)
@@ -259,7 +259,7 @@
                 w06[d, x, block] = DT_SATURATION * weight
         return c
 
-    several(wide, weigh, 4)
+    several(wide, weigh, 6)
 
     def spread(ref, d, x, block, j):
         return jnp.broadcast_to(ref[d, x, block, j : j + 1, :], (group, lanes))
@@ -334,7 +334,7 @@
 
             return lax.fori_loop(0, chunks, save_chunk, none)
 
-        several(rows, save, 2)
+        several(rows, save, 4)
 
     if fast:
         last = slice((STEPS - 1) * group, STEPS * group)

time: 72.6 us -> 72.2 us (level)
  no operation moved by 1% of the time
where the time goes in v5:
time: 72.2 us; the launch traced here: 71.8 us
  Pallas kernels  34.7 us (48%)
  waiting for transfers between devices  19.8 us (27%)
  starting transfers between devices  12.5 us (17%)
  local copies, waits for them, and re-layouts  3.83 us (5%)
  between operations  0.93 us (1%)
    pallas_call x1, Pallas kernels, small(): pl.pallas_call(functools.partial(small_kernel, 1.0 / rows_total), out_sha...  23.2 us
    ppermute x4, waiting for transfers between devices, all_sum(): lax.ppermute(value, AXES, [(i, i ^ (odd if i & pair else even)) for i in...  16.2 us
    pallas_call x1, Pallas kernels, flux(): pl.pallas_call(lambda *refs: flux_kernel(fast, *refs), out_shape=outs, in...  8.17 us
    ppermute x1, starting transfers between devices, all_sum(): return (value, lax.ppermute(value, AXES, swap), swapped)  4.46 us
    ppermute x1, starting transfers between devices, body(): beside = lax.ppermute(outward, AXES, straight)  3.96 us
    unnamed x14, local copies, waits for them, and re-layouts  3.83 us
    ppermute x1, waiting for transfers between devices, body(): cross = lax.ppermute(inward, AXES, crossed)  2.26 us
    ppermute x1, starting transfers between devices, body(): cross = lax.ppermute(inward, AXES, crossed)  1.92 us
  transfers between devices with their start and end apart: 10, of which 6 were waited for; matrix products, arithmetic and copies ran while one was open for 0% of the time, Pallas kernels for 4%

profile of v5, /device:TPU:25, one launch (start us, length us, event | category | flops | bytes accessed | tf_op | source)
XLA Modules:
  0.0 71.8 jit_solution(1762746602913232335)
XLA Ops:
  0.6 0.0 copy-start.1
  0.6 1.0 %copy-done.1 = f32[16,8,8,128]{3,2,1,0:T(8,128)S(1)} copy-done((f32[16,8,8,128]{3,2,1,0:T(8,128)S(1)}, f32[16,8,8,128]{3,2,1,0:T(8,128)}, u32[]{:S(2)}) %copy-start.1) | copy-done | bytes 524312
  1.7 0.0 copy-start.2
  1.7 0.7 copy-done.2
  2.4 0.5 shard_map.94
  2.9 1.3 %collective-permute-start = (bf16[8,9,16,128]{3,2,1,0:T(8,128)(2,1)S(1)}, bf16[8,9,16,128]{3,2,1,0:T(8,128)(2,1)S(1)}, u32[]{:S(2)}, u32[]{:S(2)}) collective-permute-start(bf16[8,9,16,128]{3,2,1,0:T(8,128)(2,1)S(1)} %get-tuple-element.21.packed.refs_1_), channel_id=1, source_target_pairs={{0,1},{1,0},{2,3},{3,2},{4,5},{5,4},{6,7},{7,6},{8,9},{9,8},{10,11... | collective-permute-start | bytes 884744 | tf_op jit(solution)/shard_map/ppermute | solution.py:772
  4.2 4.0 %collective-permute-start.1 = (bf16[4,9,16,128]{3,2,1,0:T(8,128)(2,1)S(1)}, bf16[4,9,16,128]{3,2,1,0:T(8,128)(2,1)S(1)}, u32[]{:S(2)}, u32[]{:S(2)}) collective-permute-start(bf16[4,9,16,128]{3,2,1,0:T(8,128)(2,1)S(1)} %get-tuple-element.22), channel_id=1, source_target_pairs={{3,1},{0,2},{5,3},{2,4},{7,5},{4,6},{9,7},{6,8},{11,9},{8,10},{13,... | collective-permute-start | bytes 442376 | tf_op jit(solution)/shard_map/ppermute | solution.py:774
  8.2 1.9 %collective-permute-start.2 = (bf16[4,9,16,128]{3,2,1,0:T(8,128)(2,1)S(1)}, bf16[4,9,16,128]{3,2,1,0:T(8,128)(2,1)S(1)}, u32[]{:S(2)}, u32[]{:S(2)}) collective-permute-start(bf16[4,9,16,128]{3,2,1,0:T(8,128)(2,1)S(1)} %get-tuple-element.23), channel_id=1, source_target_pairs={{2,1},{1,2},{4,3},{3,4},{6,5},{5,6},{8,7},{7,8},{10,9},{9,10},{12,... | collective-permute-start | bytes 442376 | tf_op jit(solution)/shard_map/ppermute | solution.py:773
  10.1 0.0 copy-start.3
  10.1 0.7 copy-done.3
  10.8 0.0 copy-start.4
  10.8 0.7 copy-done.4
  11.5 0.0 copy-start.5
  11.5 0.7 copy-done.5
  12.2 1.8 %shard_map.96 = (f32[1536,128]{1,0:T(8,128)S(1)}, f32[3,16,128]{2,1,0:T(8,128)S(1)}) custom-call(s32[1,256]{1,0:T(1,128)S(1)} %bitcast.13, f32[16,256]{1,0:T(8,128)S(1)} %copy-done.3, f32[3,16]{1,0:T(4,128)S(1)} %copy-done.4), custom_call_target="tpu_custom_call" | custom-call | tf_op jit(solution)/shard_map/pallas_call | solution.py:132
  13.9 0.0 collective-permute-done.1.refs_3_
  13.9 2.3 %collective-permute-done.2.refs_4_ = bf16[4,9,16,128]{3,2,1,0:T(8,128)(2,1)S(1)} collective-permute-done((bf16[4,9,16,128]{3,2,1,0:T(8,128)(2,1)S(1)}, bf16[4,9,16,128]{3,2,1,0:T(8,128)(2,1)S(1)}, u32[]{:S(2)}, u32[]{:S(2)}) %collective-permute-start.2) | collective-permute-done | bytes 147488 | tf_op jit(solution)/shard_map/ppermute | solution.py:773
  16.2 0.0 collective-permute-done.refs_2_
  16.2 0.0 copy-start
  16.2 0.0 copy-start.6
  16.2 8.2 %shard_map.97 = (bf16[64,64,128]{2,1,0:T(8,128)(2,1)S(1)}, f32[216,128]{1,0:T(8,128)S(1)}, f32[216,128]{1,0:T(8,128)S(1)}, f32[4,8,16,128]{3,2,1,0:T(8,128)S(1)}, f32[4,8,16,128]{3,2,1,0:T(8,128)S(1)}) custom-call(f32[8,8,16,128]{3,2,1,0:T(8,128)S(1)} %get-tuple-element.20.refs_0_, bf16[8,9,16,128]{3,2,1,0:T(8,128)(2,1)S(1)} %get-tuple-element.21.packed.refs_1_, ...), custom_call_target="tpu_custom_call" | custom-call | tf_op jit(solution)/shard_map/pallas_call | solution.py:456
  24.4 0.1 collective-permute-start.3
  24.5 1.3 %collective-permute-done.3 = f32[216,128]{1,0:T(8,128)S(1)} collective-permute-done((f32[216,128]{1,0:T(8,128)S(1)}, f32[216,128]{1,0:T(8,128)S(1)}, u32[]{:S(2)}, u32[]{:S(2)}) %collective-permute-start.3) | collective-permute-done | bytes 110624 | tf_op jit(solution)/shard_map/ppermute | solution.py:509
  25.8 0.1 collective-permute-start.4
  25.9 3.9 %collective-permute-done.4 = f32[216,128]{1,0:T(8,128)S(1)} collective-permute-done((f32[216,128]{1,0:T(8,128)S(1)}, f32[216,128]{1,0:T(8,128)S(1)}, u32[]{:S(2)}, u32[]{:S(2)}) %collective-permute-start.4) | collective-permute-done | bytes 110624 | tf_op jit(solution)/shard_map/ppermute | solution.py:515
  29.8 0.3 collective-permute-start.5
  30.0 3.4 %collective-permute-done.5 = f32[216,128]{1,0:T(8,128)S(1)} collective-permute-done((f32[216,128]{1,0:T(8,128)S(1)}, f32[216,128]{1,0:T(8,128)S(1)}, u32[]{:S(2)}, u32[]{:S(2)}) %collective-permute-start.5) | collective-permute-done | bytes 110624 | tf_op jit(solution)/shard_map/ppermute | solution.py:515
  33.4 0.1 collective-permute-start.7
  33.6 0.2 collective-permute-start.6
  33.8 5.3 %collective-permute-done.7 = f32[216,128]{1,0:T(8,128)S(1)} collective-permute-done((f32[216,128]{1,0:T(8,128)S(1)}, f32[216,128]{1,0:T(8,128)S(1)}, u32[]{:S(2)}, u32[]{:S(2)}) %collective-permute-start.7) | collective-permute-done | bytes 110624 | tf_op jit(solution)/shard_map/ppermute | solution.py:515
  39.1 0.1 collective-permute-start.8
  39.2 3.6 %collective-permute-done.8 = f32[216,128]{1,0:T(8,128)S(1)} collective-permute-done((f32[216,128]{1,0:T(8,128)S(1)}, f32[216,128]{1,0:T(8,128)S(1)}, u32[]{:S(2)}, u32[]{:S(2)}) %collective-permute-start.8) | collective-permute-done | bytes 110624 | tf_op jit(solution)/shard_map/ppermute | solution.py:515
  42.8 4.5 %collective-permute-start.9 = (f32[216,128]{1,0:T(8,128)S(1)}, f32[216,128]{1,0:T(8,128)S(1)}, u32[]{:S(2)}, u32[]{:S(2)}) collective-permute-start(f32[216,128]{1,0:T(8,128)S(1)} %add.19.mine_ref), channel_id=1, source_target_pairs={{0,2},{1,3},{2,0},{3,1},{4,6},{5,7},{6,4},{7,5},{8,10},{9,11},{10,... | collective-permute-start | bytes 331784 | tf_op jit(solution)/shard_map/ppermute | solution.py:519
  47.3 0.0 collective-permute-done.6.refs_1_
  47.3 1.1 %shard_map.98 = f32[1024,128]{1,0:T(8,128)} custom-call(f32[4,8,16,128]{3,2,1,0:T(8,128)S(1)} %get-tuple-element.26.refs_0_, f32[4,8,16,128]{3,2,1,0:T(8,128)S(1)} %collective-permute-done.6.refs_1_), custom_call_target="tpu_custom_call" | custom-call | tf_op jit(solution)/shard_map/pallas_call | solution.py:495
  48.4 0.0 collective-permute-done.9.other_ref
  48.4 0.0 copy-done
  48.4 0.0 copy-done.6
  48.4 23.2 %shard_map.99 = (bf16[8192,256]{1,0:T(8,128)(2,1)}, f32[1,256]{1,0:T(1,128)}) custom-call(f32[216,128]{1,0:T(8,128)S(1)} %add.19.mine_ref, f32[216,128]{1,0:T(8,128)S(1)} %collective-permute-done.9.other_ref, f32[1,256]{1,0:T(1,128)S(1)} %bitcast.14, bf16[64,64,128]{2,1,0:T(8,128)(2,1)S(1)} %get-tuple-element.34.snaps_hbm, bf16[8192,256]{1,0:T(8,128)(2,1)S(1)} %bitcast.10), custom_call_target="tpu_custom_call" | custom-call | flops 20000000000 | bytes 1048576 | tf_op jit(solution)/shard_map/pallas_call | solution.py:727
  (6 shorter events, 0.1 us)
Async XLA Ops:
  0.6 1.0 %copy-start.1 = (f32[16,8,8,128]{3,2,1,0:T(8,128)S(1)}, f32[16,8,8,128]{3,2,1,0:T(8,128)}, u32[]{:S(2)}) copy-start(f32[16,8,8,128]{3,2,1,0:T(8,128)} %param.7) | copy-start | bytes 1572868
  1.7 0.7 copy-start.2
  2.9 13.3 %collective-permute-start = (bf16[8,9,16,128]{3,2,1,0:T(8,128)(2,1)S(1)}, bf16[8,9,16,128]{3,2,1,0:T(8,128)(2,1)S(1)}, u32[]{:S(2)}, u32[]{:S(2)}) collective-permute-start(bf16[8,9,16,128]{3,2,1,0:T(8,128)(2,1)S(1)} %get-tuple-element.21.packed.refs_1_), channel_id=1, source_target_pairs={{0,1},{1,0},{2,3},{3,2},{4,5},{5,4},{6,7},{7,6},{8,9},{9,8},{10,11... | collective-permute-start | bytes 884744 | tf_op jit(solution)/shard_map/ppermute | solution.py:772
  4.2 9.7 %collective-permute-start.1 = (bf16[4,9,16,128]{3,2,1,0:T(8,128)(2,1)S(1)}, bf16[4,9,16,128]{3,2,1,0:T(8,128)(2,1)S(1)}, u32[]{:S(2)}, u32[]{:S(2)}) collective-permute-start(bf16[4,9,16,128]{3,2,1,0:T(8,128)(2,1)S(1)} %get-tuple-element.22), channel_id=1, source_target_pairs={{3,1},{0,2},{5,3},{2,4},{7,5},{4,6},{9,7},{6,8},{11,9},{8,10},{13,... | collective-permute-start | bytes 442376 | tf_op jit(solution)/shard_map/ppermute | solution.py:774
  8.2 8.0 %collective-permute-start.2 = (bf16[4,9,16,128]{3,2,1,0:T(8,128)(2,1)S(1)}, bf16[4,9,16,128]{3,2,1,0:T(8,128)(2,1)S(1)}, u32[]{:S(2)}, u32[]{:S(2)}) collective-permute-start(bf16[4,9,16,128]{3,2,1,0:T(8,128)(2,1)S(1)} %get-tuple-element.23), channel_id=1, source_target_pairs={{2,1},{1,2},{4,3},{3,4},{6,5},{5,6},{8,7},{7,8},{10,9},{9,10},{12,... | collective-permute-start | bytes 442376 | tf_op jit(solution)/shard_map/ppermute | solution.py:773
  10.1 0.7 %copy-start.3 = (f32[16,256]{1,0:T(8,128)S(1)}, f32[16,256]{1,0:T(8,128)}, u32[]{:S(2)}) copy-start(f32[16,256]{1,0:T(8,128)} %rate_ref.1) | copy-start | bytes 49156
  10.8 0.7 copy-start.4
  11.5 0.7 copy-start.5
  16.2 32.2 %copy-start = (bf16[4,16,128,256]{3,2,1,0:T(8,128)(2,1)S(1)}, bf16[4,16,128,256]{3,2,1,0:T(8,128)(2,1)}, u32[]{:S(2)}) copy-start(bf16[4,16,128,256]{3,2,1,0:T(8,128)(2,1)} %param.12) | copy-start | bytes 12582916
  16.2 32.2 %copy-start.6 = (f32[256]{0:T(256)S(1)}, f32[256]{0:T(256)}, u32[]{:S(2)}) copy-start(f32[256]{0:T(256)} %param.13) | copy-start | bytes 3076
  24.4 1.4 %collective-permute-start.3 = (f32[216,128]{1,0:T(8,128)S(1)}, f32[216,128]{1,0:T(8,128)S(1)}, u32[]{:S(2)}, u32[]{:S(2)}) collective-permute-start(f32[216,128]{1,0:T(8,128)S(1)} %get-tuple-element.29), channel_id=1, source_target_pairs={{0,2},{1,3},{2,0},{3,1},{4,6},{5,7},{6,4},{7,5},{8,10},{9,11},{10,... | collective-permute-start | bytes 331784 | tf_op jit(solution)/shard_map/ppermute | solution.py:509
  25.8 4.0 %collective-permute-start.4 = (f32[216,128]{1,0:T(8,128)S(1)}, f32[216,128]{1,0:T(8,128)S(1)}, u32[]{:S(2)}, u32[]{:S(2)}) collective-permute-start(f32[216,128]{1,0:T(8,128)S(1)} %add.15), channel_id=1, source_target_pairs={{0,1},{1,0},{2,6},{3,7},{4,5},{5,4},{6,2},{7,3},{8,9},{9,8},{10,14... | collective-permute-start | bytes 331784 | tf_op jit(solution)/shard_map/ppermute | solution.py:515
  29.8 3.7 %collective-permute-start.5 = (f32[216,128]{1,0:T(8,128)S(1)}, f32[216,128]{1,0:T(8,128)S(1)}, u32[]{:S(2)}, u32[]{:S(2)}) collective-permute-start(f32[216,128]{1,0:T(8,128)S(1)} %add.16), channel_id=1, source_target_pairs={{0,4},{1,5},{2,3},{3,2},{4,0},{5,1},{6,7},{7,6},{8,12},{9,13},{10,... | collective-permute-start | bytes 331784 | tf_op jit(solution)/shard_map/ppermute | solution.py:515
  33.4 5.7 %collective-permute-start.7 = (f32[216,128]{1,0:T(8,128)S(1)}, f32[216,128]{1,0:T(8,128)S(1)}, u32[]{:S(2)}, u32[]{:S(2)}) collective-permute-start(f32[216,128]{1,0:T(8,128)S(1)} %add.17), channel_id=1, source_target_pairs={{0,8},{1,9},{2,18},{3,19},{4,12},{5,13},{6,22},{7,23},{8,0},{9,1},... | collective-permute-start | bytes 331784 | tf_op jit(solution)/shard_map/ppermute | solution.py:515
  33.6 13.7 %collective-permute-start.6 = (f32[4,8,16,128]{3,2,1,0:T(8,128)S(1)}, f32[4,8,16,128]{3,2,1,0:T(8,128)S(1)}, u32[]{:S(2)}, u32[]{:S(2)}) collective-permute-start(f32[4,8,16,128]{3,2,1,0:T(8,128)S(1)} %get-tuple-element.30), channel_id=1, source_target_pairs={{0,1},{1,0},{2,3},{3,2},{4,5},{5,4},{6,7},{7,6},{8,9},{9,8},{10,11... | collective-permute-start | bytes 786440 | tf_op jit(solution)/shard_map/ppermute | solution.py:518
  39.1 3.7 %collective-permute-start.8 = (f32[216,128]{1,0:T(8,128)S(1)}, f32[216,128]{1,0:T(8,128)S(1)}, u32[]{:S(2)}, u32[]{:S(2)}) collective-permute-start(f32[216,128]{1,0:T(8,128)S(1)} %add.18), channel_id=1, source_target_pairs={{0,16},{1,17},{2,10},{3,11},{4,20},{5,21},{6,14},{7,15},{8,24},{9,... | collective-permute-start | bytes 331784 | tf_op jit(solution)/shard_map/ppermute | solution.py:515
  42.8 5.6 %collective-permute-start.9 = (f32[216,128]{1,0:T(8,128)S(1)}, f32[216,128]{1,0:T(8,128)S(1)}, u32[]{:S(2)}, u32[]{:S(2)}) collective-permute-start(f32[216,128]{1,0:T(8,128)S(1)} %add.19.mine_ref), channel_id=1, source_target_pairs={{0,2},{1,3},{2,0},{3,1},{4,6},{5,7},{6,4},{7,5},{8,10},{9,11},{10,... | collective-permute-start | bytes 331784 | tf_op jit(solution)/shard_map/ppermute | solution.py:519
